TPU v7x, 32 devices: a whole 2x2x4 slice. The times are simulated.
32 devices in a mesh: parts: 2 (over x), dp: 2 (over core), tensor: 8 (over z, y).
Axes of the slice: x: 2, y: 2, z: 4, core: 2. Of those that a mesh axis runs over, the one named last changes fastest.
Arguments:
- home: bfloat16 [8192, 6144], P('tensor', ('parts', 'dp')), parts along dimension 1, as said below
- gain: bfloat16 [8192], replicated, may hold values from 0.099609375 to 1.8984375
- q_values: bfloat16 [8192, 2048], P(None, 'tensor')
- q_scales: float32 [64, 16], P(None, 'tensor'), may hold values from 0.5 to 2
- k_values: bfloat16 [256, 8192], P('tensor')
- k_scales: float32 [2, 64], replicated, may hold values from 0.5 to 2
- v_values: bfloat16 [256, 8192], P('tensor'), may hold values from -0.1875 to 0.1875
- v_scales: float32 [2, 64], replicated, may hold values from 0.5 to 2
- o_values: bfloat16 [2048, 8192], P('tensor'), may hold values from -0.1875 to 0.1875
- o_scales: float32 [16, 64], P('tensor'), may hold values from 0.5 to 2
- row_lengths: int32 [32], P('parts'), parts along dimension 0, may hold values from 1 to 192, as said below
- row_dest: int32 [32], P('parts'), parts along dimension 0, may hold values from 0 to 1, as said below
Outputs:
- attended: bfloat16 [8192, 3072], P('tensor', ('parts', 'dp')), parts along dimension 1
There are 2 independent parts, one for each index of `parts`. A program takes and returns all parts, laid end to end along the dimension named above; an argument that names none is the same for every part. Nothing has to cross between parts.
Inputs may be any that keep to these rules, and one draw needn't show every extreme that they name: `row_lengths`: each group has exactly four rows bound for each group; their lengths add up to 384, and one of them has exactly 192 tokens. `row_dest`: each group sends four of its 8 rows to every group, itself included. `home`: slots past a row's length hold arbitrary finite values.
All inputs are finite; a program needn't handle non-finite values.
Results may differ from a plain program's by a relative error of at most 0.013.
Values may be sent and summed in bfloat16 or wider, within the bound.
No kernel may reach another device: no remote copies, remote signals or barrier semaphores. Data moves between devices by JAX's collectives and lax.ppermute only.
A program may use at most 128 MiB of HBM per device.

v0:
```python
import math

import jax
import jax.numpy as jnp
from jax import lax
from jax.sharding import PartitionSpec as P

D = 8192
HD = 128
TOKD = 768


epsilon = 1e-06
rope_base = 1000000.0


def swapped(value, axis, stride):
    return lax.ppermute(value, axis, [(i, i ^ 1 << stride) for i in range(lax.axis_size(axis))])


def dequantize(stored, scales):
    row_repeat = stored.shape[0] // scales.shape[0]
    column_repeat = stored.shape[1] // scales.shape[1]
    spread = jnp.repeat(jnp.repeat(scales, row_repeat, axis=0), column_repeat, axis=1)
    return (stored.astype(jnp.float32) * spread).astype(jnp.bfloat16)


def row_layout(lengths, chosen, columns):
    live_taken = jnp.where(chosen, lengths, 0)
    finish = jnp.cumsum(live_taken, axis=1)
    row_begin = finish - live_taken
    places = jnp.arange(columns, dtype=jnp.int32)[None, :, None]
    inside = chosen[:, None, :] & (row_begin[:, None, :] <= places) & (places < finish[:, None, :])
    numbers = jnp.arange(lengths.shape[1], dtype=jnp.int32)[None, None, :]
    row_of = jnp.sum(jnp.where(inside, numbers, 0), axis=2)
    within = jnp.sum(jnp.where(inside, places - row_begin[:, None, :], 0), axis=2)
    return (row_of, within)


def row_picks(chosen, per_target):
    ordinal = jnp.cumsum(chosen.astype(jnp.int32), axis=1) - 1
    wanted = jnp.arange(per_target, dtype=jnp.int32)[None, :, None]
    matches = chosen[:, None, :] & (ordinal[:, None, :] == wanted)
    numbers = jnp.arange(chosen.shape[1], dtype=jnp.int32)[None, None, :]
    return (jnp.sum(jnp.where(matches, numbers, 0), axis=2), matches)


def rope_tables(position, head_size):
    half_size = head_size // 2
    frequency = rope_base ** (-2.0 * jnp.arange(half_size, dtype=jnp.float32) / head_size)
    phases = position.astype(jnp.float32)[:, None] * frequency[None, :]
    return (jnp.cos(phases), jnp.sin(phases))


def body(
    home,
    gain,
    q_values,
    q_scales,
    k_values,
    k_scales,
    v_values,
    v_scales,
    o_values,
    o_scales,
    row_lengths,
    row_dest,
):
    groups = lax.axis_size("dp")
    my_group = lax.axis_index("dp")
    my_rank = lax.axis_index("tensor")
    features = home.shape[0]
    per_group = TOKD // groups
    row_count = row_lengths.shape[0] // groups
    slot_size = per_group // 2
    all_lengths = row_lengths.reshape(groups, row_count)
    all_dest = row_dest.reshape(groups, row_count)
    incoming = all_dest == my_group
    receive_row, receive_pos = row_layout(all_lengths, incoming, per_group)
    row_keys = (jnp.arange(groups, dtype=jnp.int32)[:, None] * row_count + receive_row).reshape(-1)
    position = receive_pos.reshape(-1)
    own_dest = lax.dynamic_index_in_dim(all_dest, my_group, 0, keepdims=True)
    targets = jnp.arange(groups, dtype=jnp.int32)[:, None]
    own_chosen = own_dest == targets
    per_target = row_count // groups
    picked_rows, own_matches = row_picks(own_chosen, per_target)
    outgoing = home.reshape(features, row_count, slot_size)[:, picked_rows]
    arrived = lax.all_to_all(outgoing, "dp", split_axis=1, concat_axis=1, tiled=True)
    flattened = arrived.reshape(features, groups * per_target * slot_size)
    source_picks, source_matches = row_picks(incoming, per_target)
    picked_lengths = jnp.sum(jnp.where(source_matches, all_lengths[:, None, :], 0), axis=2)
    slot_row, slot_pos = row_layout(picked_lengths, picked_lengths > 0, per_group)
    sources = jnp.arange(groups, dtype=jnp.int32)[:, None]
    packed = flattened[:, ((sources * per_target + slot_row) * slot_size + slot_pos).reshape(-1)]
    tokens = packed.shape[1]
    gain_wide = gain.astype(jnp.float32)
    q_weight = dequantize(q_values, q_scales)
    head_part = k_values.shape[0]
    scale_row = my_rank * head_part // HD
    k_weight = dequantize(k_values, lax.dynamic_slice_in_dim(k_scales, scale_row, 1, 0))
    v_weight = dequantize(v_values, lax.dynamic_slice_in_dim(v_scales, scale_row, 1, 0))
    kv_weight = jnp.concatenate([k_weight, v_weight], axis=0)
    o_weight = dequantize(o_values, o_scales)
    wide_rows = packed.astype(jnp.float32)
    square_sum = lax.psum(jnp.sum(wide_rows * wide_rows, axis=0), "tensor")
    inverse = lax.rsqrt(square_sum / D + epsilon)
    own_gain = lax.dynamic_slice_in_dim(gain_wide, my_rank * features, features)
    normed = (wide_rows * inverse[None, :] * own_gain[:, None]).astype(jnp.bfloat16)
    shard_piece = lax.all_gather(normed, "tensor", axis=0, tiled=True)
    q_add = lax.dot_general(
        shard_piece, q_weight, (((0,), (0,)), ((), ())), preferred_element_type=jnp.float32
    )
    kv_add = jnp.dot(kv_weight, shard_piece, preferred_element_type=jnp.float32)
    query_proj = q_add.astype(jnp.bfloat16)
    kv_block = kv_add.astype(jnp.bfloat16).reshape(2, head_part, tokens)
    levels = (HD // head_part).bit_length() - 1
    for section_bit in range(levels):
        partner = swapped(kv_block, "tensor", section_bit)
        on_high = my_rank >> section_bit & 1 == 1
        kv_block = jnp.where(
            on_high,
            jnp.concatenate([partner, kv_block], axis=1),
            jnp.concatenate([kv_block, partner], axis=1),
        )
    cosine, sine_table = rope_tables(position, HD)
    half_size = HD // 2
    query_wide = query_proj.astype(jnp.float32).reshape(tokens, -1, HD)
    query_low = query_wide[..., :half_size]
    query_high = query_wide[..., half_size:]
    cos_rows = cosine[:, None, :]
    sin_rows = sine_table[:, None, :]
    rotated_q = jnp.concatenate(
        [
            query_low * cos_rows - query_high * sin_rows,
            query_high * cos_rows + query_low * sin_rows,
        ],
        axis=-1,
    ).astype(jnp.bfloat16)
    key_wide = kv_block[0].astype(jnp.float32)
    key_low = key_wide[:half_size]
    key_high = key_wide[half_size:]
    cos_cols = cosine.T
    sin_cols = sine_table.T
    rotated_k = jnp.concatenate(
        [key_low * cos_cols - key_high * sin_cols, key_high * cos_cols + key_low * sin_cols], axis=0
    ).astype(jnp.bfloat16)
    column_index = jnp.arange(tokens, dtype=jnp.int32)
    allowed = (row_keys[:, None] == row_keys[None, :]) & (
        column_index[None, :] <= column_index[:, None]
    )
    score_scale = 1.0 / math.sqrt(HD)
    scores = (
        jnp.einsum("thd,dk->htk", rotated_q, rotated_k, preferred_element_type=jnp.float32)
        * score_scale
    )
    scores = jnp.where(allowed[None], scores, -1e30)
    highest = jnp.max(scores, axis=2, keepdims=True)
    weights = jnp.exp(scores - highest)
    attention = (weights / jnp.sum(weights, axis=2, keepdims=True)).astype(jnp.bfloat16)
    context = (
        jnp.einsum("htk,dk->thd", attention, kv_block[1], preferred_element_type=jnp.float32)
        .astype(jnp.bfloat16)
        .reshape(tokens, -1)
    )
    return lax.psum_scatter(
        lax.dot_general(
            o_weight, context, (((0,), (1,)), ((), ())), preferred_element_type=jnp.float32
        ).astype(jnp.bfloat16),
        "tensor",
        scatter_dimension=0,
        tiled=True,
    )


def solution(mesh):
    in_specs = (
        P("tensor", ("parts", "dp")),
        P(),
        P(None, "tensor"),
        P(None, "tensor"),
        P("tensor", None),
        P(),
        P("tensor", None),
        P(),
        P("tensor", None),
        P("tensor", None),
        P("parts"),
        P("parts"),
    )
    out_specs = P("tensor", ("parts", "dp"))
    return jax.shard_map(body, mesh=mesh, in_specs=in_specs, out_specs=out_specs, check_vma=False)
```

profile of v0, /device:TPU:0, one launch (start us, length us, event | category | flops | bytes accessed | tf_op | source)
XLA Modules:
  0.0 529.6 jit_solution(10574196949899457559)
XLA Ops:
  6.5 0.7 reshape.325
  7.3 3.2 copy.31
  10.9 2.4 gather_fusion
  13.4 4.1 all-to-all-start
  18.4 2.7 all-to-all-done
  21.0 3.5 gather_fusion.1
  24.6 1.9 fusion.7
  26.5 23.1 %psum.7 = f32[768]{0:T(1024)S(1)} all-reduce(f32[768]{0:T(1024)S(1)} %fusion.7), channel_id=1, replica_groups=mesh['parts'=2,'dp'=2,'tensor'=8] {'tensor'}, use_global_device_ids=true, to_apply=%region_8.9 | all-reduce | flops 768 | bytes 6144 | tf_op jit(solution)/shard_map/psum | solution.py:105
  50.3 3.0 fusion.15
  54.1 1.2 fusion.12
  55.3 1.4 multiply_cosine_fusion
  56.9 170.2 %all-gather.2.cloned.1.call-done = bf16[8192,768]{0,1:T(8,128)(2,1)} async-done(((bf16[1024,768]{0,1:T(8,128)(2,1)}), bf16[8192,768]{0,1:T(8,128)(2,1)}) %all-gather.2.cloned.1.call-update) | async-done | bytes 12582928 | tf_op jit(solution)/shard_map/all_gather | solution.py:109
  227.2 8.5 %convolution_convert_fusion.1 = bf16[64,768]{1,0:T(8,128)(2,1)S(1)} fusion(bf16[8192,768]{0,1:T(8,128)(2,1)} %all-gather.2.cloned.1.call-done, bf16[32,8192]{1,0:T(8,128)(2,1)S(1)} %multiply_convert_fusion, bf16[32,8192]{1,0:T(8,128)(2,1)S(1)} %multiply_convert_fusion.1), kind=kOutput, calls=%fused_computation.27 | convolution fusion | flops 807452672 | bytes 13729792 | tf_op jit(solution)/shard_map/dot_general | solution.py:113
  236.8 19.9 %broadcast_in_dim.152 = f32[8192,2,128]{2,1,0:T(2,128)} broadcast(f32[8192,2]{1,0:T(8,128)S(1)} %bitcast.94), dimensions={0,1} | broadcast | bytes 8454144 | tf_op jit(solution)/shard_map/broadcast_in_dim | solution.py:24
  256.7 11.6 %fusion.17 = bf16[768,256]{0,1:T(8,128)(2,1)S(1)} fusion(bf16[8192,768]{0,1:T(8,128)(2,1)} %all-gather.2.cloned.1.call-done, f32[1024,8,2,128]{3,2,1,0:T(2,128)} %bitcast.91, bf16[8192,256]{1,0:T(8,128)(2,1)} %param.14), kind=kOutput, calls=%fused_computation.26 | convolution fusion | flops 3227713536 | bytes 25559040 | tf_op jit(solution)/shard_map/dot_general | solution.py:110
  268.9 1.6 maximum_select_fusion
  270.6 1.0 subtract_convert_fusion
  271.6 9.2 %collective-permute-done.1 = bf16[2,64,768]{1,2,0:T(8,128)(2,1)S(1)} collective-permute-done((bf16[2,64,768]{1,2,0:T(8,128)(2,1)S(1)}, bf16[2,64,768]{1,2,0:T(8,128)(2,1)S(1)}, u32[]{:S(2)}, u32[]{:S(2)}) %collective-permute-start.1) | collective-permute-done | bytes 196640 | tf_op jit(solution)/shard_map/ppermute | solution.py:18
  281.2 1.8 fusion.30
  283.1 5.1 fusion.55
  288.1 2.9 fusion.16
  291.0 4.5 broadcast_in_dim.134
  295.6 20.1 %convolution_convert_fusion = bf16[8192,768]{1,0:T(8,128)(2,1)} fusion(bf16[768,256]{0,1:T(8,128)(2,1)S(1)} %bitcast.97, f32[32,8,64,128]{3,2,1,0:T(8,128)} %bitcast.90, bf16[256,8192]{1,0:T(8,128)(2,1)} %param.20), kind=kOutput, calls=%fused_computation.3 | convolution fusion | flops 3233808384 | bytes 25559040 | tf_op jit(solution)/shard_map/dot_general | solution.py:166
  315.7 207.1 %reduce-scatter.2.cloned.1.call-done = bf16[1024,768]{1,0:T(8,128)(2,1)} async-done(((bf16[8192,768]{1,0:T(8,128)(2,1)}), bf16[1024,768]{1,0:T(8,128)(2,1)}) %reduce-scatter.2.cloned.1.call-update) | async-done | bytes 1572880 | tf_op jit(solution)/shard_map/reduce_scatter | solution.py:165
  (72 shorter events, 5.2 us)
Async XLA Ops:
  13.3 4.2 copy-start.7
  13.4 7.7 %all-to-all-start = ((bf16[1024,2,4,192]{0,3,2,1:T(8,128)(2,1)}), bf16[1024,2,4,192]{0,3,2,1:T(8,128)(2,1)S(1)}, u32[]{:S(2)}, u32[]{:S(2)}) async-start(bf16[1024,2,4,192]{0,3,2,1:T(8,128)(2,1)} %bitcast.92), calls=%async_computation | async-start | bytes 6291456 | tf_op jit(solution)/shard_map/all_to_all | solution.py:88
  17.4 209.7 %all-gather.2.cloned.1.call-start = ((), (), s32[]{:S(2)}) async-start(), calls=%async_computation.2 | async-start | bytes 14155776 | tf_op jit(solution)/shard_map/all_gather | solution.py:109
  24.6 29.2 %copy-start.4 = (f32[64,2]{0,1:T(2,128)S(1)}, f32[64,2]{0,1:T(2,128)}, u32[]{:S(2)}) copy-start(f32[64,2]{0,1:T(2,128)} %param.15) | copy-start | bytes 1540
  24.6 29.3 %copy-start.5 = (f32[2,64]{1,0:T(2,128)S(1)}, f32[2,64]{1,0:T(2,128)}, u32[]{:S(2)}) copy-start(f32[2,64]{1,0:T(2,128)} %param.17) | copy-start | bytes 1540
  24.6 29.3 %copy-start.6 = (f32[2,64]{1,0:T(2,128)S(1)}, f32[2,64]{1,0:T(2,128)}, u32[]{:S(2)}) copy-start(f32[2,64]{1,0:T(2,128)} %param.19) | copy-start | bytes 1540
  24.6 32.1 %copy-start.1 = (bf16[32,8192]{1,0:T(8,128)(2,1)S(1)}, bf16[32,8192]{1,0:T(8,128)(2,1)}, u32[]{:S(2)}) copy-start(bf16[32,8192]{1,0:T(8,128)(2,1)} %param.18) | copy-start | bytes 1572868
  24.6 32.2 %copy-start.2 = (bf16[32,8192]{1,0:T(8,128)(2,1)S(1)}, bf16[32,8192]{1,0:T(8,128)(2,1)}, u32[]{:S(2)}) copy-start(bf16[32,8192]{1,0:T(8,128)(2,1)} %param.16) | copy-start | bytes 1572868
  53.3 469.5 %reduce-scatter.2.cloned.1.call-start = ((), (), s32[]{:S(2)}) async-start(), calls=%async_computation.3 | async-start | bytes 14155776 | tf_op jit(solution)/shard_map/reduce_scatter | solution.py:165
  235.9 33.0 %collective-permute-start = (bf16[2,32,768]{1,2,0:T(8,128)(2,1)S(1)}, bf16[2,32,768]{1,2,0:T(8,128)(2,1)}, u32[]{:S(2)}, u32[]{:S(2)}) collective-permute-start(bf16[2,32,768]{1,2,0:T(8,128)(2,1)S(1)} %copy.32), channel_id=1, source_target_pairs={{0,1},{1,0},{2,3},{3,2},{4,5},{5,4},{6,7},{7,6},{8,9},{9,8},{10,11... | collective-permute-start | bytes 294920 | tf_op jit(solution)/shard_map/ppermute | solution.py:18
  268.9 14.2 %copy-start = (pred[768,768]{0,1:T(8,128)(4,1)S(1)}, pred[768,768]{0,1:T(8,128)(4,1)}, u32[]{:S(2)}) copy-start(pred[768,768]{0,1:T(8,128)(4,1)} %fusion.12) | copy-start | bytes 1769476
  270.5 10.2 %collective-permute-start.1 = (bf16[2,64,768]{1,2,0:T(8,128)(2,1)S(1)}, bf16[2,64,768]{1,2,0:T(8,128)(2,1)S(1)}, u32[]{:S(2)}, u32[]{:S(2)}) collective-permute-start(bf16[2,64,768]{1,2,0:T(8,128)(2,1)S(1)} %maximum_select_fusion), channel_id=1, source_target_pairs={{0,2},{1,3},{2,0},{3,1},{4,6},{5,7},{6,4},{7,5},{8,10},{9,11},{10,... | collective-permute-start | bytes 589832 | tf_op jit(solution)/shard_map/ppermute | solution.py:18
  288.1 2.9 copy-start.3
Sparse Core Ops, SparseCore 0:
  53.4 173.6 all-gather.1
  315.8 206.9 reduce-scatter.1
where the time goes:
time: 530 us
  waiting for transfers between devices  389 us (73%)
  matrix products  48.1 us (9%)
  local copies, waits for them, and re-layouts  35.8 us (7%)
  blocking collectives  23.1 us (4%)
  other arithmetic  14.7 us (3%)
  between operations  13.7 us (3%)
    reduce_scatter x1, waiting for transfers between devices, body(): lax.psum_scatter(lax.dot_general(o_weight, context, (((0,), (1,)), ((), (...  207 us
    all_gather x1, waiting for transfers between devices, body(): shard_piece = lax.all_gather(normed, 'tensor', axis=0, tiled=True)  170 us
    broadcast_in_dim x4, local copies, waits for them, and re-layouts, dequantize(): jnp.repeat(jnp.repeat(scales, row_repeat, axis=0), column_repeat, axis=1)  24.5 us
    psum x1, blocking collectives, body(): square_sum = lax.psum(jnp.sum(wide_rows * wide_rows, axis=0), 'tensor')  23.1 us
    dot_general x1, matrix products, body(): lax.dot_general(o_weight, context, (((0,), (1,)), ((), ())), preferred_el...  20.1 us
    dot_general x1, matrix products, body(): lax.dot_general(shard_piece, q_weight, (((0,), (0,)), ((), ())), preferre...  11.6 us
  transfers between devices with their start and end apart: 5, of which 4 were waited for; matrix products, arithmetic and copies ran while one was open for 7% of the time, Pallas kernels for 0%

commit v1 on v0

v1 whole, which is shorter than its diff:
```python
import functools
import math

import jax
import jax.numpy as jnp
from jax import lax
from jax.experimental import pallas as pl
from jax.experimental.pallas import tpu as pltpu
from jax.sharding import PartitionSpec as P

D = 8192
HD = 128
BLOCKS = 4

epsilon = 1e-06
rope_base = 1000000.0

F32 = jnp.float32
BF16 = jnp.bfloat16
NN = (((1,), (0,)), ((), ()))
NT = (((1,), (1,)), ((), ()))
MIB = 1 << 20


def dot(a, b, dims=NN):
    return lax.dot_general(a, b, dims, preferred_element_type=F32)


def in_vmem():
    return pl.BlockSpec(memory_space=pltpu.VMEM)


def in_smem():
    return pl.BlockSpec(memory_space=pltpu.SMEM)


def row_facts(lens, dest, source, target, rows, slot):
    zero = jnp.int32(0)
    start, seen = zero, zero
    full = [zero, zero]
    short = [[zero, zero, zero] for _ in range(3)]
    for i in range(rows):
        mine = dest[source * rows + i] == target
        size = jnp.where(mine, lens[source * rows + i], 0)
        is_full = size == slot
        is_short = jnp.logical_and(mine, size != slot)
        full = [jnp.where(is_full, i, full[0]), jnp.where(is_full, start, full[1])]
        for k in range(3):
            hit = jnp.logical_and(is_short, seen == k)
            for e, value in enumerate((jnp.int32(i), start, size)):
                short[k][e] = jnp.where(hit, value, short[k][e])
        seen = seen + jnp.where(is_short, 1, 0)
        start = start + size
    return full, short


def qkv_pieces_kernel(chunks, width, place, q_ref, k_ref, v_ref, qs, ks, vs, *outs):
    unit = pl.program_id(0)
    quarter, head = place[0], place[1]
    part = k_ref.shape[0]
    for chunk in range(chunks):
        out = outs[chunk]
        for i in range(width // HD):
            rows = slice(chunk * width + i * HD, chunk * width + (i + 1) * HD)
            block = (unit * 4 + quarter) * (chunks * width // HD) + chunk * (width // HD) + i
            for h in range(q_ref.shape[1] // HD):
                cols = slice(h * HD, (h + 1) * HD)
                out[0, i * HD : (i + 1) * HD, cols] = (
                    q_ref[rows, cols].astype(F32) * qs[block, h]
                ).astype(BF16)
            lanes = slice(i * HD, (i + 1) * HD)
            out[0, width : width + part, lanes] = (
                k_ref[:, rows].astype(F32) * ks[head, block]
            ).astype(BF16)
            out[0, width + part : width + 2 * part, lanes] = (
                v_ref[:, rows].astype(F32) * vs[head, block]
            ).astype(BF16)
        if width < q_ref.shape[1]:
            out[0, width:, width:] = jnp.zeros((2 * part, q_ref.shape[1] - width), BF16)


def qkv_pieces(place, q_values, q_scales, k_values, k_scales, v_values, v_scales, units):
    own = q_values.shape[1]
    part = k_values.shape[0]
    quarter = q_values.shape[0] // units // 4
    width = min(quarter, 256)
    chunks = quarter // width
    shape = jax.ShapeDtypeStruct((units, width + 2 * part, own), BF16)
    grid_spec = pltpu.PrefetchScalarGridSpec(
        num_scalar_prefetch=1,
        grid=(units,),
        in_specs=[
            pl.BlockSpec((quarter, own), lambda i, s: (i * 4 + s[0], 0)),
            pl.BlockSpec((part, quarter), lambda i, s: (0, i * 4 + s[0])),
            pl.BlockSpec((part, quarter), lambda i, s: (0, i * 4 + s[0])),
            in_smem(),
            in_smem(),
            in_smem(),
        ],
        out_specs=[pl.BlockSpec((1, width + 2 * part, own), lambda i, s: (i, 0, 0))] * chunks,
    )
    return pl.pallas_call(
        functools.partial(qkv_pieces_kernel, chunks, width),
        grid_spec=grid_spec,
        out_shape=[shape] * chunks,
        name="qkv_pieces",
    )(place, q_values, k_values, v_values, q_scales, k_scales, v_scales)


def o_pieces_kernel(fq, place, o_ref, scales, out):
    target = pl.program_id(0)
    quarter = place[0]
    own = o_ref.shape[0]
    if o_ref.shape[1] == fq:
        first = (target * 4 + quarter) * fq
        for h in range(own // HD):
            for i in range(fq // HD):
                s = scales[h, first // HD + i]
                block = o_ref[h * HD : (h + 1) * HD, i * HD : (i + 1) * HD].astype(F32) * s
                out[0, i * HD : (i + 1) * HD, h * HD : (h + 1) * HD] = block.T.astype(BF16)
    else:
        for h in range(own // HD):
            total = jnp.zeros((fq, HD), F32)
            for i in range(4):
                s = scales[h, (target * 4 + i) * fq // HD]
                block = o_ref[h * HD : (h + 1) * HD, :].astype(F32).T[i * fq : (i + 1) * fq] * s
                total = jnp.where(quarter == i, block, total)
            out[0, :, h * HD : (h + 1) * HD] = total.astype(BF16)


def o_pieces(place, o_values, o_scales, ranks):
    own = o_values.shape[0]
    features = o_values.shape[1] // ranks
    fq = features // 4
    if fq % HD == 0:
        spec = pl.BlockSpec((own, fq), lambda i, s: (0, i * 4 + s[0]))
    else:
        spec = pl.BlockSpec((own, features), lambda i, s: (0, i))
    grid_spec = pltpu.PrefetchScalarGridSpec(
        num_scalar_prefetch=1,
        grid=(ranks,),
        in_specs=[spec, in_smem()],
        out_specs=pl.BlockSpec((1, fq, own), lambda i, s: (i, 0, 0)),
    )
    return pl.pallas_call(
        functools.partial(o_pieces_kernel, fq),
        grid_spec=grid_spec,
        out_shape=jax.ShapeDtypeStruct((ranks, fq, own), BF16),
        name="o_pieces",
    )(place, o_values, o_scales)


def deal_kernel(rows, slot, place, lens, dest, home, keep, send, squares, pos, pick, folded):
    step = pl.program_id(0)
    group, block = place[0], place[1]

    @pl.when(step == 0)
    def _():
        column = lax.broadcasted_iota(jnp.int32, (slot, 1), 0)
        lane = lax.broadcasted_iota(jnp.int32, (slot, rows * slot), 1)
        for turn in range(2):
            full, short = row_facts(lens, dest, group, group ^ turn, rows, slot)
            first = short[0][2]
            second = first + short[1][2]
            from_short = jnp.where(
                column < first,
                short[0][0] * slot + column,
                jnp.where(
                    column < second,
                    short[1][0] * slot + column - first,
                    short[2][0] * slot + column - second,
                ),
            )
            for kind, index in enumerate((full[0] * slot + column, from_short)):
                at = (turn * 2 + kind) * slot
                pick[at : at + slot, :] = jnp.where(lane == index, 1.0, 0.0).astype(BF16)
        _, short = row_facts(lens, dest, group ^ (block >> 1), group, rows, slot)
        first = short[0][2]
        second = first + short[1][2]
        begin = jnp.where(column < first, 0, jnp.where(column < second, first, second))
        place_in_row = column - jnp.where((block & 1) == 1, begin, 0)
        pos[...] = jnp.broadcast_to(place_in_row.astype(F32), pos.shape)
        folded[...] = jnp.zeros_like(folded)

    taken = dot(pick[...], home[...], NT)
    half = 2 * slot
    keep[...] = taken[:half].astype(BF16)
    send[...] = taken[half:].astype(BF16)
    total = folded[...]
    for i in range(taken.shape[1] // 128):
        part = taken[:, i * 128 : (i + 1) * 128]
        total = total + part * part
    folded[...] = total

    @pl.when(step == pl.num_programs(0) - 1)
    def _():
        sums = jnp.sum(folded[...].T, axis=0, keepdims=True)
        squares[...] = jnp.broadcast_to(sums, squares.shape)


def deal(place, lens, dest, home, rows, slot):
    features = home.shape[0]
    width = min(features, 256)
    tokens = BLOCKS * slot
    return pl.pallas_call(
        functools.partial(deal_kernel, rows, slot),
        grid=(features // width,),
        in_specs=[
            in_smem(),
            in_smem(),
            in_smem(),
            pl.BlockSpec((width, home.shape[1]), lambda i: (i, 0)),
        ],
        out_specs=[
            pl.BlockSpec((tokens // 2, width), lambda i: (0, i)),
            pl.BlockSpec((tokens // 2, width), lambda i: (0, i)),
            pl.BlockSpec((8, tokens), lambda i: (0, 0)),
            pl.BlockSpec((slot, 128), lambda i: (0, 0)),
        ],
        out_shape=[
            jax.ShapeDtypeStruct((tokens // 2, features), BF16),
            jax.ShapeDtypeStruct((tokens // 2, features), BF16),
            jax.ShapeDtypeStruct((8, tokens), F32),
            jax.ShapeDtypeStruct((slot, 128), F32),
        ],
        scratch_shapes=[
            pltpu.VMEM((tokens, rows * slot), BF16),
            pltpu.VMEM((tokens, 128), F32),
        ],
        compiler_params=pltpu.CompilerParams(vmem_limit_bytes=32 * MIB),
        name="deal",
    )(place, lens, dest, home)


def project_kernel(units, chunks, width, place, squares, gain, keep, got, keep2, got2, *rest):
    weights = rest[: 4 * chunks]
    q_outs = rest[4 * chunks : 4 * chunks + units]
    kv_outs = rest[4 * chunks + units : 4 * chunks + 2 * units]
    normed, total = rest[4 * chunks + 2 * units :]
    unit, side, quarter = place[0], place[1], place[2]
    half, features = keep.shape
    tokens = 2 * half
    slot = tokens // BLOCKS
    inverse = lax.rsqrt(squares[...] / D + epsilon).T[:, :1]
    for at, pair in ((side, (keep, got)), (1 - side, (keep2, got2))):
        lanes = pl.ds(pl.multiple_of(at * features, 128), features)
        own_gain = gain[:, lanes]
        for e, ref in enumerate(pair):
            rows = slice(e * half, (e + 1) * half)
            normed[rows, lanes] = (ref[...].astype(F32) * inverse[rows] * own_gain).astype(BF16)

    def lanes_of(turn, chunk):
        at = (quarter ^ turn) * (chunks * width) + chunk * width
        return pl.ds(pl.multiple_of(at, 128), width)

    pieces = [(r, c) for r in range(4) for c in range(chunks)]

    def hand_out(group, outs, cols):
        for k in range(units):
            target = unit ^ k

            def write(out=outs[k], target=target):
                rows = pl.ds(pl.multiple_of((target & 3) * slot, 16), slot)
                out[:, cols] = total[rows, :].astype(BF16)

            if units == BLOCKS:
                write()
            else:
                pl.when((target >> 2) == group)(write)

    own = total.shape[1]
    for group in range(units // BLOCKS):
        value = None
        for r, c in pieces:
            w = weights[r * chunks + c]
            w = w[group * 4 : group * 4 + 4, width:, :width]
            w = w.reshape(4 * w.shape[1], width)
            term = dot(normed[:, lanes_of(r, c)], w, NT)
            value = term if value is None else value + term
        total[...] = value
        hand_out(group, kv_outs, slice(0, own))
        for s in range(4):
            value = None
            for r, c in pieces:
                w = weights[r * chunks + c][group * 4 + s, :width, :]
                term = dot(normed[:, lanes_of(r, c)], w)
                value = term if value is None else value + term
            total[...] = value
            hand_out(group, q_outs, slice(s * own, (s + 1) * own))


def project(place, squares, gain, keep, got, keep2, got2, weights, units, chunks, width):
    half, features = keep.shape
    slot = half // 2
    own = weights[0].shape[2]
    kv = 4 * (weights[0].shape[1] - width)
    outs = pl.pallas_call(
        functools.partial(project_kernel, units, chunks, width),
        in_specs=[in_smem()] + [in_vmem()] * (6 + len(weights)),
        out_specs=[in_vmem()] * (2 * units),
        out_shape=[jax.ShapeDtypeStruct((slot, 4 * own), BF16)] * units
        + [jax.ShapeDtypeStruct((slot, kv), BF16)] * units,
        scratch_shapes=[
            pltpu.VMEM((2 * half, 2 * features), BF16),
            pltpu.VMEM((2 * half, own), F32),
        ],
        compiler_params=pltpu.CompilerParams(vmem_limit_bytes=40 * MIB),
        name="project",
    )(place, squares, gain, keep, got, keep2, got2, *weights)
    return outs[:units], outs[units:]


def key_value_kernel(units, *refs):
    parts, (cosine, sine), out = refs[:units], refs[units : units + 2], refs[units + 2]
    value = parts[0][...].astype(F32)
    for part in parts[1:]:
        value = value + part[...].astype(F32)
    value = value.astype(BF16).astype(F32)
    part = value.shape[1] // 8
    keys = [value[:, 2 * i * part : (2 * i + 1) * part] for i in range(4)]
    values = [value[:, (2 * i + 1) * part : (2 * i + 2) * part] for i in range(4)]
    turned = []
    for h in range(2):
        low, high = keys[2 * h], keys[2 * h + 1]
        turned.append(low * cosine[...] - high * sine[...])
        turned.append(high * cosine[...] + low * sine[...])
    out[...] = jnp.concatenate(turned + values, axis=1).astype(BF16)


def key_value(parts, cosine, sine):
    return pl.pallas_call(
        functools.partial(key_value_kernel, len(parts)),
        in_specs=[in_vmem()] * (len(parts) + 2),
        out_specs=in_vmem(),
        out_shape=jax.ShapeDtypeStruct(parts[0].shape, BF16),
        name="key_value",
    )(*parts, cosine, sine)


def attend_kernel(units, rows, slot, place, lens, dest, cosine, sine, own_kv, other_kv, *refs):
    parts, out = refs[:units], refs[units]
    group, block, side = place[0], place[1], place[2]
    _, short = row_facts(lens, dest, group ^ (block >> 1), group, rows, slot)
    many = (block & 1) == 1
    first = jnp.where(many, short[0][2], slot)
    second = jnp.where(many, first + short[1][2], slot)

    def segment(shape, axis):
        at = lax.broadcasted_iota(jnp.int32, shape, axis)
        return jnp.where(at >= first, 1, 0) + jnp.where(at >= second, 1, 0)

    shape = (slot, slot)
    allowed = jnp.logical_and(
        segment(shape, 0) == segment(shape, 1),
        lax.broadcasted_iota(jnp.int32, shape, 1) <= lax.broadcasted_iota(jnp.int32, shape, 0),
    )
    mine, theirs = own_kv[...].astype(F32), other_kv[...].astype(F32)
    even = jnp.where(side == 0, mine, theirs)
    odd = jnp.where(side == 0, theirs, mine)
    part = HD // 4
    heads = []
    for h in range(4):
        pieces = []
        for b in range(2):
            at = slice((2 * h + b) * part, (2 * h + b + 1) * part)
            pieces += [even[:, at], odd[:, at]]
        heads.append(jnp.concatenate(pieces, axis=1).astype(BF16))
    cos, sin = cosine[...], sine[...]
    scale = 1.0 / math.sqrt(HD)
    count = out.shape[1] // HD
    for head in range(count):
        at = slice(head * HD, (head + 1) * HD)
        query = parts[0][:, at].astype(F32)
        for ref in parts[1:]:
            query = query + ref[:, at].astype(F32)
        query = query.astype(BF16).astype(F32)
        swapped = jnp.concatenate([query[:, HD // 2 :], query[:, : HD // 2]], axis=1)
        query = (query * cos + swapped * sin).astype(BF16)
        kv = head // (count // 2)
        scores = dot(query, heads[kv], NT) * scale
        scores = jnp.where(allowed, scores, -1e30)
        weights = jnp.exp(scores - jnp.max(scores, axis=1, keepdims=True))
        attention = (weights / jnp.sum(weights, axis=1, keepdims=True)).astype(BF16)
        out[:, at] = dot(attention, heads[2 + kv]).astype(BF16)


def attend(place, lens, dest, cosine, sine, own_kv, other_kv, parts, rows, slot):
    return pl.pallas_call(
        functools.partial(attend_kernel, len(parts), rows, slot),
        in_specs=[in_smem()] * 3 + [in_vmem()] * (4 + len(parts)),
        out_specs=in_vmem(),
        out_shape=jax.ShapeDtypeStruct(parts[0].shape, BF16),
        name="attend",
    )(place, lens, dest, cosine, sine, own_kv, other_kv, *parts)


def output_kernel(units, rows, slot, place, lens, dest, *refs):
    weights = refs[:4]
    mine, theirs = refs[4 : 4 + units], refs[4 + units : 4 + 2 * units]
    out, context, order = refs[4 + 2 * units :]
    unit, side, quarter, group = place[0], place[1], place[2], place[3]
    own = weights[0].shape[2]
    tokens = BLOCKS * slot
    for k in range(units):
        source = unit ^ k
        at_rows = pl.ds(pl.multiple_of((source & 3) * slot, 16), slot)
        for pieces, y in ((mine, side), (theirs, 1 - side)):
            for s in range(4):
                rank = ((source >> 2) * 4 + s) * 2 + y
                context[at_rows, pl.ds(pl.multiple_of(rank * own, 128), own)] = pieces[k][
                    :, s * own : (s + 1) * own
                ]
    half = 2 * slot
    column = lax.broadcasted_iota(jnp.int32, (1, half), 1)
    for source in range(2):
        full, short = row_facts(lens, dest, source, group, rows, slot)
        index = column - full[1]
        done = jnp.int32(0)
        for k in range(3):
            inside = jnp.logical_and(
                column >= short[k][1], column < short[k][1] + short[k][2]
            )
            index = jnp.where(inside, slot + done + column - short[k][1], index)
            done = done + short[k][2]
        index = index + (group ^ source) * half
        row = lax.broadcasted_iota(jnp.int32, (tokens, half), 0)
        order[:, source * half : (source + 1) * half] = jnp.where(
            row == index, 1.0, 0.0
        ).astype(BF16)
    ranks, fq = weights[0].shape[:2]
    for r in range(4):
        value = None
        for rank in range(ranks):
            term = dot(weights[r][rank], context[:, rank * own : (rank + 1) * own], NT)
            value = term if value is None else value + term
        at = pl.multiple_of((quarter ^ r) * fq, 16)
        out[pl.ds(at, fq), :] = dot(value.astype(BF16), order[...]).astype(BF16)


def output(place, lens, dest, weights, mine, theirs, rows, slot):
    units = len(mine)
    ranks, fq, own = weights[0].shape
    tokens = BLOCKS * slot
    return pl.pallas_call(
        functools.partial(output_kernel, units, rows, slot),
        in_specs=[in_smem()] * 3 + [in_vmem()] * (4 + 2 * units),
        out_specs=in_vmem(),
        out_shape=jax.ShapeDtypeStruct((4 * fq, tokens), BF16),
        scratch_shapes=[
            pltpu.VMEM((tokens, ranks * own), BF16),
            pltpu.VMEM((tokens, tokens), BF16),
        ],
        compiler_params=pltpu.CompilerParams(vmem_limit_bytes=48 * MIB),
        name="output",
    )(place, lens, dest, *weights, *mine, *theirs)


def swap(value, axis, mask=1):
    size = lax.axis_size(axis)
    return lax.ppermute(value, axis, [(i, i ^ mask) for i in range(size)])


def all_quarters(value):
    across = swap(value, "parts")
    return [value, swap(value, "dp"), across, swap(across, "dp")]


def body(
    home,
    gain,
    q_values,
    q_scales,
    k_values,
    k_scales,
    v_values,
    v_scales,
    o_values,
    o_scales,
    row_lengths,
    row_dest,
):
    ranks = lax.axis_size("tensor")
    units = ranks // 2
    rank = lax.axis_index("tensor")
    unit, side = rank >> 1, rank & 1
    group = lax.axis_index("dp")
    quarter = (lax.axis_index("parts") & 1) * 2 + group
    block = unit & (BLOCKS - 1)
    features = home.shape[0]
    rows = row_lengths.shape[0] // 2
    slot = home.shape[1] // rows
    half = 2 * slot

    def places(*values):
        return jnp.stack([jnp.asarray(v, jnp.int32) for v in values])

    columns = [[2 * u + y for u in range(units)] for y in range(2)]
    kv_head = rank * k_values.shape[0] // HD
    pieces = qkv_pieces(
        places(quarter, kv_head),
        q_values,
        q_scales,
        k_values,
        k_scales,
        v_values,
        v_scales,
        units,
    )
    chunks = len(pieces)
    width = D // units // 4 // chunks
    by_chunk = []
    for piece in pieces:
        moved = lax.all_to_all(
            piece, "tensor", split_axis=0, concat_axis=0, tiled=True, axis_index_groups=columns
        )
        by_chunk.append(all_quarters(moved))
    weights = [by_chunk[c][r] for r in range(4) for c in range(chunks)]

    keep, send, squares, pos = deal(
        places(group, block), row_lengths, row_dest, home, rows, slot
    )
    got = swap(send, "dp")
    keep2 = swap(keep, "tensor")
    got2 = lax.ppermute(
        send, ("dp", "tensor"), [(i, i ^ (ranks + 1)) for i in range(2 * ranks)]
    )
    bit = 1
    while bit < ranks:
        squares = squares + swap(squares, "tensor", bit)
        bit *= 2
    squares = jnp.concatenate([squares[:, :half], swap(squares[:, half:], "dp")], axis=1)

    own_gain = lax.dynamic_slice_in_dim(
        gain.astype(F32), unit * 2 * features, 2 * features
    ).reshape(1, -1)
    q_parts, kv_parts = project(
        places(unit, side, quarter),
        squares,
        own_gain,
        keep,
        got,
        keep2,
        got2,
        weights,
        units,
        chunks,
        width,
    )
    kv_parts = [kv_parts[0]] + [swap(kv_parts[k], "tensor", 2 * k) for k in range(1, units)]
    q_parts = [q_parts[0]] + [swap(q_parts[k], "tensor", 2 * k) for k in range(1, units)]

    frequency = rope_base ** (-2.0 * jnp.arange(HD // 2, dtype=F32) / HD)
    phases = pos[:, :1] * frequency[None, :]
    cosine, sine = jnp.cos(phases), jnp.sin(phases)
    part = HD // 4
    own_cos = lax.dynamic_slice_in_dim(cosine, side * part, part, 1)
    own_sin = lax.dynamic_slice_in_dim(sine, side * part, part, 1)
    own_kv = key_value(kv_parts, own_cos, own_sin)
    other_kv = swap(own_kv, "tensor")
    context = attend(
        places(group, block, side),
        row_lengths,
        row_dest,
        jnp.concatenate([cosine, cosine], axis=1),
        jnp.concatenate([-sine, sine], axis=1),
        own_kv,
        other_kv,
        q_parts,
        rows,
        slot,
    )

    o_moved = lax.all_to_all(
        o_pieces(places(quarter), o_values, o_scales, ranks),
        "tensor",
        split_axis=0,
        concat_axis=0,
        tiled=True,
    )
    o_weights = all_quarters(o_moved)
    mine = [context] + [swap(context, "tensor", 2 * k) for k in range(1, units)]
    theirs = [swap(value, "tensor") for value in mine]
    return output(
        places(unit, side, quarter, group),
        row_lengths,
        row_dest,
        o_weights,
        mine,
        theirs,
        rows,
        slot,
    )


def solution(mesh):
    in_specs = (
        P("tensor", ("parts", "dp")),
        P(),
        P(None, "tensor"),
        P(None, "tensor"),
        P("tensor", None),
        P(),
        P("tensor", None),
        P(),
        P("tensor", None),
        P("tensor", None),
        P("parts"),
        P("parts"),
    )
    out_specs = P("tensor", ("parts", "dp"))
    return jax.shard_map(body, mesh=mesh, in_specs=in_specs, out_specs=out_specs, check_vma=False)
```

time: 530 us -> 247 us (0.47)
  waiting for transfers between devices: 389 us -> 114 us
  matrix products: 48.1 us -> 0 us
  starting transfers between devices: 4.85 us -> 44.9 us
  Pallas kernels: 0 us -> 39.8 us
  local copies, waits for them, and re-layouts: 35.8 us -> 18.6 us
  between operations: 13.7 us -> 0.11 us
  other arithmetic: 14.7 us -> 5.08 us
    reduce_scatter x1 -> x0, waiting for transfers between devices: 207 us -> none  [body(): lax.psum_scatter(lax.dot_general(o_weight, context, (((0,), (1,)), ((), (...]
    all_gather x1 -> x0, waiting for transfers between devices: 170 us -> none  [body(): shard_piece = lax.all_gather(normed, 'tensor', axis=0, tiled=True)]
    ppermute x2 -> x30, waiting for transfers between devices: 9.2 us -> 103 us  [the longest x29 89.4 us: swap(): return lax.ppermute(value, axis, [(i, i ^ mask) for i in range(size)])]
    dot_general x4 -> x0, matrix products: 43 us -> none  [the longest x1 20.1 us: body(): lax.dot_general(o_weight, context, (((0,), (1,)), ((), ())), preferred_el...]
    pallas_call x0 -> x7, Pallas kernels: none -> 39.8 us  [the longest x1 10.1 us: output(): pl.pallas_call(functools.partial(output_kernel, units, rows, slot), in_sp...]
    ppermute x2 -> x30, starting transfers between devices: 0.69 us -> 37.6 us  [the longest x29 37.2 us: swap(): return lax.ppermute(value, axis, [(i, i ^ mask) for i in range(size)])]
    broadcast_in_dim x7 -> x0, local copies, waits for them, and re-layouts: 24.9 us -> none  [the longest x4 24.5 us: dequantize(): jnp.repeat(jnp.repeat(scales, row_repeat, axis=0), column_repeat, axis=1)]
    all_to_all x0 -> x1, blocking collectives: none -> 23.6 us  [body(): lax.all_to_all(piece, 'tensor', split_axis=0, concat_axis=0, tiled=True,...]
  transfers between devices with their start and end apart: 5 -> 32, of which waited for: 4 -> 17; matrix products, arithmetic and copies ran while one was open for 7% -> 2% of each run, Pallas kernels for 0% -> 10%
where the time goes in v1:
time: 247 us; the launch traced here: 246 us
  waiting for transfers between devices  114 us (46%)
  starting transfers between devices  44.9 us (18%)
  Pallas kernels  39.8 us (16%)
  blocking collectives  23.6 us (10%)
  local copies, waits for them, and re-layouts  18.6 us (8%)
  other arithmetic  5.08 us (2%)
    ppermute x29, waiting for transfers between devices, swap(): return lax.ppermute(value, axis, [(i, i ^ mask) for i in range(size)])  89.4 us
    ppermute x29, starting transfers between devices, swap(): return lax.ppermute(value, axis, [(i, i ^ mask) for i in range(size)])  37.2 us
    all_to_all x1, blocking collectives, body(): lax.all_to_all(piece, 'tensor', split_axis=0, concat_axis=0, tiled=True,...  23.6 us
    unnamed x51, local copies, waits for them, and re-layouts  17.7 us
    ppermute x1, waiting for transfers between devices, body(): lax.ppermute(send, ('dp', 'tensor'), [(i, i ^ ranks + 1) for i in range(2...  13.7 us
    all_to_all x1, waiting for transfers between devices, body(): lax.all_to_all(piece, 'tensor', split_axis=0, concat_axis=0, tiled=True,...  10.8 us
    pallas_call x1, Pallas kernels, output(): pl.pallas_call(functools.partial(output_kernel, units, rows, slot), in_sp...  10.1 us
    pallas_call x1, Pallas kernels, project(): pl.pallas_call(functools.partial(project_kernel, units, chunks, width), i...  7.42 us
  transfers between devices with their start and end apart: 32, of which 17 were waited for; matrix products, arithmetic and copies ran while one was open for 2% of the time, Pallas kernels for 10%

profile of v1, /device:TPU:0, one launch (start us, length us, event | category | flops | bytes accessed | tf_op | source)
XLA Modules:
  0.0 246.0 jit_solution(12892809267476927094)
XLA Ops:
  2.0 4.6 %qkv_pieces.1 = (bf16[4,320,256]{2,1,0:T(8,128)(2,1)}, bf16[4,320,256]{2,1,0:T(8,128)(2,1)}) custom-call(s32[2]{0:T(128)} %pad_add_fusion.4.place, bf16[8192,256]{1,0:T(8,128)(2,1)} %q_ref.1, bf16[32,8192]{1,0:T(8,128)(2,1)} %k_ref.1, bf16[32,8192]{1,0:T(8,128)(2,1)} %v_ref.1, f32[64,2]{1,0:T(8,128)} %copy.14.qs, f32[2,64]{1,0:T(2,128)} %ks.1, f32[2,64]{1,0:T(2,128)} %vs.1), custom_call_target="tpu_custom_call" | custom-call | tf_op jit(solution)/shard_map/qkv_pieces/pallas_call | solution.py:102
  6.6 23.6 %all_to_all.15.rest_0_ = bf16[4,320,256]{2,1,0:T(8,128)(2,1)S(1)} all-to-all(bf16[4,320,256]{2,1,0:T(8,128)(2,1)} %get-tuple-element.23), channel_id=1, replica_groups={{0,2,4,6},{1,3,5,7},{8,10,12,14},{9,11,13,15},{16,18,20,22},{17,19,21,2..., dimensions={0} | all-to-all | bytes 1310720 | tf_op jit(solution)/shard_map/all_to_all | solution.py:513
  30.3 3.6 %all-to-all-start.2 = ((bf16[4,320,256]{2,1,0:T(8,128)(2,1)}), bf16[4,320,256]{2,1,0:T(8,128)(2,1)S(1)}, u32[]{:S(2)}, u32[]{:S(2)}) async-start(bf16[4,320,256]{2,1,0:T(8,128)(2,1)} %get-tuple-element.24), calls=%async_computation.2 | async-start | bytes 1310720 | tf_op jit(solution)/shard_map/all_to_all | solution.py:513
  33.9 5.6 %o_pieces.1 = bf16[8,256,256]{2,1,0:T(8,128)(2,1)} custom-call(s32[1]{0:T(128)} %bitcast.2.place, bf16[256,8192]{1,0:T(8,128)(2,1)} %o_ref.1, f32[2,64]{1,0:T(2,128)} %scales.1), custom_call_target="tpu_custom_call" | custom-call | tf_op jit(solution)/shard_map/o_pieces/pallas_call | solution.py:145
  39.5 10.8 %all-to-all-done.2.rest_1_ = bf16[4,320,256]{2,1,0:T(8,128)(2,1)S(1)} async-done(((bf16[4,320,256]{2,1,0:T(8,128)(2,1)}), bf16[4,320,256]{2,1,0:T(8,128)(2,1)S(1)}, u32[]{:S(2)}, u32[]{:S(2)}) %all-to-all-start.2) | async-done | bytes 655392 | tf_op jit(solution)/shard_map/all_to_all | solution.py:513
  50.3 3.7 %all-to-all-start = ((bf16[8,256,256]{2,1,0:T(8,128)(2,1)}), bf16[8,256,256]{2,1,0:T(8,128)(2,1)S(1)}, u32[]{:S(2)}, u32[]{:S(2)}) async-start(bf16[8,256,256]{2,1,0:T(8,128)(2,1)} %o_pieces.1), calls=%async_computation | async-start | bytes 2097152 | tf_op jit(solution)/shard_map/all_to_all | solution.py:573
  55.9 5.4 %deal.1 = (bf16[384,1024]{1,0:T(8,128)(2,1)S(1)}, bf16[384,1024]{1,0:T(8,128)(2,1)}, f32[8,768]{1,0:T(8,128)S(1)}, f32[192,128]{1,0:T(8,128)S(1)}) custom-call(s32[2]{0:T(128)S(1)} %pad_add_fusion.2.place, s32[16]{0:T(128)S(1)} %copy-done.12, s32[16]{0:T(128)S(1)} %copy-done.14, bf16[1024,1536]{1,0:T(8,128)(2,1)S(1)} %copy-done), custom_call_target="tpu_custom_call" | custom-call | tf_op jit(solution)/shard_map/deal/pallas_call | solution.py:205
  63.3 3.3 %collective-permute-done.3 = f32[8,768]{1,0:T(8,128)S(1)} collective-permute-done((f32[8,768]{1,0:T(8,128)S(1)}, f32[8,768]{1,0:T(8,128)S(1)}, u32[]{:S(2)}, u32[]{:S(2)}) %collective-permute-start.3) | collective-permute-done | bytes 24608 | tf_op jit(solution)/shard_map/ppermute | solution.py:460
  68.0 2.9 %collective-permute-done.4 = f32[8,768]{1,0:T(8,128)S(1)} collective-permute-done((f32[8,768]{1,0:T(8,128)S(1)}, f32[8,768]{1,0:T(8,128)S(1)}, u32[]{:S(2)}, u32[]{:S(2)}) %collective-permute-start.4) | collective-permute-done | bytes 24608 | tf_op jit(solution)/shard_map/ppermute | solution.py:460
  70.9 5.0 %collective-permute-start.5 = (f32[8,768]{1,0:T(8,128)S(1)}, f32[8,768]{1,0:T(8,128)S(1)}, u32[]{:S(2)}, u32[]{:S(2)}) collective-permute-start(f32[8,768]{1,0:T(8,128)S(1)} %add.22), channel_id=1, source_target_pairs={{0,4},{1,5},{2,6},{3,7},{4,0},{5,1},{6,2},{7,3},{8,12},{9,13},{10,... | collective-permute-start | bytes 73736 | tf_op jit(solution)/shard_map/ppermute | solution.py:460
  83.9 12.3 %collective-permute-done.8.keep2 = bf16[384,1024]{1,0:T(8,128)(2,1)S(1)} collective-permute-done((bf16[384,1024]{1,0:T(8,128)(2,1)S(1)}, bf16[384,1024]{1,0:T(8,128)(2,1)S(1)}, u32[]{:S(2)}, u32[]{:S(2)}) %collective-permute-start.8) | collective-permute-done | bytes 786464 | tf_op jit(solution)/shard_map/ppermute | solution.py:460
  98.6 13.7 %collective-permute-done.9.got2 = bf16[384,1024]{1,0:T(8,128)(2,1)S(1)} collective-permute-done((bf16[384,1024]{1,0:T(8,128)(2,1)}, bf16[384,1024]{1,0:T(8,128)(2,1)S(1)}, u32[]{:S(2)}, u32[]{:S(2)}) %collective-permute-start.9) | collective-permute-done | bytes 786464 | tf_op jit(solution)/shard_map/ppermute | solution.py:524
  122.1 7.4 %project.1 = (bf16[192,1024]{1,0:T(8,128)(2,1)S(1)}, bf16[192,1024]{1,0:T(8,128)(2,1)S(1)}, bf16[192,1024]{1,0:T(8,128)(2,1)S(1)}, bf16[192,1024]{1,0:T(8,128)(2...) custom-call(s32[3]{0:T(128)S(1)} %pad_add_fusion.3.place, ...), custom_call_target="tpu_custom_call" | custom-call | tf_op jit(solution)/shard_map/project/pallas_call | solution.py:297
  133.7 3.9 %collective-permute-start.18 = (bf16[192,256]{1,0:T(8,128)(2,1)S(1)}, bf16[192,256]{1,0:T(8,128)(2,1)S(1)}, u32[]{:S(2)}, u32[]{:S(2)}) collective-permute-start(bf16[192,256]{1,0:T(8,128)(2,1)S(1)} %get-tuple-element.28), channel_id=1, source_target_pairs={{0,6},{1,7},{2,4},{3,5},{4,2},{5,3},{6,0},{7,1},{8,14},{9,15},{10,... | collective-permute-start | bytes 294920 | tf_op jit(solution)/shard_map/ppermute | solution.py:460
  139.5 4.5 %collective-permute-done.17.refs_2_ = bf16[192,256]{1,0:T(8,128)(2,1)S(1)} collective-permute-done((bf16[192,256]{1,0:T(8,128)(2,1)S(1)}, bf16[192,256]{1,0:T(8,128)(2,1)S(1)}, u32[]{:S(2)}, u32[]{:S(2)}) %collective-permute-start.17) | collective-permute-done | bytes 98336 | tf_op jit(solution)/shard_map/ppermute | solution.py:460
  155.5 10.4 %collective-permute-done.20.refs_1_ = bf16[192,1024]{1,0:T(8,128)(2,1)} collective-permute-done((bf16[192,1024]{1,0:T(8,128)(2,1)}, bf16[192,1024]{1,0:T(8,128)(2,1)}, u32[]{:S(2)}, u32[]{:S(2)}) %collective-permute-start.20) | collective-permute-done | bytes 393248 | tf_op jit(solution)/shard_map/ppermute | solution.py:460
  165.9 14.5 %collective-permute-done.21.refs_2_ = bf16[192,1024]{1,0:T(8,128)(2,1)} collective-permute-done((bf16[192,1024]{1,0:T(8,128)(2,1)}, bf16[192,1024]{1,0:T(8,128)(2,1)}, u32[]{:S(2)}, u32[]{:S(2)}) %collective-permute-start.21) | collective-permute-done | bytes 393248 | tf_op jit(solution)/shard_map/ppermute | solution.py:460
  180.4 4.5 %attend.1.refs_4_ = bf16[192,1024]{1,0:T(8,128)(2,1)} custom-call(s32[3]{0:T(128)} %pad_add_fusion.1.place, s32[16]{0:T(128)} %lens.5, s32[16]{0:T(128)} %dest.5, f32[192,128]{1,0:T(8,128)} %get-tuple-element.38.cosine, f32[192,128]{1,0:T(8,128)} %get-tuple-element.39.sine, bf16[192,256]{1,0:T(8,128)(2,1)} %key_value.1.own_kv, bf16[192,256]{1,0:T(8,128)(2,1)} %copy-done.21, ...), custom_call_target="tpu_custom_call" | custom-call | tf_op jit(solution)/shard_map/attend/pallas_call | solution.py:388
  184.9 7.0 %collective-permute-start.23 = (bf16[192,1024]{1,0:T(8,128)(2,1)}, bf16[192,1024]{1,0:T(8,128)(2,1)S(1)}, u32[]{:S(2)}, u32[]{:S(2)}) collective-permute-start(bf16[192,1024]{1,0:T(8,128)(2,1)} %attend.1.refs_4_), channel_id=1, source_target_pairs={{0,2},{1,3},{2,0},{3,1},{4,6},{5,7},{6,4},{7,5},{8,10},{9,11},{10,... | collective-permute-start | bytes 1179656 | tf_op jit(solution)/shard_map/ppermute | solution.py:460
  194.9 10.8 %collective-permute-done.23.refs_5_ = bf16[192,1024]{1,0:T(8,128)(2,1)S(1)} collective-permute-done((bf16[192,1024]{1,0:T(8,128)(2,1)}, bf16[192,1024]{1,0:T(8,128)(2,1)S(1)}, u32[]{:S(2)}, u32[]{:S(2)}) %collective-permute-start.23) | collective-permute-done | bytes 393248 | tf_op jit(solution)/shard_map/ppermute | solution.py:460
  206.3 15.6 %collective-permute-done.24.refs_6_ = bf16[192,1024]{1,0:T(8,128)(2,1)S(1)} collective-permute-done((bf16[192,1024]{1,0:T(8,128)(2,1)}, bf16[192,1024]{1,0:T(8,128)(2,1)S(1)}, u32[]{:S(2)}, u32[]{:S(2)}) %collective-permute-start.24) | collective-permute-done | bytes 393248 | tf_op jit(solution)/shard_map/ppermute | solution.py:460
  224.0 5.7 %collective-permute-done.28.refs_10_ = bf16[192,1024]{1,0:T(8,128)(2,1)S(1)} collective-permute-done((bf16[192,1024]{1,0:T(8,128)(2,1)S(1)}, bf16[192,1024]{1,0:T(8,128)(2,1)S(1)}, u32[]{:S(2)}, u32[]{:S(2)}) %collective-permute-start.28) | collective-permute-done | bytes 393248 | tf_op jit(solution)/shard_map/ppermute | solution.py:460
  229.7 4.2 %collective-permute-done.29.refs_11_ = bf16[192,1024]{1,0:T(8,128)(2,1)S(1)} collective-permute-done((bf16[192,1024]{1,0:T(8,128)(2,1)S(1)}, bf16[192,1024]{1,0:T(8,128)(2,1)S(1)}, u32[]{:S(2)}, u32[]{:S(2)}) %collective-permute-start.29) | collective-permute-done | bytes 393248 | tf_op jit(solution)/shard_map/ppermute | solution.py:460
  235.9 10.1 %output.1 = bf16[1024,768]{1,0:T(8,128)(2,1)} custom-call(s32[4]{0:T(128)S(1)} %pad_add_fusion.place, s32[16]{0:T(128)S(1)} %copy-done.13, s32[16]{0:T(128)S(1)} %copy-done.15, bf16[8,256,256]{2,1,0:T(8,128)(2,1)S(1)} %all-to-all-done.refs_0_, bf16[8,256,256]{2,1,0:T(8,128)(2,1)S(1)} %collective-permute-done.refs_1_, ...), custom_call_target="tpu_custom_call" | custom-call | tf_op jit(solution)/shard_map/output/pallas_call | solution.py:444
  (115 shorter events, 52.9 us)
Async XLA Ops:
  30.3 20.0 %all-to-all-start.2 = ((bf16[4,320,256]{2,1,0:T(8,128)(2,1)}), bf16[4,320,256]{2,1,0:T(8,128)(2,1)S(1)}, u32[]{:S(2)}, u32[]{:S(2)}) async-start(bf16[4,320,256]{2,1,0:T(8,128)(2,1)} %get-tuple-element.24), calls=%async_computation.2 | async-start | bytes 1310720 | tf_op jit(solution)/shard_map/all_to_all | solution.py:513
  50.3 46.8 %all-to-all-start = ((bf16[8,256,256]{2,1,0:T(8,128)(2,1)}), bf16[8,256,256]{2,1,0:T(8,128)(2,1)S(1)}, u32[]{:S(2)}, u32[]{:S(2)}) async-start(bf16[8,256,256]{2,1,0:T(8,128)(2,1)} %o_pieces.1), calls=%async_computation | async-start | bytes 2097152 | tf_op jit(solution)/shard_map/all_to_all | solution.py:573
  70.9 9.4 %collective-permute-start.5 = (f32[8,768]{1,0:T(8,128)S(1)}, f32[8,768]{1,0:T(8,128)S(1)}, u32[]{:S(2)}, u32[]{:S(2)}) collective-permute-start(f32[8,768]{1,0:T(8,128)S(1)} %add.22), channel_id=1, source_target_pairs={{0,4},{1,5},{2,6},{3,7},{4,0},{5,1},{6,2},{7,3},{8,12},{9,13},{10,... | collective-permute-start | bytes 73736 | tf_op jit(solution)/shard_map/ppermute | solution.py:460
  75.8 7.2 %collective-permute-start.7 = (bf16[384,1024]{1,0:T(8,128)(2,1)}, bf16[384,1024]{1,0:T(8,128)(2,1)S(1)}, u32[]{:S(2)}, u32[]{:S(2)}) collective-permute-start(bf16[384,1024]{1,0:T(8,128)(2,1)} %get-tuple-element.22), channel_id=1, source_target_pairs={{0,8},{8,0},{1,9},{9,1},{2,10},{10,2},{3,11},{11,3},{4,12},{12,4},... | collective-permute-start | bytes 2359304 | tf_op jit(solution)/shard_map/ppermute | solution.py:460
  75.8 20.3 %collective-permute-start.8 = (bf16[384,1024]{1,0:T(8,128)(2,1)S(1)}, bf16[384,1024]{1,0:T(8,128)(2,1)S(1)}, u32[]{:S(2)}, u32[]{:S(2)}) collective-permute-start(bf16[384,1024]{1,0:T(8,128)(2,1)S(1)} %get-tuple-element.21.keep), channel_id=1, source_target_pairs={{0,1},{1,0},{2,3},{3,2},{4,5},{5,4},{6,7},{7,6},{8,9},{9,8},{10,11... | collective-permute-start | bytes 2359304 | tf_op jit(solution)/shard_map/ppermute | solution.py:460
  78.2 34.1 %collective-permute-start.9 = (bf16[384,1024]{1,0:T(8,128)(2,1)}, bf16[384,1024]{1,0:T(8,128)(2,1)S(1)}, u32[]{:S(2)}, u32[]{:S(2)}) collective-permute-start(bf16[384,1024]{1,0:T(8,128)(2,1)} %get-tuple-element.22), channel_id=1, source_target_pairs={{0,9},{1,8},{2,11},{3,10},{4,13},{5,12},{6,15},{7,14},{8,1},{9,0},... | collective-permute-start | bytes 2359304 | tf_op jit(solution)/shard_map/ppermute | solution.py:524
  80.4 33.4 %collective-permute-start.12 = (bf16[4,320,256]{2,1,0:T(8,128)(2,1)S(1)}, bf16[4,320,256]{2,1,0:T(8,128)(2,1)}, u32[]{:S(2)}, u32[]{:S(2)}) collective-permute-start(bf16[4,320,256]{2,1,0:T(8,128)(2,1)S(1)} %all_to_all.15.rest_0_), channel_id=1, source_target_pairs={{0,16},{16,0},{1,17},{17,1},{2,18},{18,2},{3,19},{19,3},{4,20},{20... | collective-permute-start | bytes 1966088 | tf_op jit(solution)/shard_map/ppermute | solution.py:460
  81.9 31.8 %collective-permute-start.13 = (bf16[4,320,256]{2,1,0:T(8,128)(2,1)S(1)}, bf16[4,320,256]{2,1,0:T(8,128)(2,1)}, u32[]{:S(2)}, u32[]{:S(2)}) collective-permute-start(bf16[4,320,256]{2,1,0:T(8,128)(2,1)S(1)} %all-to-all-done.2.rest_1_), channel_id=1, source_target_pairs={{0,16},{16,0},{1,17},{17,1},{2,18},{18,2},{3,19},{19,3},{4,20},{20... | collective-permute-start | bytes 1966088 | tf_op jit(solution)/shard_map/ppermute | solution.py:460
  83.9 32.3 %collective-permute-start.10 = (bf16[4,320,256]{2,1,0:T(8,128)(2,1)S(1)}, bf16[4,320,256]{2,1,0:T(8,128)(2,1)}, u32[]{:S(2)}, u32[]{:S(2)}) collective-permute-start(bf16[4,320,256]{2,1,0:T(8,128)(2,1)S(1)} %all_to_all.15.rest_0_), channel_id=1, source_target_pairs={{0,8},{8,0},{1,9},{9,1},{2,10},{10,2},{3,11},{11,3},{4,12},{12,4},... | collective-permute-start | bytes 1966088 | tf_op jit(solution)/shard_map/ppermute | solution.py:460
  97.1 56.0 %collective-permute-start.1 = (bf16[8,256,256]{2,1,0:T(8,128)(2,1)S(1)}, bf16[8,256,256]{2,1,0:T(8,128)(2,1)}, u32[]{:S(2)}, u32[]{:S(2)}) collective-permute-start(bf16[8,256,256]{2,1,0:T(8,128)(2,1)S(1)} %all-to-all-done.refs_0_), channel_id=1, source_target_pairs={{0,16},{16,0},{1,17},{17,1},{2,18},{18,2},{3,19},{19,3},{4,20},{20... | collective-permute-start | bytes 3145736 | tf_op jit(solution)/shard_map/ppermute | solution.py:460
  116.2 78.0 %collective-permute-start = (bf16[8,256,256]{2,1,0:T(8,128)(2,1)S(1)}, bf16[8,256,256]{2,1,0:T(8,128)(2,1)S(1)}, u32[]{:S(2)}, u32[]{:S(2)}) collective-permute-start(bf16[8,256,256]{2,1,0:T(8,128)(2,1)S(1)} %all-to-all-done.refs_0_), channel_id=1, source_target_pairs={{0,8},{8,0},{1,9},{9,1},{2,10},{10,2},{3,11},{11,3},{4,12},{12,4},... | collective-permute-start | bytes 3145736 | tf_op jit(solution)/shard_map/ppermute | solution.py:460
  133.2 10.8 %collective-permute-start.17 = (bf16[192,256]{1,0:T(8,128)(2,1)S(1)}, bf16[192,256]{1,0:T(8,128)(2,1)S(1)}, u32[]{:S(2)}, u32[]{:S(2)}) collective-permute-start(bf16[192,256]{1,0:T(8,128)(2,1)S(1)} %get-tuple-element.27), channel_id=1, source_target_pairs={{0,4},{1,5},{2,6},{3,7},{4,0},{5,1},{6,2},{7,3},{8,12},{9,13},{10,... | collective-permute-start | bytes 294920 | tf_op jit(solution)/shard_map/ppermute | solution.py:460
  133.7 10.3 %collective-permute-start.18 = (bf16[192,256]{1,0:T(8,128)(2,1)S(1)}, bf16[192,256]{1,0:T(8,128)(2,1)S(1)}, u32[]{:S(2)}, u32[]{:S(2)}) collective-permute-start(bf16[192,256]{1,0:T(8,128)(2,1)S(1)} %get-tuple-element.28), channel_id=1, source_target_pairs={{0,6},{1,7},{2,4},{3,5},{4,2},{5,3},{6,0},{7,1},{8,14},{9,15},{10,... | collective-permute-start | bytes 294920 | tf_op jit(solution)/shard_map/ppermute | solution.py:460
  148.1 17.7 %collective-permute-start.20 = (bf16[192,1024]{1,0:T(8,128)(2,1)}, bf16[192,1024]{1,0:T(8,128)(2,1)}, u32[]{:S(2)}, u32[]{:S(2)}) collective-permute-start(bf16[192,1024]{1,0:T(8,128)(2,1)} %copy-done.18), channel_id=1, source_target_pairs={{0,2},{1,3},{2,0},{3,1},{4,6},{5,7},{6,4},{7,5},{8,10},{9,11},{10,... | collective-permute-start | bytes 1179656 | tf_op jit(solution)/shard_map/ppermute | solution.py:460
  150.2 30.1 %collective-permute-start.21 = (bf16[192,1024]{1,0:T(8,128)(2,1)}, bf16[192,1024]{1,0:T(8,128)(2,1)}, u32[]{:S(2)}, u32[]{:S(2)}) collective-permute-start(bf16[192,1024]{1,0:T(8,128)(2,1)} %copy-done.17), channel_id=1, source_target_pairs={{0,4},{1,5},{2,6},{3,7},{4,0},{5,1},{6,2},{7,3},{8,12},{9,13},{10,... | collective-permute-start | bytes 1179656 | tf_op jit(solution)/shard_map/ppermute | solution.py:460
  151.6 28.8 %collective-permute-start.22 = (bf16[192,1024]{1,0:T(8,128)(2,1)}, bf16[192,1024]{1,0:T(8,128)(2,1)}, u32[]{:S(2)}, u32[]{:S(2)}) collective-permute-start(bf16[192,1024]{1,0:T(8,128)(2,1)} %copy-done.16), channel_id=1, source_target_pairs={{0,6},{1,7},{2,4},{3,5},{4,2},{5,3},{6,0},{7,1},{8,14},{9,15},{10,... | collective-permute-start | bytes 1179656 | tf_op jit(solution)/shard_map/ppermute | solution.py:460
  153.1 80.8 %collective-permute-start.2 = (bf16[8,256,256]{2,1,0:T(8,128)(2,1)}, bf16[8,256,256]{2,1,0:T(8,128)(2,1)S(1)}, u32[]{:S(2)}, u32[]{:S(2)}) collective-permute-start(bf16[8,256,256]{2,1,0:T(8,128)(2,1)} %collective-permute-done.1.refs_2_), channel_id=1, source_target_pairs={{0,8},{8,0},{1,9},{9,1},{2,10},{10,2},{3,11},{11,3},{4,12},{12,4},... | collective-permute-start | bytes 3145736 | tf_op jit(solution)/shard_map/ppermute | solution.py:460
  184.9 20.8 %collective-permute-start.23 = (bf16[192,1024]{1,0:T(8,128)(2,1)}, bf16[192,1024]{1,0:T(8,128)(2,1)S(1)}, u32[]{:S(2)}, u32[]{:S(2)}) collective-permute-start(bf16[192,1024]{1,0:T(8,128)(2,1)} %attend.1.refs_4_), channel_id=1, source_target_pairs={{0,2},{1,3},{2,0},{3,1},{4,6},{5,7},{6,4},{7,5},{8,10},{9,11},{10,... | collective-permute-start | bytes 1179656 | tf_op jit(solution)/shard_map/ppermute | solution.py:460
  191.9 30.0 %collective-permute-start.24 = (bf16[192,1024]{1,0:T(8,128)(2,1)}, bf16[192,1024]{1,0:T(8,128)(2,1)S(1)}, u32[]{:S(2)}, u32[]{:S(2)}) collective-permute-start(bf16[192,1024]{1,0:T(8,128)(2,1)} %attend.1.refs_4_), channel_id=1, source_target_pairs={{0,4},{1,5},{2,6},{3,7},{4,0},{5,1},{6,2},{7,3},{8,12},{9,13},{10,... | collective-permute-start | bytes 1179656 | tf_op jit(solution)/shard_map/ppermute | solution.py:460
  191.9 30.6 %collective-permute-start.25 = (bf16[192,1024]{1,0:T(8,128)(2,1)}, bf16[192,1024]{1,0:T(8,128)(2,1)S(1)}, u32[]{:S(2)}, u32[]{:S(2)}) collective-permute-start(bf16[192,1024]{1,0:T(8,128)(2,1)} %attend.1.refs_4_), channel_id=1, source_target_pairs={{0,6},{1,7},{2,4},{3,5},{4,2},{5,3},{6,0},{7,1},{8,14},{9,15},{10,... | collective-permute-start | bytes 1179656 | tf_op jit(solution)/shard_map/ppermute | solution.py:460
  194.3 29.8 %collective-permute-start.26 = (bf16[192,1024]{1,0:T(8,128)(2,1)}, bf16[192,1024]{1,0:T(8,128)(2,1)S(1)}, u32[]{:S(2)}, u32[]{:S(2)}) collective-permute-start(bf16[192,1024]{1,0:T(8,128)(2,1)} %attend.1.refs_4_), channel_id=1, source_target_pairs={{0,1},{1,0},{2,3},{3,2},{4,5},{5,4},{6,7},{7,6},{8,9},{9,8},{10,11... | collective-permute-start | bytes 1179656 | tf_op jit(solution)/shard_map/ppermute | solution.py:460
  205.7 18.4 %collective-permute-start.27 = (bf16[192,1024]{1,0:T(8,128)(2,1)S(1)}, bf16[192,1024]{1,0:T(8,128)(2,1)S(1)}, u32[]{:S(2)}, u32[]{:S(2)}) collective-permute-start(bf16[192,1024]{1,0:T(8,128)(2,1)S(1)} %collective-permute-done.23.refs_5_), channel_id=1, source_target_pairs={{0,1},{1,0},{2,3},{3,2},{4,5},{5,4},{6,7},{7,6},{8,9},{9,8},{10,11... | collective-permute-start | bytes 1179656 | tf_op jit(solution)/shard_map/ppermute | solution.py:460
  221.9 7.8 %collective-permute-start.28 = (bf16[192,1024]{1,0:T(8,128)(2,1)S(1)}, bf16[192,1024]{1,0:T(8,128)(2,1)S(1)}, u32[]{:S(2)}, u32[]{:S(2)}) collective-permute-start(bf16[192,1024]{1,0:T(8,128)(2,1)S(1)} %collective-permute-done.24.refs_6_), channel_id=1, source_target_pairs={{0,1},{1,0},{2,3},{3,2},{4,5},{5,4},{6,7},{7,6},{8,9},{9,8},{10,11... | collective-permute-start | bytes 1179656 | tf_op jit(solution)/shard_map/ppermute | solution.py:460
  222.5 11.4 %collective-permute-start.29 = (bf16[192,1024]{1,0:T(8,128)(2,1)S(1)}, bf16[192,1024]{1,0:T(8,128)(2,1)S(1)}, u32[]{:S(2)}, u32[]{:S(2)}) collective-permute-start(bf16[192,1024]{1,0:T(8,128)(2,1)S(1)} %collective-permute-done.25.refs_7_), channel_id=1, source_target_pairs={{0,1},{1,0},{2,3},{3,2},{4,5},{5,4},{6,7},{7,6},{8,9},{9,8},{10,11... | collective-permute-start | bytes 1179656 | tf_op jit(solution)/shard_map/ppermute | solution.py:460
  (33 other events, 376.9 us)

commit v2 on v0

v2 whole, which is shorter than its diff:
```python
import functools
import math

import jax
import jax.numpy as jnp
from jax import lax
from jax.experimental import pallas as pl
from jax.experimental.pallas import tpu as pltpu
from jax.sharding import PartitionSpec as P

D = 8192
HD = 128
BLOCKS = 4

epsilon = 1e-06
rope_base = 1000000.0

F32 = jnp.float32
BF16 = jnp.bfloat16
NN = (((1,), (0,)), ((), ()))
NT = (((1,), (1,)), ((), ()))
TN = (((0,), (0,)), ((), ()))
VMEM = 58 << 20


def dot(a, b, dims=NN):
    return lax.dot_general(a, b, dims, preferred_element_type=F32)


def in_vmem():
    return pl.BlockSpec(memory_space=pltpu.VMEM)


def in_smem():
    return pl.BlockSpec(memory_space=pltpu.SMEM)


def anywhere():
    return pl.BlockSpec(memory_space=pltpu.HBM)


def start_copies(pairs, sems, first=0):
    copies = [
        pltpu.make_async_copy(source, target, sems.at[first + i])
        for i, (source, target) in enumerate(pairs)
    ]
    for copy in copies:
        copy.start()
    return copies


def aligned(value, size):
    return pl.ds(pl.multiple_of(value, size), size)


GROUP, UNIT, SIDE, QUARTER, KV_HEAD = range(5)


def row_facts(lens, dest, source, target, rows, slot):
    zero = jnp.int32(0)
    start, seen = zero, zero
    full = [zero, zero]
    short = [[zero, zero, zero] for _ in range(3)]
    for i in range(rows):
        mine = dest[source * rows + i] == target
        size = jnp.where(mine, lens[source * rows + i], 0)
        is_full = size == slot
        is_short = jnp.logical_and(mine, size != slot)
        full = [jnp.where(is_full, i, full[0]), jnp.where(is_full, start, full[1])]
        for k in range(3):
            hit = jnp.logical_and(is_short, seen == k)
            for e, value in enumerate((jnp.int32(i), start, size)):
                short[k][e] = jnp.where(hit, value, short[k][e])
        seen = seen + jnp.where(is_short, 1, 0)
        start = start + size
    return full, short


def pieces_kernel(units, place, qs, ks, vs, os, q_hbm, k_hbm, v_hbm, o_hbm, *rest):
    outs, o_out = rest[:units], rest[units]
    q_buf, k_buf, v_buf, o_buf, pieces, o_pieces, in_sems, out_sems = rest[units + 1 :]
    unit, quarter, head = place[UNIT], place[QUARTER], place[KV_HEAD]
    _, size, own = q_buf.shape
    part = k_buf.shape[1]
    width = min(size, own)
    ranks, o_rows, features = o_pieces.shape
    copies = []
    for k in range(units):
        at = ((unit ^ k) * 4 + quarter) * size
        copies.append(
            start_copies(
                [
                    (q_hbm.at[aligned(at, size)], q_buf.at[k]),
                    (k_hbm.at[:, aligned(at, size)], k_buf.at[k]),
                    (v_hbm.at[:, aligned(at, size)], v_buf.at[k]),
                ],
                in_sems,
                3 * k,
            )
        )
    (o_copy,) = start_copies(
        [(o_hbm.at[aligned(quarter * o_rows, o_rows)], o_buf)], in_sems, 3 * units
    )
    sent = []
    for k in range(units):
        for copy in copies[k]:
            copy.wait()
        base = ((unit ^ k) * 4 + quarter) * (size // HD)
        for i in range(size // HD):
            rows = slice(i * HD, (i + 1) * HD)
            for h in range(own // HD):
                cols = slice(h * HD, (h + 1) * HD)
                scaled = q_buf[k, rows, cols].astype(F32) * qs[h, base + i]
                pieces[k, rows, cols] = scaled.astype(BF16)
            turn, lane = divmod(i * HD, width)
            at = size + 2 * part * turn
            lanes = slice(lane, lane + HD)
            pieces[k, at : at + part, lanes] = (
                k_buf[k, :, rows].astype(F32) * ks[head, base + i]
            ).astype(BF16)
            pieces[k, at + part : at + 2 * part, lanes] = (
                v_buf[k, :, rows].astype(F32) * vs[head, base + i]
            ).astype(BF16)
        if width < own:
            pieces[k, size:, width:] = jnp.zeros((2 * part, own - width), BF16)
        sent += start_copies([(pieces.at[k], outs[k])], out_sems, k)
    o_copy.wait()
    o_head = quarter * o_rows // HD
    for rank in range(ranks):
        for i in range(features // HD):
            block = rank * (features // HD) + i
            scaled = o_buf[:, block * HD : (block + 1) * HD].astype(F32) * os[o_head, block]
            o_pieces[rank, :, i * HD : (i + 1) * HD] = scaled.astype(BF16)
    sent += start_copies([(o_pieces, o_out)], out_sems, units)
    for copy in sent:
        copy.wait()


def weight_pieces(
    place, q_values, q_scales, k_values, k_scales, v_values, v_scales, o_values, o_scales, ranks
):
    units = ranks // 2
    o_shape = (ranks, o_values.shape[0] // 4, o_values.shape[1] // ranks)
    own = q_values.shape[1]
    part = k_values.shape[0]
    size = q_values.shape[0] // units // 4
    rows = size + 2 * part * max(1, size // own)
    outs = pl.pallas_call(
        functools.partial(pieces_kernel, units),
        in_specs=[in_smem()] * 5 + [anywhere()] * 4,
        out_specs=[anywhere()] * (units + 1),
        out_shape=[jax.ShapeDtypeStruct((rows, own), BF16)] * units
        + [jax.ShapeDtypeStruct(o_shape, BF16)],
        scratch_shapes=[
            pltpu.VMEM((units, size, own), BF16),
            pltpu.VMEM((units, part, size), BF16),
            pltpu.VMEM((units, part, size), BF16),
            pltpu.VMEM((o_shape[1], o_values.shape[1]), BF16),
            pltpu.VMEM((units, rows, own), BF16),
            pltpu.VMEM(o_shape, BF16),
            pltpu.SemaphoreType.DMA((3 * units + 1,)),
            pltpu.SemaphoreType.DMA((units + 1,)),
        ],
        compiler_params=pltpu.CompilerParams(vmem_limit_bytes=VMEM),
        name="weight_pieces",
    )(place, q_scales.T, k_scales, v_scales, o_scales, q_values, k_values, v_values, o_values)
    return outs[:units], outs[units]


def deal_kernel(rows, slot, count, place, lens, dest, home, *rest):
    keep, send, pos, pick = rest[count:]
    step = pl.program_id(0)
    group, block = place[GROUP], place[UNIT] & (BLOCKS - 1)

    @pl.when(step == 0)
    def _():
        column = lax.broadcasted_iota(jnp.int32, (slot, 1), 0)
        lane = lax.broadcasted_iota(jnp.int32, (slot, rows * slot), 1)
        for turn in range(2):
            full, short = row_facts(lens, dest, group, group ^ turn, rows, slot)
            first = short[0][2]
            second = first + short[1][2]
            from_short = jnp.where(
                column < first,
                short[0][0] * slot + column,
                jnp.where(
                    column < second,
                    short[1][0] * slot + column - first,
                    short[2][0] * slot + column - second,
                ),
            )
            for kind, index in enumerate((full[0] * slot + column, from_short)):
                at = (turn * 2 + kind) * slot
                pick[at : at + slot, :] = jnp.where(lane == index, 1.0, 0.0).astype(BF16)
        _, short = row_facts(lens, dest, group ^ (block >> 1), group, rows, slot)
        first = short[0][2]
        second = first + short[1][2]
        begin = jnp.where(column < first, 0, jnp.where(column < second, first, second))
        place_in_row = column - jnp.where((block & 1) == 1, begin, 0)
        pos[...] = jnp.broadcast_to(place_in_row.astype(F32), pos.shape)

    taken = dot(pick[...], home[...], NT)
    half = 2 * slot
    keep[...] = taken[:half].astype(BF16)
    send[...] = taken[half:].astype(BF16)


def deal(place, lens, dest, home, rows, slot, after):
    features = home.shape[0]
    width = min(features, 256)
    tokens = BLOCKS * slot
    return pl.pallas_call(
        functools.partial(deal_kernel, rows, slot, len(after)),
        grid=(features // width,),
        in_specs=[
            in_smem(),
            in_smem(),
            in_smem(),
            pl.BlockSpec((width, home.shape[1]), lambda i: (i, 0)),
        ]
        + [anywhere()] * len(after),
        out_specs=[
            pl.BlockSpec((tokens // 2, width), lambda i: (0, i)),
            pl.BlockSpec((tokens // 2, width), lambda i: (0, i)),
            pl.BlockSpec((slot, 128), lambda i: (0, 0)),
        ],
        out_shape=[
            jax.ShapeDtypeStruct((tokens // 2, features), BF16),
            jax.ShapeDtypeStruct((tokens // 2, features), BF16),
            jax.ShapeDtypeStruct((slot, 128), F32),
        ],
        scratch_shapes=[
            pltpu.VMEM((tokens, rows * slot), BF16),
        ],
        compiler_params=pltpu.CompilerParams(vmem_limit_bytes=VMEM),
        name="deal",
    )(place, lens, dest, home, *after)


def collect_kernel(count, extra, *refs):
    tokens, pieces = refs[:4], refs[4 : 4 + count]
    out, sums = refs[4 + count + extra : 6 + count + extra]
    x_buf, buf, x_sems, sems, out_sems = refs[-5:]
    copies = start_copies([(ref, buf.at[k]) for k, ref in enumerate(pieces)], sems)
    x_copies = start_copies([(ref, x_buf.at[i]) for i, ref in enumerate(tokens)], x_sems)
    sent = []
    for k, copy in enumerate(copies):
        copy.wait()
        sent += start_copies([(buf.at[k], out.at[k])], out_sems, k)
    _, half, features = x_buf.shape
    for i in range(2):
        total = None
        for j in (i, i + 2):
            x_copies[j].wait()
            for at in range(features // 128):
                piece = x_buf[j, :, at * 128 : (at + 1) * 128].astype(F32)
                total = piece * piece if total is None else total + piece * piece
        sums[:, i * half : (i + 1) * half] = jnp.broadcast_to(
            jnp.sum(total.T, axis=0, keepdims=True), (8, half)
        )
    for copy in sent:
        copy.wait()


def collect(tokens, pieces, after):
    count = len(pieces)
    half, features = tokens[0].shape
    return pl.pallas_call(
        functools.partial(collect_kernel, count, len(after)),
        in_specs=[anywhere()] * (4 + count + len(after)),
        out_specs=[anywhere(), in_vmem()],
        out_shape=[
            jax.ShapeDtypeStruct((count, *pieces[0].shape), BF16),
            jax.ShapeDtypeStruct((8, 2 * half), F32),
        ],
        scratch_shapes=[
            pltpu.VMEM((4, half, features), BF16),
            pltpu.VMEM((count, *pieces[0].shape), BF16),
            pltpu.SemaphoreType.DMA((4,)),
            pltpu.SemaphoreType.DMA((count,)),
            pltpu.SemaphoreType.DMA((count,)),
        ],
        compiler_params=pltpu.CompilerParams(vmem_limit_bytes=VMEM),
        name="collect",
    )(*tokens, *pieces, *after)


def gate_kernel(*refs):
    pass


def gate(through, after):
    count = len(through)
    return pl.pallas_call(
        gate_kernel,
        in_specs=[anywhere()] * (count + len(after)),
        out_specs=[anywhere()] * count,
        out_shape=[jax.ShapeDtypeStruct(value.shape, value.dtype) for value in through],
        input_output_aliases={i: i for i in range(count)},
        compiler_params=pltpu.CompilerParams(vmem_limit_bytes=VMEM),
        name="gate",
    )(*through, *after)


def normalize_kernel(units, place, *rest):
    squares, (gain, keep, got, keep2, got2) = rest[:units], rest[units : units + 5]
    out, x_buf, normed, x_sems, out_sems = rest[units + 5 :]
    side = place[SIDE]
    _, half, features = x_buf.shape
    copies = start_copies(
        [(ref, x_buf.at[i]) for i, ref in enumerate((keep, got, keep2, got2))], x_sems
    )
    total = squares[0][...]
    for ref in squares[1:]:
        total = total + ref[...]
    inverse = lax.rsqrt(total / D + epsilon).T[:, :1]
    sent = []
    for i in range(4):
        at = side if i < 2 else 1 - side
        lanes = aligned(at * features, features)
        rows = slice((i & 1) * half, ((i & 1) + 1) * half)
        copies[i].wait()
        wide_rows = x_buf[i].astype(F32)
        normed[i] = (wide_rows * inverse[rows] * gain[:, lanes]).astype(BF16)
        sent += start_copies([(normed.at[i], out.at[rows, lanes])], out_sems, i)
    for copy in sent:
        copy.wait()


def normalize(place, squares, gain, keep, got, keep2, got2):
    half, features = keep.shape
    return pl.pallas_call(
        functools.partial(normalize_kernel, len(squares)),
        in_specs=[in_smem()] + [in_vmem()] * (len(squares) + 1) + [anywhere()] * 4,
        out_specs=anywhere(),
        out_shape=jax.ShapeDtypeStruct((2 * half, 2 * features), BF16),
        scratch_shapes=[
            pltpu.VMEM((4, half, features), BF16),
            pltpu.VMEM((4, half, features), BF16),
            pltpu.SemaphoreType.DMA((4,)),
            pltpu.SemaphoreType.DMA((4,)),
        ],
        compiler_params=pltpu.CompilerParams(vmem_limit_bytes=VMEM),
        name="normalize",
    )(place, *squares, gain, keep, got, keep2, got2)


def project_kernel(units, place, normed, *rest):
    own_pieces, weights, outs = rest[:4], rest[4:8], rest[8 : 8 + units]
    weight, tokens, buf, x_sem, w_sems, out_sems = rest[8 + units :]
    unit, quarter = place[UNIT], place[QUARTER]
    count, wide = tokens.shape
    slot = count // BLOCKS
    own = weight.shape[3]
    size = wide // 4
    width = min(size, own)
    part = (weight.shape[2] - size) // (size // width)
    (x_copy,) = start_copies([(normed, tokens)], x_sem)
    copies = start_copies(
        [
            (
                weights[r].at[k - 1] if k else own_pieces[r],
                weight.at[quarter ^ r, (k >> 2) * 4 + ((unit ^ k) & 3)],
            )
            for k in range(units)
            for r in range(4)
        ],
        w_sems,
    )
    x_copy.wait()
    sent = []

    def hand_out(group, cols, index):
        for k in range(4 * group, 4 * group + 4):
            rows = aligned(((unit ^ k) & 3) * slot, slot)
            pair = (buf.at[group, rows, cols], outs[k].at[:, cols])
            sent.extend(start_copies([pair], out_sems, 5 * k + index))

    for group in range(units // BLOCKS):
        for k in range(4 * group, 4 * group + 4):
            for r in range(4):
                copies[k * 4 + r].wait()
            s = (unit ^ k) & 3
            value = None
            for q in range(4):
                term = dot(tokens[:, q * size : (q + 1) * size], weight[q, group * 4 + s, :size])
                value = term if value is None else value + term
            cols = aligned(s * own, own)
            buf[group, :, cols] = value.astype(BF16)
            hand_out(group, cols, k & 3)
        sources = slice(group * 4, group * 4 + 4)
        value = None
        for q in range(4):
            for e in range(size // width):
                at = q * size + e * width
                first = size + e * part
                middle, last = first + part // 2, first + part
                w = jnp.concatenate(
                    [
                        weight[q, sources, first:middle, :width].reshape(2 * part, width),
                        weight[q, sources, middle:last, :width].reshape(2 * part, width),
                    ],
                    axis=0,
                )
                term = dot(tokens[:, at : at + width], w, NT)
                value = term if value is None else value + term
        buf[group, :, 4 * own :] = value.astype(BF16)
        hand_out(group, pl.ds(4 * own, 4 * part), 4)
    for copy in sent:
        copy.wait()


def project(place, normed, own_pieces, weights, units):
    tokens, wide = normed.shape
    slot = tokens // BLOCKS
    rows, own = own_pieces[0].shape
    size = wide // 4
    part = (rows - size) // (size // min(size, own))
    groups = units // BLOCKS
    outs = pl.pallas_call(
        functools.partial(project_kernel, units),
        in_specs=[in_smem()] + [anywhere()] * 9,
        out_specs=[anywhere()] * units,
        out_shape=[jax.ShapeDtypeStruct((slot, 4 * own + 4 * part), BF16)] * units,
        scratch_shapes=[
            pltpu.VMEM((4, units, rows, own), BF16),
            pltpu.VMEM((tokens, wide), BF16),
            pltpu.VMEM((groups, tokens, 4 * own + 4 * part), BF16),
            pltpu.SemaphoreType.DMA((1,)),
            pltpu.SemaphoreType.DMA((4 * units,)),
            pltpu.SemaphoreType.DMA((5 * units,)),
        ],
        compiler_params=pltpu.CompilerParams(vmem_limit_bytes=VMEM),
        name="project",
    )(place, normed, *own_pieces, *weights)
    return outs


def key_value_kernel(units, cosine, sine, *refs):
    parts, (out, buf, sems) = refs[:units], refs[units:]
    wide = parts[0].shape[1] - buf.shape[2]
    copies = start_copies([(ref.at[:, wide:], buf.at[k]) for k, ref in enumerate(parts)], sems)
    value = None
    for k, copy in enumerate(copies):
        copy.wait()
        term = buf[k].astype(F32)
        value = term if value is None else value + term
    value = value.astype(BF16).astype(F32)
    keys, values = value[:, :HD], value[:, HD:]
    part = HD // 4
    lane = lax.broadcasted_iota(jnp.int32, keys.shape, 1)
    odd = (lane & part) != 0
    swapped = jnp.where(odd, pltpu.roll(keys, part, 1), pltpu.roll(keys, HD - part, 1))
    out[:, :HD] = (keys * cosine[...] + swapped * sine[...]).astype(BF16)
    out[:, HD:] = values.astype(BF16)


def key_value(parts, cosine, sine):
    shape = (parts[0].shape[0], parts[0].shape[1] // 5)
    return pl.pallas_call(
        functools.partial(key_value_kernel, len(parts)),
        in_specs=[in_vmem()] * 2 + [anywhere()] * len(parts),
        out_specs=in_vmem(),
        out_shape=jax.ShapeDtypeStruct(shape, BF16),
        scratch_shapes=[
            pltpu.VMEM((len(parts), *shape), BF16),
            pltpu.SemaphoreType.DMA((len(parts),)),
        ],
        name="key_value",
    )(cosine, sine, *parts)


def query_kernel(units, cosine, sine, *refs):
    parts, (out, buf, sems) = refs[:units], refs[units:]
    wide = out.shape[1]
    copies = start_copies([(ref.at[:, :wide], buf.at[k]) for k, ref in enumerate(parts)], sems)
    cos, sin = cosine[...], sine[...]
    for copy in copies:
        copy.wait()
    for head in range(wide // HD):
        at = slice(head * HD, (head + 1) * HD)
        query = buf[0, :, at].astype(F32)
        for k in range(1, units):
            query = query + buf[k, :, at].astype(F32)
        query = query.astype(BF16).astype(F32)
        swapped = jnp.concatenate([query[:, HD // 2 :], query[:, : HD // 2]], axis=1)
        out[:, at] = (query * cos + swapped * sin).astype(BF16)


def queries(parts, cosine, sine):
    shape = (parts[0].shape[0], parts[0].shape[1] // 5 * 4)
    return pl.pallas_call(
        functools.partial(query_kernel, len(parts)),
        in_specs=[in_vmem()] * 2 + [anywhere()] * len(parts),
        out_specs=in_vmem(),
        out_shape=jax.ShapeDtypeStruct(shape, BF16),
        scratch_shapes=[
            pltpu.VMEM((len(parts), *shape), BF16),
            pltpu.SemaphoreType.DMA((len(parts),)),
        ],
        name="queries",
    )(cosine, sine, *parts)


def attend_kernel(rows, slot, place, lens, dest, query, own_kv, other_kv, out):
    group, block, side = place[GROUP], place[UNIT] & (BLOCKS - 1), place[SIDE]
    _, short = row_facts(lens, dest, group ^ (block >> 1), group, rows, slot)
    many = (block & 1) == 1
    first = jnp.where(many, short[0][2], slot)
    second = jnp.where(many, first + short[1][2], slot)

    def segment(shape, axis):
        at = lax.broadcasted_iota(jnp.int32, shape, axis)
        return jnp.where(at >= first, 1, 0) + jnp.where(at >= second, 1, 0)

    shape = (slot, slot)
    allowed = jnp.logical_and(
        segment(shape, 0) == segment(shape, 1),
        lax.broadcasted_iota(jnp.int32, shape, 1) <= lax.broadcasted_iota(jnp.int32, shape, 0),
    )
    mine, theirs = own_kv[...].astype(F32), other_kv[...].astype(F32)
    even = jnp.where(side == 0, mine, theirs)
    odd = jnp.where(side == 0, theirs, mine)
    part = HD // 4

    def whole_head(index):
        pieces = []
        for b in range(2):
            at = slice((2 * index + b) * part, (2 * index + b + 1) * part)
            pieces += [even[:, at], odd[:, at]]
        return jnp.concatenate(pieces, axis=1).astype(BF16)

    heads = [whole_head(i) for i in range(4)]
    scale = 1.0 / math.sqrt(HD)
    count = out.shape[1] // HD
    for head in range(count):
        key, value = heads[head // (count // 2)], heads[2 + head // (count // 2)]
        at = slice(head * HD, (head + 1) * HD)
        scores = dot(query[:, at], key, NT) * scale
        scores = jnp.where(allowed, scores, -1e30)
        weights = jnp.exp(scores - jnp.max(scores, axis=1, keepdims=True))
        attention = (weights / jnp.sum(weights, axis=1, keepdims=True)).astype(BF16)
        out[:, at] = dot(attention, value).astype(BF16)


def attend(place, lens, dest, query, own_kv, other_kv, rows, slot):
    return pl.pallas_call(
        functools.partial(attend_kernel, rows, slot),
        in_specs=[in_smem()] * 3 + [in_vmem()] * 3,
        out_specs=in_vmem(),
        out_shape=jax.ShapeDtypeStruct(query.shape, BF16),
        compiler_params=pltpu.CompilerParams(vmem_limit_bytes=VMEM),
        name="attend",
    )(place, lens, dest, query, own_kv, other_kv)


def output_kernel(units, rows, slot, place, lens, dest, *refs):
    weights, contexts = refs[:4], refs[4 : 4 + 2 * units]
    out, context, weight, buf, order, c_sems, w_sems, out_sems = refs[4 + 2 * units :]
    unit, side, quarter, group = place[UNIT], place[SIDE], place[QUARTER], place[GROUP]
    part = weights[0].shape[2]
    own = 4 * part
    half = 2 * slot
    features = weight.shape[3]
    c_copies, w_copies = [], []
    for e, y in enumerate((side, 1 - side)):
        w_copies.append(
            start_copies(
                [
                    (weights[r].at[:, y], weight.at[e, :, aligned((quarter ^ r) * part, part)])
                    for r in range(4)
                ],
                w_sems,
                4 * e,
            )
        )
        pairs = []
        for k in range(units):
            source = unit ^ k
            lanes = aligned((source >> 2) * 4 * own, 4 * own)
            at = aligned((source & 3) * slot, slot)
            pairs.append((contexts[e * units + k], context.at[e, at, lanes]))
        c_copies.append(start_copies(pairs, c_sems, e * units))
    column = lax.broadcasted_iota(jnp.int32, (1, half), 1)
    row = lax.broadcasted_iota(jnp.int32, (half, half), 0)
    for turn in range(2):
        full, short = row_facts(lens, dest, group ^ turn, group, rows, slot)
        index = column - full[1]
        done = jnp.int32(0)
        for k in range(3):
            inside = jnp.logical_and(column >= short[k][1], column < short[k][1] + short[k][2])
            index = jnp.where(inside, slot + done + column - short[k][1], index)
            done = done + short[k][2]
        order[turn] = jnp.where(row == index, 1.0, 0.0).astype(BF16)
    sums = [None, None]
    sent = []
    for e in range(2):
        for copy in w_copies[e] + c_copies[e]:
            copy.wait()
        for turn in range(2):
            term = dot(
                context[e, turn * half : (turn + 1) * half],
                weight[e].reshape(units * own, features),
            )
            sums[turn] = term if e == 0 else sums[turn] + term
            if e:
                buf[turn] = dot(sums[turn].astype(BF16), order[turn], TN).astype(BF16)
                columns = aligned((group ^ turn) * half, half)
                sent += start_copies([(buf.at[turn], out.at[:, columns])], out_sems, turn)
    for copy in sent:
        copy.wait()


def output(place, lens, dest, weights, contexts, rows, slot):
    units, _, part, features = weights[0].shape
    tokens = BLOCKS * slot
    return pl.pallas_call(
        functools.partial(output_kernel, units, rows, slot),
        in_specs=[in_smem()] * 3 + [anywhere()] * (4 + len(contexts)),
        out_specs=anywhere(),
        out_shape=jax.ShapeDtypeStruct((features, tokens), BF16),
        scratch_shapes=[
            pltpu.VMEM((2, tokens, units * 4 * part), BF16),
            pltpu.VMEM((2, units, 4 * part, features), BF16),
            pltpu.VMEM((2, features, tokens // 2), BF16),
            pltpu.VMEM((2, tokens // 2, tokens // 2), BF16),
            pltpu.SemaphoreType.DMA((len(contexts),)),
            pltpu.SemaphoreType.DMA((8,)),
            pltpu.SemaphoreType.DMA((2,)),
        ],
        compiler_params=pltpu.CompilerParams(vmem_limit_bytes=VMEM),
        name="output",
    )(place, lens, dest, *weights, *contexts)


def swap(value, axis, mask=1):
    size = lax.axis_size(axis)
    return lax.ppermute(value, axis, [(i, i ^ mask) for i in range(size)])


def over_units(values):
    return [values[0]] + [swap(values[k], "tensor", 2 * k) for k in range(1, len(values))]


def all_quarters(value):
    across = swap(value, "parts")
    return [value, swap(value, "dp"), across, swap(across, "dp")]


def body(
    home,
    gain,
    q_values,
    q_scales,
    k_values,
    k_scales,
    v_values,
    v_scales,
    o_values,
    o_scales,
    row_lengths,
    row_dest,
):
    ranks = lax.axis_size("tensor")
    units = ranks // 2
    rank = lax.axis_index("tensor")
    unit, side = rank >> 1, rank & 1
    group = lax.axis_index("dp")
    quarter = (lax.axis_index("parts") & 1) * 2 + group
    features = home.shape[0]
    rows = row_lengths.shape[0] // 2
    slot = home.shape[1] // rows
    kv_head = rank * k_values.shape[0] // HD
    place = jnp.stack([jnp.asarray(v, jnp.int32) for v in (group, unit, side, quarter, kv_head)])

    pieces, o_pieces = weight_pieces(
        place,
        q_values,
        q_scales,
        k_values,
        k_scales,
        v_values,
        v_scales,
        o_values,
        o_scales,
        ranks,
    )
    keep, send, pos = deal(place, row_lengths, row_dest, home, rows, slot, pieces[:1])
    own_gain = lax.dynamic_slice_in_dim(
        gain.astype(F32), unit * 2 * features, 2 * features
    ).reshape(1, -1)
    frequency = rope_base ** (-2.0 * jnp.arange(HD // 2, dtype=F32) / HD)
    phases = pos[:, :1] * frequency[None, :]
    cosine, sine = jnp.cos(phases), jnp.sin(phases)
    part = HD // 4
    own_cos = lax.dynamic_slice_in_dim(cosine, side * part, part, 1)
    own_sin = lax.dynamic_slice_in_dim(sine, side * part, part, 1)
    own_cos = jnp.concatenate([own_cos] * 4, axis=1)
    own_sin = jnp.concatenate([-own_sin, own_sin] * 2, axis=1)
    wide_cos = jnp.concatenate([cosine, cosine], axis=1)
    wide_sin = jnp.concatenate([-sine, sine], axis=1)

    got = swap(send, "dp")
    keep2 = swap(keep, "tensor")
    got2 = lax.ppermute(
        send, ("dp", "tensor"), [(i, i ^ (ranks + 1)) for i in range(2 * ranks)]
    )
    own_piece, *pieces = over_units(pieces)
    own_pieces = [own_piece, swap(own_piece, "dp"), swap(own_piece, "parts")]
    collected, squares = collect(
        [keep, got, keep2, got2],
        pieces,
        [own_gain, own_cos, own_sin, wide_cos, wide_sin, *own_pieces[1:]],
    )

    squares = over_units([squares] * units)
    own_pieces.append(swap(own_pieces[2], "dp"))
    weights = [collected, swap(collected, "dp"), swap(collected, "parts")]
    (o_pieces,) = gate([o_pieces], squares[1:])
    o_moved = lax.all_to_all(o_pieces, "tensor", split_axis=0, concat_axis=0, tiled=True)
    (weights[2],) = gate(weights[2:], [weights[1], own_pieces[3]])

    weights.append(swap(weights[2], "dp"))
    normed = normalize(place, squares, own_gain, keep, got, keep2, got2)
    parts = over_units(project(place, normed, own_pieces, weights, units))
    (o_moved,) = gate([o_moved], parts[:1])
    own_kv = key_value(parts, own_cos, own_sin)
    other_kv = swap(own_kv, "tensor")
    query = queries(parts, wide_cos, wide_sin)
    o_weights = [
        value.reshape(units, 2, *value.shape[1:]) for value in all_quarters(o_moved)
    ]
    context = attend(place, row_lengths, row_dest, query, own_kv, other_kv, rows, slot)
    mine = [context]
    for k in range(1, units):
        mine.append(swap(mine[k & (k - 1)], "tensor", 2 * (k & -k)))
    theirs = [swap(value, "tensor") for value in mine]
    return output(place, row_lengths, row_dest, o_weights, mine + theirs, rows, slot)


def solution(mesh):
    in_specs = (
        P("tensor", ("parts", "dp")),
        P(),
        P(None, "tensor"),
        P(None, "tensor"),
        P("tensor", None),
        P(),
        P("tensor", None),
        P(),
        P("tensor", None),
        P("tensor", None),
        P("parts"),
        P("parts"),
    )
    out_specs = P("tensor", ("parts", "dp"))
    return jax.shard_map(body, mesh=mesh, in_specs=in_specs, out_specs=out_specs, check_vma=False)
```

time: 530 us -> 215 us (0.41)
  waiting for transfers between devices: 389 us -> 109 us
  matrix products: 48.1 us -> 0 us
  Pallas kernels: 0 us -> 46.8 us
  starting transfers between devices: 4.85 us -> 41.7 us
  local copies, waits for them, and re-layouts: 35.8 us -> 11.1 us
  blocking collectives: 23.1 us -> 0 us
  between operations: 13.7 us -> 0.48 us
  other arithmetic: 14.7 us -> 5.05 us
    reduce_scatter x1 -> x0, waiting for transfers between devices: 207 us -> none  [body(): lax.psum_scatter(lax.dot_general(o_weight, context, (((0,), (1,)), ((), (...]
    all_gather x1 -> x0, waiting for transfers between devices: 170 us -> none  [body(): shard_piece = lax.all_gather(normed, 'tensor', axis=0, tiled=True)]
    ppermute x2 -> x29, waiting for transfers between devices: 9.2 us -> 109 us  [the longest x28 109 us: swap(): return lax.ppermute(value, axis, [(i, i ^ mask) for i in range(size)])]
    pallas_call x0 -> x12, Pallas kernels: none -> 46.8 us  [the longest x1 10.5 us: project(): pl.pallas_call(functools.partial(project_kernel, units), in_specs=[in_sme...]
    dot_general x4 -> x0, matrix products: 43 us -> none  [the longest x1 20.1 us: body(): lax.dot_general(o_weight, context, (((0,), (1,)), ((), ())), preferred_el...]
    ppermute x2 -> x29, starting transfers between devices: 0.69 us -> 37.9 us  [the longest x28 37.3 us: swap(): return lax.ppermute(value, axis, [(i, i ^ mask) for i in range(size)])]
    broadcast_in_dim x7 -> x0, local copies, waits for them, and re-layouts: 24.9 us -> none  [the longest x4 24.5 us: dequantize(): jnp.repeat(jnp.repeat(scales, row_repeat, axis=0), column_repeat, axis=1)]
    psum x1 -> x0, blocking collectives: 23.1 us -> none  [body(): square_sum = lax.psum(jnp.sum(wide_rows * wide_rows, axis=0), 'tensor')]
  transfers between devices with their start and end apart: 5 -> 30, of which waited for: 4 -> 16; matrix products, arithmetic and copies ran while one was open for 7% -> 3% of each run, Pallas kernels for 0% -> 14%
where the time goes in v2:
time: 215 us; the launch traced here: 214 us
  waiting for transfers between devices  109 us (51%)
  Pallas kernels  46.8 us (22%)
  starting transfers between devices  41.7 us (19%)
  local copies, waits for them, and re-layouts  11.1 us (5%)
  other arithmetic  5.05 us (2%)
    ppermute x28, waiting for transfers between devices, swap(): return lax.ppermute(value, axis, [(i, i ^ mask) for i in range(size)])  109 us
    ppermute x28, starting transfers between devices, swap(): return lax.ppermute(value, axis, [(i, i ^ mask) for i in range(size)])  37.3 us
    pallas_call x1, Pallas kernels, project(): pl.pallas_call(functools.partial(project_kernel, units), in_specs=[in_sme...  10.5 us
    unnamed x62, local copies, waits for them, and re-layouts  9.33 us
    pallas_call x1, Pallas kernels, output(): pl.pallas_call(functools.partial(output_kernel, units, rows, slot), in_sp...  9.23 us
    pallas_call x1, Pallas kernels, deal(): pl.pallas_call(functools.partial(deal_kernel, rows, slot, len(after)), gr...  6.12 us
  transfers between devices with their start and end apart: 30, of which 16 were waited for; matrix products, arithmetic and copies ran while one was open for 3% of the time, Pallas kernels for 14%

profile of v2, /device:TPU:0, one launch (start us, length us, event | category | flops | bytes accessed | tf_op | source)
XLA Modules:
  0.0 214.4 jit_solution(8733093797933705006)
XLA Ops:
  0.7 3.8 %weight_pieces.1 = (bf16[640,256]{1,0:T(8,128)(2,1)}, bf16[640,256]{1,0:T(8,128)(2,1)}, bf16[640,256]{1,0:T(8,128)(2,1)}, bf16[640,256]{1,0:T(8,128)(2,1)}, bf16[8,64,1024]{2,1,0:T(8,128)(2,1)}) custom-call(s32[5]{0:T(128)} %stack.23.place, f32[2,64]{1,0:T(2,128)} %bitcast.16, f32[2,64]{1,0:T(2,128)} %ks.1, f32[2,64]{1,0:T(2,128)} %vs.1, f32[2,64]{1,0:T(2,128)} %os.1, ...), custom_call_target="tpu_custom_call" | custom-call | tf_op jit(solution)/shard_map/weight_pieces/pallas_call | solution.py:148
  4.5 3.1 %collective-permute-start.3 = (bf16[640,256]{1,0:T(8,128)(2,1)}, bf16[640,256]{1,0:T(8,128)(2,1)S(1)}, u32[]{:S(2)}, u32[]{:S(2)}) collective-permute-start(bf16[640,256]{1,0:T(8,128)(2,1)} %get-tuple-element.23), channel_id=1, source_target_pairs={{0,2},{1,3},{2,0},{3,1},{4,6},{5,7},{6,4},{7,5},{8,10},{9,11},{10,... | collective-permute-start | bytes 983048 | tf_op jit(solution)/shard_map/ppermute | solution.py:638
  7.6 6.1 %deal.1 = (bf16[384,1024]{1,0:T(8,128)(2,1)}, bf16[384,1024]{1,0:T(8,128)(2,1)}, f32[192,128]{1,0:T(8,128)}) custom-call(s32[5]{0:T(128)} %stack.23.place, s32[16]{0:T(128)} %lens.5, s32[16]{0:T(128)} %dest.5, bf16[1024,1536]{1,0:T(8,128)(2,1)} %home.1, bf16[640,256]{1,0:T(8,128)(2,1)} %get-tuple-element.20.rest_0_), custom_call_target="tpu_custom_call" | custom-call | tf_op jit(solution)/shard_map/deal/pallas_call | solution.py:212
  15.3 2.6 %collective-permute-start.4 = (bf16[640,256]{1,0:T(8,128)(2,1)}, bf16[640,256]{1,0:T(8,128)(2,1)S(1)}, u32[]{:S(2)}, u32[]{:S(2)}) collective-permute-start(bf16[640,256]{1,0:T(8,128)(2,1)} %get-tuple-element.24), channel_id=1, source_target_pairs={{0,4},{1,5},{2,6},{3,7},{4,0},{5,1},{6,2},{7,3},{8,12},{9,13},{10,... | collective-permute-start | bytes 983048 | tf_op jit(solution)/shard_map/ppermute | solution.py:638
  21.5 18.6 %collective-permute-done.4.refs_5_ = bf16[640,256]{1,0:T(8,128)(2,1)S(1)} collective-permute-done((bf16[640,256]{1,0:T(8,128)(2,1)}, bf16[640,256]{1,0:T(8,128)(2,1)S(1)}, u32[]{:S(2)}, u32[]{:S(2)}) %collective-permute-start.4) | collective-permute-done | bytes 327712 | tf_op jit(solution)/shard_map/ppermute | solution.py:638
  45.5 4.2 %collective-permute-done.7.refs_13_.rest_2_ = bf16[640,256]{1,0:T(8,128)(2,1)S(1)} collective-permute-done((bf16[640,256]{1,0:T(8,128)(2,1)S(1)}, bf16[640,256]{1,0:T(8,128)(2,1)S(1)}, u32[]{:S(2)}, u32[]{:S(2)}) %collective-permute-start.7) | collective-permute-done | bytes 327712 | tf_op jit(solution)/shard_map/ppermute | solution.py:638
  51.5 3.6 %collect.1 = (bf16[3,640,256]{2,1,0:T(8,128)(2,1)}, f32[8,768]{1,0:T(8,128)}) custom-call(bf16[384,1024]{1,0:T(8,128)(2,1)} %get-tuple-element.21.refs_0_.rest_5_, bf16[384,1024]{1,0:T(8,128)(2,1)} %copy-done.5, bf16[384,1024]{1,0:T(8,128)(2,1)} %copy-done.6, bf16[384,1024]{1,0:T(8,128)(2,1)} %copy-done.4, bf16[640,256]{1,0:T(8,128)(2,1)} %copy-done.25, ...), custom_call_target="tpu_custom_call" | custom-call | tf_op jit(solution)/shard_map/collect/pallas_call | solution.py:268
  56.6 2.5 %collective-permute-start.10 = (f32[8,768]{1,0:T(8,128)}, f32[8,768]{1,0:T(8,128)S(1)}, u32[]{:S(2)}, u32[]{:S(2)}) collective-permute-start(f32[8,768]{1,0:T(8,128)} %get-tuple-element.27.rest_0_), channel_id=1, source_target_pairs={{0,6},{1,7},{2,4},{3,5},{4,2},{5,3},{6,0},{7,1},{8,14},{9,15},{10,... | collective-permute-start | bytes 73736 | tf_op jit(solution)/shard_map/ppermute | solution.py:638
  64.9 3.7 %all-to-all-start = ((bf16[8,64,1024]{2,1,0:T(8,128)(2,1)}), bf16[8,64,1024]{2,1,0:T(8,128)(2,1)S(1)}, u32[]{:S(2)}, u32[]{:S(2)}) async-start(bf16[8,64,1024]{2,1,0:T(8,128)(2,1)} %gate.3), calls=%async_computation | async-start | bytes 2097152 | tf_op jit(solution)/shard_map/all_to_all | solution.py:720
  70.4 8.7 %collective-permute-done.13.refs_0_ = bf16[3,640,256]{2,1,0:T(8,128)(2,1)S(1)} collective-permute-done((bf16[3,640,256]{2,1,0:T(8,128)(2,1)}, bf16[3,640,256]{2,1,0:T(8,128)(2,1)S(1)}, u32[]{:S(2)}, u32[]{:S(2)}) %collective-permute-start.13) | collective-permute-done | bytes 983072 | tf_op jit(solution)/shard_map/ppermute | solution.py:638
  81.0 3.9 %normalize.1.normed = bf16[768,2048]{1,0:T(8,128)(2,1)} custom-call(s32[5]{0:T(128)} %stack.23.place, f32[8,768]{1,0:T(8,128)} %get-tuple-element.27.rest_0_, f32[8,768]{1,0:T(8,128)} %copy-done.29, f32[8,768]{1,0:T(8,128)} %copy-done.28, f32[8,768]{1,0:T(8,128)} %copy-done.27, f32[1,2048]{1,0:T(1,128)} %bitcast.15, ...), custom_call_target="tpu_custom_call" | custom-call | tf_op jit(solution)/shard_map/normalize/pallas_call | solution.py:332
  85.9 10.5 %project.1 = (bf16[192,1280]{1,0:T(8,128)(2,1)}, bf16[192,1280]{1,0:T(8,128)(2,1)}, bf16[192,1280]{1,0:T(8,128)(2,1)}, bf16[192,1280]{1,0:T(8,128)(2,1)}) custom-call(s32[5]{0:T(128)} %stack.23.place, bf16[768,2048]{1,0:T(8,128)(2,1)} %normalize.1.normed, bf16[640,256]{1,0:T(8,128)(2,1)} %get-tuple-element.20.rest_0_, bf16[640,256]{1,0:T(8,128)(2,1)} %copy-done.12, ...), custom_call_target="tpu_custom_call" | custom-call | tf_op jit(solution)/shard_map/project/pallas_call | solution.py:420
  103.7 19.3 %collective-permute-done.18.refs_1_ = bf16[192,1280]{1,0:T(8,128)(2,1)S(1)} collective-permute-done((bf16[192,1280]{1,0:T(8,128)(2,1)}, bf16[192,1280]{1,0:T(8,128)(2,1)S(1)}, u32[]{:S(2)}, u32[]{:S(2)}) %collective-permute-start.18) | collective-permute-done | bytes 491552 | tf_op jit(solution)/shard_map/ppermute | solution.py:638
  123.0 14.5 %collective-permute-done.19.refs_2_ = bf16[192,1280]{1,0:T(8,128)(2,1)S(1)} collective-permute-done((bf16[192,1280]{1,0:T(8,128)(2,1)}, bf16[192,1280]{1,0:T(8,128)(2,1)S(1)}, u32[]{:S(2)}, u32[]{:S(2)}) %collective-permute-start.19) | collective-permute-done | bytes 491552 | tf_op jit(solution)/shard_map/ppermute | solution.py:638
  139.0 2.8 %key_value.1.own_kv = bf16[192,256]{1,0:T(8,128)(2,1)} custom-call(f32[192,128]{1,0:T(8,128)} %get-tuple-element.40.refs_8_.cosine, f32[192,128]{1,0:T(8,128)} %get-tuple-element.41.refs_9_.sine, bf16[192,1280]{1,0:T(8,128)(2,1)} %get-tuple-element.29.refs_1_.refs_0_, bf16[192,1280]{1,0:T(8,128)(2,1)} %copy-done.7, bf16[192,1280]{1,0:T(8,128)(2,1)} %copy-done.8, ...), custom_call_target="tpu_custom_call" | custom-call | tf_op jit(solution)/shard_map/key_value/pallas_call | solution.py:460
  142.3 3.6 %queries.1.query = bf16[192,1024]{1,0:T(8,128)(2,1)} custom-call(f32[192,128]{1,0:T(8,128)} %get-tuple-element.38.refs_10_.cosine, f32[192,128]{1,0:T(8,128)} %get-tuple-element.39.refs_11_.sine, bf16[192,1280]{1,0:T(8,128)(2,1)} %get-tuple-element.29.refs_1_.refs_0_, bf16[192,1280]{1,0:T(8,128)(2,1)} %copy-done.7, bf16[192,1280]{1,0:T(8,128)(2,1)} %copy-done.8, ...), custom_call_target="tpu_custom_call" | custom-call | tf_op jit(solution)/shard_map/queries/pallas_call | solution.py:492
  147.3 3.3 %attend.1.refs_4_ = bf16[192,1024]{1,0:T(8,128)(2,1)} custom-call(s32[5]{0:T(128)} %stack.23.place, s32[16]{0:T(128)} %lens.5, s32[16]{0:T(128)} %dest.5, bf16[192,1024]{1,0:T(8,128)(2,1)} %queries.1.query, bf16[192,256]{1,0:T(8,128)(2,1)} %key_value.1.own_kv, bf16[192,256]{1,0:T(8,128)(2,1)} %copy-done.30), custom_call_target="tpu_custom_call" | custom-call | tf_op jit(solution)/shard_map/attend/pallas_call | solution.py:547
  150.6 10.4 %collective-permute-start.23 = (bf16[192,1024]{1,0:T(8,128)(2,1)}, bf16[192,1024]{1,0:T(8,128)(2,1)S(1)}, u32[]{:S(2)}, u32[]{:S(2)}) collective-permute-start(bf16[192,1024]{1,0:T(8,128)(2,1)} %attend.1.refs_4_), channel_id=1, source_target_pairs={{0,4},{1,5},{2,6},{3,7},{4,0},{5,1},{6,2},{7,3},{8,12},{9,13},{10,... | collective-permute-start | bytes 1179656 | tf_op jit(solution)/shard_map/ppermute | solution.py:638
  162.3 14.8 %collective-permute-done.23.refs_6_ = bf16[192,1024]{1,0:T(8,128)(2,1)S(1)} collective-permute-done((bf16[192,1024]{1,0:T(8,128)(2,1)}, bf16[192,1024]{1,0:T(8,128)(2,1)S(1)}, u32[]{:S(2)}, u32[]{:S(2)}) %collective-permute-start.23) | collective-permute-done | bytes 393248 | tf_op jit(solution)/shard_map/ppermute | solution.py:638
  178.8 3.1 %collective-permute-done.22.refs_5_ = bf16[192,1024]{1,0:T(8,128)(2,1)S(1)} collective-permute-done((bf16[192,1024]{1,0:T(8,128)(2,1)}, bf16[192,1024]{1,0:T(8,128)(2,1)S(1)}, u32[]{:S(2)}, u32[]{:S(2)}) %collective-permute-start.22) | collective-permute-done | bytes 393248 | tf_op jit(solution)/shard_map/ppermute | solution.py:638
  183.1 6.0 %collective-permute-done.24.refs_7_ = bf16[192,1024]{1,0:T(8,128)(2,1)S(1)} collective-permute-done((bf16[192,1024]{1,0:T(8,128)(2,1)S(1)}, bf16[192,1024]{1,0:T(8,128)(2,1)S(1)}, u32[]{:S(2)}, u32[]{:S(2)}) %collective-permute-start.24) | collective-permute-done | bytes 393248 | tf_op jit(solution)/shard_map/ppermute | solution.py:638
  190.3 7.4 %collective-permute-done.26.refs_9_ = bf16[192,1024]{1,0:T(8,128)(2,1)S(1)} collective-permute-done((bf16[192,1024]{1,0:T(8,128)(2,1)S(1)}, bf16[192,1024]{1,0:T(8,128)(2,1)S(1)}, u32[]{:S(2)}, u32[]{:S(2)}) %collective-permute-start.26) | collective-permute-done | bytes 393248 | tf_op jit(solution)/shard_map/ppermute | solution.py:638
  197.7 6.3 %collective-permute-done.28.refs_11_ = bf16[192,1024]{1,0:T(8,128)(2,1)S(1)} collective-permute-done((bf16[192,1024]{1,0:T(8,128)(2,1)S(1)}, bf16[192,1024]{1,0:T(8,128)(2,1)S(1)}, u32[]{:S(2)}, u32[]{:S(2)}) %collective-permute-start.28) | collective-permute-done | bytes 393248 | tf_op jit(solution)/shard_map/ppermute | solution.py:638
  205.0 9.2 %output.1 = bf16[1024,768]{1,0:T(8,128)(2,1)} custom-call(s32[5]{0:T(128)} %stack.23.place, s32[16]{0:T(128)} %lens.5, s32[16]{0:T(128)} %dest.5, bf16[4,2,64,1024]{3,2,1,0:T(8,128)(2,1)} %bitcast.11, bf16[4,2,64,1024]{3,2,1,0:T(8,128)(2,1)} %bitcast.12, bf16[4,2,64,1024]{3,2,1,0:T(8,128)(2,1)} %bitcast.9.refs_2_, bf16[4,2,64,1024]{3,2,1,0:T(8,128)(2,1)} %bitcast.13, ...), custom_call_target="tpu_custom_call" | custom-call | tf_op jit(solution)/shard_map/output/pallas_call | solution.py:617
  (119 shorter events, 42.2 us)
Async XLA Ops:
  4.5 14.7 %collective-permute-start.3 = (bf16[640,256]{1,0:T(8,128)(2,1)}, bf16[640,256]{1,0:T(8,128)(2,1)S(1)}, u32[]{:S(2)}, u32[]{:S(2)}) collective-permute-start(bf16[640,256]{1,0:T(8,128)(2,1)} %get-tuple-element.23), channel_id=1, source_target_pairs={{0,2},{1,3},{2,0},{3,1},{4,6},{5,7},{6,4},{7,5},{8,10},{9,11},{10,... | collective-permute-start | bytes 983048 | tf_op jit(solution)/shard_map/ppermute | solution.py:638
  13.7 35.9 %collective-permute-start.2 = (bf16[384,1024]{1,0:T(8,128)(2,1)}, bf16[384,1024]{1,0:T(8,128)(2,1)S(1)}, u32[]{:S(2)}, u32[]{:S(2)}) collective-permute-start(bf16[384,1024]{1,0:T(8,128)(2,1)} %get-tuple-element.22), channel_id=1, source_target_pairs={{0,9},{1,8},{2,11},{3,10},{4,13},{5,12},{6,15},{7,14},{8,1},{9,0},... | collective-permute-start | bytes 2359304 | tf_op jit(solution)/shard_map/ppermute | solution.py:705
  14.4 35.3 %collective-permute-start = (bf16[384,1024]{1,0:T(8,128)(2,1)}, bf16[384,1024]{1,0:T(8,128)(2,1)S(1)}, u32[]{:S(2)}, u32[]{:S(2)}) collective-permute-start(bf16[384,1024]{1,0:T(8,128)(2,1)} %get-tuple-element.22), channel_id=1, source_target_pairs={{0,8},{8,0},{1,9},{9,1},{2,10},{10,2},{3,11},{11,3},{4,12},{12,4},... | collective-permute-start | bytes 2359304 | tf_op jit(solution)/shard_map/ppermute | solution.py:638
  15.3 24.7 %collective-permute-start.4 = (bf16[640,256]{1,0:T(8,128)(2,1)}, bf16[640,256]{1,0:T(8,128)(2,1)S(1)}, u32[]{:S(2)}, u32[]{:S(2)}) collective-permute-start(bf16[640,256]{1,0:T(8,128)(2,1)} %get-tuple-element.24), channel_id=1, source_target_pairs={{0,4},{1,5},{2,6},{3,7},{4,0},{5,1},{6,2},{7,3},{8,12},{9,13},{10,... | collective-permute-start | bytes 983048 | tf_op jit(solution)/shard_map/ppermute | solution.py:638
  17.9 23.7 %collective-permute-start.5 = (bf16[640,256]{1,0:T(8,128)(2,1)}, bf16[640,256]{1,0:T(8,128)(2,1)}, u32[]{:S(2)}, u32[]{:S(2)}) collective-permute-start(bf16[640,256]{1,0:T(8,128)(2,1)} %get-tuple-element.25), channel_id=1, source_target_pairs={{0,6},{1,7},{2,4},{3,5},{4,2},{5,3},{6,0},{7,1},{8,14},{9,15},{10,... | collective-permute-start | bytes 983048 | tf_op jit(solution)/shard_map/ppermute | solution.py:638
  19.9 30.7 %collective-permute-start.1 = (bf16[384,1024]{1,0:T(8,128)(2,1)}, bf16[384,1024]{1,0:T(8,128)(2,1)S(1)}, u32[]{:S(2)}, u32[]{:S(2)}) collective-permute-start(bf16[384,1024]{1,0:T(8,128)(2,1)} %get-tuple-element.21.refs_0_.rest_5_), channel_id=1, source_target_pairs={{0,1},{1,0},{2,3},{3,2},{4,5},{5,4},{6,7},{7,6},{8,9},{9,8},{10,11... | collective-permute-start | bytes 2359304 | tf_op jit(solution)/shard_map/ppermute | solution.py:638
  40.1 9.6 %collective-permute-start.7 = (bf16[640,256]{1,0:T(8,128)(2,1)S(1)}, bf16[640,256]{1,0:T(8,128)(2,1)S(1)}, u32[]{:S(2)}, u32[]{:S(2)}) collective-permute-start(bf16[640,256]{1,0:T(8,128)(2,1)S(1)} %copy-done.14), channel_id=1, source_target_pairs={{0,16},{16,0},{1,17},{17,1},{2,18},{18,2},{3,19},{19,3},{4,20},{20... | collective-permute-start | bytes 983048 | tf_op jit(solution)/shard_map/ppermute | solution.py:638
  41.6 8.0 %collective-permute-start.6 = (bf16[640,256]{1,0:T(8,128)(2,1)S(1)}, bf16[640,256]{1,0:T(8,128)(2,1)S(1)}, u32[]{:S(2)}, u32[]{:S(2)}) collective-permute-start(bf16[640,256]{1,0:T(8,128)(2,1)S(1)} %copy-done.14), channel_id=1, source_target_pairs={{0,8},{8,0},{1,9},{9,1},{2,10},{10,2},{3,11},{11,3},{4,12},{12,4},... | collective-permute-start | bytes 983048 | tf_op jit(solution)/shard_map/ppermute | solution.py:638
  55.1 24.0 %collective-permute-start.13 = (bf16[3,640,256]{2,1,0:T(8,128)(2,1)}, bf16[3,640,256]{2,1,0:T(8,128)(2,1)S(1)}, u32[]{:S(2)}, u32[]{:S(2)}) collective-permute-start(bf16[3,640,256]{2,1,0:T(8,128)(2,1)} %get-tuple-element.28.rest_4_), channel_id=1, source_target_pairs={{0,16},{16,0},{1,17},{17,1},{2,18},{18,2},{3,19},{19,3},{4,20},{20... | collective-permute-start | bytes 2949128 | tf_op jit(solution)/shard_map/ppermute | solution.py:638
  56.6 22.4 %collective-permute-start.12 = (bf16[3,640,256]{2,1,0:T(8,128)(2,1)}, bf16[3,640,256]{2,1,0:T(8,128)(2,1)S(1)}, u32[]{:S(2)}, u32[]{:S(2)}) collective-permute-start(bf16[3,640,256]{2,1,0:T(8,128)(2,1)} %get-tuple-element.28.rest_4_), channel_id=1, source_target_pairs={{0,8},{8,0},{1,9},{9,1},{2,10},{10,2},{3,11},{11,3},{4,12},{12,4},... | collective-permute-start | bytes 2949128 | tf_op jit(solution)/shard_map/ppermute | solution.py:638
  64.9 31.5 %all-to-all-start = ((bf16[8,64,1024]{2,1,0:T(8,128)(2,1)}), bf16[8,64,1024]{2,1,0:T(8,128)(2,1)S(1)}, u32[]{:S(2)}, u32[]{:S(2)}) async-start(bf16[8,64,1024]{2,1,0:T(8,128)(2,1)} %gate.3), calls=%async_computation | async-start | bytes 2097152 | tf_op jit(solution)/shard_map/all_to_all | solution.py:720
  97.4 63.6 %collective-permute-start.16 = (bf16[8,64,1024]{2,1,0:T(8,128)(2,1)}, bf16[8,64,1024]{2,1,0:T(8,128)(2,1)}, u32[]{:S(2)}, u32[]{:S(2)}) collective-permute-start(bf16[8,64,1024]{2,1,0:T(8,128)(2,1)} %gate.5), channel_id=1, source_target_pairs={{0,16},{16,0},{1,17},{17,1},{2,18},{18,2},{3,19},{19,3},{4,20},{20... | collective-permute-start | bytes 3145736 | tf_op jit(solution)/shard_map/ppermute | solution.py:638
  98.9 24.1 %collective-permute-start.18 = (bf16[192,1280]{1,0:T(8,128)(2,1)}, bf16[192,1280]{1,0:T(8,128)(2,1)S(1)}, u32[]{:S(2)}, u32[]{:S(2)}) collective-permute-start(bf16[192,1280]{1,0:T(8,128)(2,1)} %get-tuple-element.30), channel_id=1, source_target_pairs={{0,2},{1,3},{2,0},{3,1},{4,6},{5,7},{6,4},{7,5},{8,10},{9,11},{10,... | collective-permute-start | bytes 1474568 | tf_op jit(solution)/shard_map/ppermute | solution.py:638
  101.2 36.3 %collective-permute-start.19 = (bf16[192,1280]{1,0:T(8,128)(2,1)}, bf16[192,1280]{1,0:T(8,128)(2,1)S(1)}, u32[]{:S(2)}, u32[]{:S(2)}) collective-permute-start(bf16[192,1280]{1,0:T(8,128)(2,1)} %get-tuple-element.31), channel_id=1, source_target_pairs={{0,4},{1,5},{2,6},{3,7},{4,0},{5,1},{6,2},{7,3},{8,12},{9,13},{10,... | collective-permute-start | bytes 1474568 | tf_op jit(solution)/shard_map/ppermute | solution.py:638
  102.2 35.2 %collective-permute-start.20 = (bf16[192,1280]{1,0:T(8,128)(2,1)}, bf16[192,1280]{1,0:T(8,128)(2,1)S(1)}, u32[]{:S(2)}, u32[]{:S(2)}) collective-permute-start(bf16[192,1280]{1,0:T(8,128)(2,1)} %get-tuple-element.32), channel_id=1, source_target_pairs={{0,6},{1,7},{2,4},{3,5},{4,2},{5,3},{6,0},{7,1},{8,14},{9,15},{10,... | collective-permute-start | bytes 1474568 | tf_op jit(solution)/shard_map/ppermute | solution.py:638
  150.6 26.5 %collective-permute-start.23 = (bf16[192,1024]{1,0:T(8,128)(2,1)}, bf16[192,1024]{1,0:T(8,128)(2,1)S(1)}, u32[]{:S(2)}, u32[]{:S(2)}) collective-permute-start(bf16[192,1024]{1,0:T(8,128)(2,1)} %attend.1.refs_4_), channel_id=1, source_target_pairs={{0,4},{1,5},{2,6},{3,7},{4,0},{5,1},{6,2},{7,3},{8,12},{9,13},{10,... | collective-permute-start | bytes 1179656 | tf_op jit(solution)/shard_map/ppermute | solution.py:638
  161.0 29.3 %collective-permute-start.15 = (bf16[8,64,1024]{2,1,0:T(8,128)(2,1)S(1)}, bf16[8,64,1024]{2,1,0:T(8,128)(2,1)S(1)}, u32[]{:S(2)}, u32[]{:S(2)}) collective-permute-start(bf16[8,64,1024]{2,1,0:T(8,128)(2,1)S(1)} %copy-done.1), channel_id=1, source_target_pairs={{0,8},{8,0},{1,9},{9,1},{2,10},{10,2},{3,11},{11,3},{4,12},{12,4},... | collective-permute-start | bytes 3145736 | tf_op jit(solution)/shard_map/ppermute | solution.py:638
  161.0 43.0 %collective-permute-start.17 = (bf16[8,64,1024]{2,1,0:T(8,128)(2,1)}, bf16[8,64,1024]{2,1,0:T(8,128)(2,1)S(1)}, u32[]{:S(2)}, u32[]{:S(2)}) collective-permute-start(bf16[8,64,1024]{2,1,0:T(8,128)(2,1)} %collective-permute-done.16), channel_id=1, source_target_pairs={{0,8},{8,0},{1,9},{9,1},{2,10},{10,2},{3,11},{11,3},{4,12},{12,4},... | collective-permute-start | bytes 3145736 | tf_op jit(solution)/shard_map/ppermute | solution.py:638
  161.5 15.6 %collective-permute-start.25 = (bf16[192,1024]{1,0:T(8,128)(2,1)}, bf16[192,1024]{1,0:T(8,128)(2,1)S(1)}, u32[]{:S(2)}, u32[]{:S(2)}) collective-permute-start(bf16[192,1024]{1,0:T(8,128)(2,1)} %attend.1.refs_4_), channel_id=1, source_target_pairs={{0,1},{1,0},{2,3},{3,2},{4,5},{5,4},{6,7},{7,6},{8,9},{9,8},{10,11... | collective-permute-start | bytes 1179656 | tf_op jit(solution)/shard_map/ppermute | solution.py:638
  162.3 19.5 %collective-permute-start.22 = (bf16[192,1024]{1,0:T(8,128)(2,1)}, bf16[192,1024]{1,0:T(8,128)(2,1)S(1)}, u32[]{:S(2)}, u32[]{:S(2)}) collective-permute-start(bf16[192,1024]{1,0:T(8,128)(2,1)} %attend.1.refs_4_), channel_id=1, source_target_pairs={{0,2},{1,3},{2,0},{3,1},{4,6},{5,7},{6,4},{7,5},{8,10},{9,11},{10,... | collective-permute-start | bytes 1179656 | tf_op jit(solution)/shard_map/ppermute | solution.py:638
  177.1 11.9 %collective-permute-start.24 = (bf16[192,1024]{1,0:T(8,128)(2,1)S(1)}, bf16[192,1024]{1,0:T(8,128)(2,1)S(1)}, u32[]{:S(2)}, u32[]{:S(2)}) collective-permute-start(bf16[192,1024]{1,0:T(8,128)(2,1)S(1)} %collective-permute-done.23.refs_6_), channel_id=1, source_target_pairs={{0,2},{1,3},{2,0},{3,1},{4,6},{5,7},{6,4},{7,5},{8,10},{9,11},{10,... | collective-permute-start | bytes 1179656 | tf_op jit(solution)/shard_map/ppermute | solution.py:638
  177.1 13.2 %collective-permute-start.27 = (bf16[192,1024]{1,0:T(8,128)(2,1)S(1)}, bf16[192,1024]{1,0:T(8,128)(2,1)S(1)}, u32[]{:S(2)}, u32[]{:S(2)}) collective-permute-start(bf16[192,1024]{1,0:T(8,128)(2,1)S(1)} %collective-permute-done.23.refs_6_), channel_id=1, source_target_pairs={{0,1},{1,0},{2,3},{3,2},{4,5},{5,4},{6,7},{7,6},{8,9},{9,8},{10,11... | collective-permute-start | bytes 1179656 | tf_op jit(solution)/shard_map/ppermute | solution.py:638
  181.8 15.9 %collective-permute-start.26 = (bf16[192,1024]{1,0:T(8,128)(2,1)S(1)}, bf16[192,1024]{1,0:T(8,128)(2,1)S(1)}, u32[]{:S(2)}, u32[]{:S(2)}) collective-permute-start(bf16[192,1024]{1,0:T(8,128)(2,1)S(1)} %collective-permute-done.22.refs_5_), channel_id=1, source_target_pairs={{0,1},{1,0},{2,3},{3,2},{4,5},{5,4},{6,7},{7,6},{8,9},{9,8},{10,11... | collective-permute-start | bytes 1179656 | tf_op jit(solution)/shard_map/ppermute | solution.py:638
  189.1 14.9 %collective-permute-start.28 = (bf16[192,1024]{1,0:T(8,128)(2,1)S(1)}, bf16[192,1024]{1,0:T(8,128)(2,1)S(1)}, u32[]{:S(2)}, u32[]{:S(2)}) collective-permute-start(bf16[192,1024]{1,0:T(8,128)(2,1)S(1)} %collective-permute-done.24.refs_7_), channel_id=1, source_target_pairs={{0,1},{1,0},{2,3},{3,2},{4,5},{5,4},{6,7},{7,6},{8,9},{9,8},{10,11... | collective-permute-start | bytes 1179656 | tf_op jit(solution)/shard_map/ppermute | solution.py:638
  (37 other events, 304.6 us)

commit v3 on v2

--- a/solution.py
+++ b/solution.py
@@ -20,7 +20,8 @@
 NN = (((1,), (0,)), ((), ()))
 NT = (((1,), (1,)), ((), ()))
 TN = (((0,), (0,)), ((), ()))
-VMEM = 58 << 20
+VMEM = 40 << 20
+ALL = 60 << 20
 
 
 def dot(a, b, dims=NN):
@@ -36,6 +37,10 @@
 
 
 def anywhere():
+    return pl.BlockSpec(memory_space=pl.ANY)
+
+
+def in_hbm():
     return pl.BlockSpec(memory_space=pltpu.HBM)
 
 
@@ -76,7 +81,8 @@
     return full, short
 
 
-def pieces_kernel(units, place, qs, ks, vs, os, q_hbm, k_hbm, v_hbm, o_hbm, *rest):
+def pieces_kernel(units, count, place, qs, ks, vs, os, q_hbm, k_hbm, v_hbm, o_hbm, *rest):
+    rest = rest[count:]
     outs, o_out = rest[:units], rest[units]
     q_buf, k_buf, v_buf, o_buf, pieces, o_pieces, in_sems, out_sems = rest[units + 1 :]
     unit, quarter, head = place[UNIT], place[QUARTER], place[KV_HEAD]
@@ -137,7 +143,17 @@
 
 
 def weight_pieces(
-    place, q_values, q_scales, k_values, k_scales, v_values, v_scales, o_values, o_scales, ranks
+    place,
+    q_values,
+    q_scales,
+    k_values,
+    k_scales,
+    v_values,
+    v_scales,
+    o_values,
+    o_scales,
+    ranks,
+    after,
 ):
     units = ranks // 2
     o_shape = (ranks, o_values.shape[0] // 4, o_values.shape[1] // ranks)
@@ -146,8 +162,8 @@
     size = q_values.shape[0] // units // 4
     rows = size + 2 * part * max(1, size // own)
     outs = pl.pallas_call(
-        functools.partial(pieces_kernel, units),
-        in_specs=[in_smem()] * 5 + [anywhere()] * 4,
+        functools.partial(pieces_kernel, units, len(after)),
+        in_specs=[in_smem()] * 5 + [in_hbm()] * 4 + [anywhere()] * len(after),
         out_specs=[anywhere()] * (units + 1),
         out_shape=[jax.ShapeDtypeStruct((rows, own), BF16)] * units
         + [jax.ShapeDtypeStruct(o_shape, BF16)],
@@ -161,14 +177,24 @@
             pltpu.SemaphoreType.DMA((3 * units + 1,)),
             pltpu.SemaphoreType.DMA((units + 1,)),
         ],
-        compiler_params=pltpu.CompilerParams(vmem_limit_bytes=VMEM),
+        compiler_params=pltpu.CompilerParams(vmem_limit_bytes=ALL),
         name="weight_pieces",
-    )(place, q_scales.T, k_scales, v_scales, o_scales, q_values, k_values, v_values, o_values)
+    )(
+        place,
+        q_scales.T,
+        k_scales,
+        v_scales,
+        o_scales,
+        q_values,
+        k_values,
+        v_values,
+        o_values,
+        *after,
+    )
     return outs[:units], outs[units]
 
 
-def deal_kernel(rows, slot, count, place, lens, dest, home, *rest):
-    keep, send, pos, pick = rest[count:]
+def deal_kernel(rows, slot, place, lens, dest, home, keep, send, pos, pick):
     step = pl.program_id(0)
     group, block = place[GROUP], place[UNIT] & (BLOCKS - 1)
 
@@ -205,20 +231,19 @@
     send[...] = taken[half:].astype(BF16)
 
 
-def deal(place, lens, dest, home, rows, slot, after):
+def deal(place, lens, dest, home, rows, slot):
     features = home.shape[0]
     width = min(features, 256)
     tokens = BLOCKS * slot
     return pl.pallas_call(
-        functools.partial(deal_kernel, rows, slot, len(after)),
+        functools.partial(deal_kernel, rows, slot),
         grid=(features // width,),
         in_specs=[
             in_smem(),
             in_smem(),
             in_smem(),
             pl.BlockSpec((width, home.shape[1]), lambda i: (i, 0)),
-        ]
-        + [anywhere()] * len(after),
+        ],
         out_specs=[
             pl.BlockSpec((tokens // 2, width), lambda i: (0, i)),
             pl.BlockSpec((tokens // 2, width), lambda i: (0, i)),
@@ -232,9 +257,9 @@
         scratch_shapes=[
             pltpu.VMEM((tokens, rows * slot), BF16),
         ],
-        compiler_params=pltpu.CompilerParams(vmem_limit_bytes=VMEM),
+        compiler_params=pltpu.CompilerParams(vmem_limit_bytes=ALL),
         name="deal",
-    )(place, lens, dest, home, *after)
+    )(place, lens, dest, home)
 
 
 def collect_kernel(count, extra, *refs):
@@ -346,8 +371,8 @@
 
 
 def project_kernel(units, place, normed, *rest):
-    own_pieces, weights, outs = rest[:4], rest[4:8], rest[8 : 8 + units]
-    weight, tokens, buf, x_sem, w_sems, out_sems = rest[8 + units :]
+    own_pieces, weights, outs = rest[:4], rest[4:8], rest[8:12]
+    weight, tokens, buf, x_sem, w_sems, out_sems = rest[12:]
     unit, quarter = place[UNIT], place[QUARTER]
     count, wide = tokens.shape
     slot = count // BLOCKS
@@ -370,25 +395,17 @@
     x_copy.wait()
     sent = []
 
-    def hand_out(group, cols, index):
+    def hand_out(group, cols, index, chunk, place_in_chunk):
         for k in range(4 * group, 4 * group + 4):
             rows = aligned(((unit ^ k) & 3) * slot, slot)
-            pair = (buf.at[group, rows, cols], outs[k].at[:, cols])
-            sent.extend(start_copies([pair], out_sems, 5 * k + index))
+            target = outs[2 * chunk + (k & 1)].at[k >> 1, :, place_in_chunk]
+            sent.extend(start_copies([(buf.at[group, rows, cols], target)], out_sems, 5 * k + index))
 
     for group in range(units // BLOCKS):
-        for k in range(4 * group, 4 * group + 4):
-            for r in range(4):
-                copies[k * 4 + r].wait()
-            s = (unit ^ k) & 3
-            value = None
-            for q in range(4):
-                term = dot(tokens[:, q * size : (q + 1) * size], weight[q, group * 4 + s, :size])
-                value = term if value is None else value + term
-            cols = aligned(s * own, own)
-            buf[group, :, cols] = value.astype(BF16)
-            hand_out(group, cols, k & 3)
         sources = slice(group * 4, group * 4 + 4)
+        if group == 0:
+            for copy in copies:
+                copy.wait()
         value = None
         for q in range(4):
             for e in range(size // width):
@@ -404,8 +421,17 @@
                 )
                 term = dot(tokens[:, at : at + width], w, NT)
                 value = term if value is None else value + term
-        buf[group, :, 4 * own :] = value.astype(BF16)
-        hand_out(group, pl.ds(4 * own, 4 * part), 4)
+        cols = slice(4 * own, 4 * own + 4 * part)
+        buf[group, :, cols] = value.astype(BF16)
+        hand_out(group, cols, 4, 0, slice(2 * own, 2 * own + 4 * part))
+        for s in range(4):
+            value = None
+            for q in range(4):
+                term = dot(tokens[:, q * size : (q + 1) * size], weight[q, group * 4 + s, :size])
+                value = term if value is None else value + term
+            cols = slice(s * own, (s + 1) * own)
+            buf[group, :, cols] = value.astype(BF16)
+            hand_out(group, cols, s, s >> 1, slice((s & 1) * own, ((s & 1) + 1) * own))
     for copy in sent:
         copy.wait()
 
@@ -420,8 +446,9 @@
     outs = pl.pallas_call(
         functools.partial(project_kernel, units),
         in_specs=[in_smem()] + [anywhere()] * 9,
-        out_specs=[anywhere()] * units,
-        out_shape=[jax.ShapeDtypeStruct((slot, 4 * own + 4 * part), BF16)] * units,
+        out_specs=[anywhere()] * 4,
+        out_shape=[jax.ShapeDtypeStruct((units // 2, slot, 2 * own + 4 * part), BF16)] * 2
+        + [jax.ShapeDtypeStruct((units // 2, slot, 2 * own), BF16)] * 2,
         scratch_shapes=[
             pltpu.VMEM((4, units, rows, own), BF16),
             pltpu.VMEM((tokens, wide), BF16),
@@ -430,22 +457,41 @@
             pltpu.SemaphoreType.DMA((4 * units,)),
             pltpu.SemaphoreType.DMA((5 * units,)),
         ],
-        compiler_params=pltpu.CompilerParams(vmem_limit_bytes=VMEM),
+        compiler_params=pltpu.CompilerParams(vmem_limit_bytes=ALL),
         name="project",
     )(place, normed, *own_pieces, *weights)
     return outs
 
 
-def key_value_kernel(units, cosine, sine, *refs):
-    parts, (out, buf, sems) = refs[:units], refs[units:]
-    wide = parts[0].shape[1] - buf.shape[2]
-    copies = start_copies([(ref.at[:, wide:], buf.at[k]) for k, ref in enumerate(parts)], sems)
-    value = None
-    for k, copy in enumerate(copies):
-        copy.wait()
-        term = buf[k].astype(F32)
-        value = term if value is None else value + term
-    value = value.astype(BF16).astype(F32)
+def pair_sum_kernel(kept, got, *outs):
+    for i, out in enumerate(outs):
+        out[...] = (kept[i + 1].astype(F32) + got[i + 1].astype(F32)).astype(BF16)
+
+
+def pair_sums(kept, got):
+    count = kept.shape[0] - 1
+    return pl.pallas_call(
+        pair_sum_kernel,
+        in_specs=[in_vmem()] * 2,
+        out_specs=[in_vmem()] * count,
+        out_shape=[jax.ShapeDtypeStruct(kept.shape[1:], BF16)] * count,
+        compiler_params=pltpu.CompilerParams(vmem_limit_bytes=VMEM),
+        name="pair_sums",
+    )(kept, got)
+
+
+def all_parts(refs, cols):
+    kept, got = refs[:2]
+    value = kept[0, :, cols].astype(F32) + got[0, :, cols].astype(F32)
+    for ref in refs[2:]:
+        value = value + ref[:, cols].astype(F32)
+    return value.astype(BF16).astype(F32)
+
+
+def key_value_kernel(cosine, sine, *refs):
+    parts, out = refs[:-1], refs[-1]
+    wide = parts[0].shape[2]
+    value = all_parts(parts, slice(wide - out.shape[1], wide))
     keys, values = value[:, :HD], value[:, HD:]
     part = HD // 4
     lane = lax.broadcasted_iota(jnp.int32, keys.shape, 1)
@@ -456,53 +502,37 @@
 
 
 def key_value(parts, cosine, sine):
-    shape = (parts[0].shape[0], parts[0].shape[1] // 5)
     return pl.pallas_call(
-        functools.partial(key_value_kernel, len(parts)),
-        in_specs=[in_vmem()] * 2 + [anywhere()] * len(parts),
+        key_value_kernel,
+        in_specs=[in_vmem()] * (2 + len(parts)),
         out_specs=in_vmem(),
-        out_shape=jax.ShapeDtypeStruct(shape, BF16),
-        scratch_shapes=[
-            pltpu.VMEM((len(parts), *shape), BF16),
-            pltpu.SemaphoreType.DMA((len(parts),)),
-        ],
+        out_shape=jax.ShapeDtypeStruct((parts[0].shape[1], parts[0].shape[2] // 3), BF16),
+        compiler_params=pltpu.CompilerParams(vmem_limit_bytes=VMEM),
         name="key_value",
     )(cosine, sine, *parts)
 
 
-def query_kernel(units, cosine, sine, *refs):
-    parts, (out, buf, sems) = refs[:units], refs[units:]
-    wide = out.shape[1]
-    copies = start_copies([(ref.at[:, :wide], buf.at[k]) for k, ref in enumerate(parts)], sems)
+def query_kernel(count, cosine, sine, *refs):
+    parts, out = refs[:count], refs[-1]
     cos, sin = cosine[...], sine[...]
-    for copy in copies:
-        copy.wait()
-    for head in range(wide // HD):
+    for head in range(out.shape[1] // HD):
         at = slice(head * HD, (head + 1) * HD)
-        query = buf[0, :, at].astype(F32)
-        for k in range(1, units):
-            query = query + buf[k, :, at].astype(F32)
-        query = query.astype(BF16).astype(F32)
-        swapped = jnp.concatenate([query[:, HD // 2 :], query[:, : HD // 2]], axis=1)
-        out[:, at] = (query * cos + swapped * sin).astype(BF16)
-
-
-def queries(parts, cosine, sine):
-    shape = (parts[0].shape[0], parts[0].shape[1] // 5 * 4)
+        query = all_parts(parts, at)
+        out[:, at] = (query * cos + pltpu.roll(query, HD // 2, 1) * sin).astype(BF16)
+
+
+def queries(parts, cosine, sine, wide, after):
     return pl.pallas_call(
         functools.partial(query_kernel, len(parts)),
-        in_specs=[in_vmem()] * 2 + [anywhere()] * len(parts),
+        in_specs=[in_vmem()] * (2 + len(parts)) + [anywhere()] * len(after),
         out_specs=in_vmem(),
-        out_shape=jax.ShapeDtypeStruct(shape, BF16),
-        scratch_shapes=[
-            pltpu.VMEM((len(parts), *shape), BF16),
-            pltpu.SemaphoreType.DMA((len(parts),)),
-        ],
+        out_shape=jax.ShapeDtypeStruct((parts[0].shape[1], wide), BF16),
+        compiler_params=pltpu.CompilerParams(vmem_limit_bytes=VMEM),
         name="queries",
-    )(cosine, sine, *parts)
-
-
-def attend_kernel(rows, slot, place, lens, dest, query, own_kv, other_kv, out):
+    )(cosine, sine, *parts, *after)
+
+
+def attend_kernel(kv_head, rows, slot, place, lens, dest, query, own_kv, other_kv, out):
     group, block, side = place[GROUP], place[UNIT] & (BLOCKS - 1), place[SIDE]
     _, short = row_facts(lens, dest, group ^ (block >> 1), group, rows, slot)
     many = (block & 1) == 1
@@ -530,11 +560,9 @@
             pieces += [even[:, at], odd[:, at]]
         return jnp.concatenate(pieces, axis=1).astype(BF16)
 
-    heads = [whole_head(i) for i in range(4)]
+    key, value = whole_head(kv_head), whole_head(2 + kv_head)
     scale = 1.0 / math.sqrt(HD)
-    count = out.shape[1] // HD
-    for head in range(count):
-        key, value = heads[head // (count // 2)], heads[2 + head // (count // 2)]
+    for head in range(out.shape[1] // HD):
         at = slice(head * HD, (head + 1) * HD)
         scores = dot(query[:, at], key, NT) * scale
         scores = jnp.where(allowed, scores, -1e30)
@@ -543,9 +571,9 @@
         out[:, at] = dot(attention, value).astype(BF16)
 
 
-def attend(place, lens, dest, query, own_kv, other_kv, rows, slot):
+def attend(place, lens, dest, query, own_kv, other_kv, kv_head, rows, slot):
     return pl.pallas_call(
-        functools.partial(attend_kernel, rows, slot),
+        functools.partial(attend_kernel, kv_head, rows, slot),
         in_specs=[in_smem()] * 3 + [in_vmem()] * 3,
         out_specs=in_vmem(),
         out_shape=jax.ShapeDtypeStruct(query.shape, BF16),
@@ -555,8 +583,8 @@
 
 
 def output_kernel(units, rows, slot, place, lens, dest, *refs):
-    weights, contexts = refs[:4], refs[4 : 4 + 2 * units]
-    out, context, weight, buf, order, c_sems, w_sems, out_sems = refs[4 + 2 * units :]
+    weights, contexts = refs[:4], refs[4 : 4 + 4 * units]
+    out, context, weight, buf, order, c_sems, w_sems, out_sems = refs[4 + 4 * units :]
     unit, side, quarter, group = place[UNIT], place[SIDE], place[QUARTER], place[GROUP]
     part = weights[0].shape[2]
     own = 4 * part
@@ -577,10 +605,11 @@
         pairs = []
         for k in range(units):
             source = unit ^ k
-            lanes = aligned((source >> 2) * 4 * own, 4 * own)
             at = aligned((source & 3) * slot, slot)
-            pairs.append((contexts[e * units + k], context.at[e, at, lanes]))
-        c_copies.append(start_copies(pairs, c_sems, e * units))
+            for h in range(2):
+                lanes = aligned((source >> 2) * 4 * own + h * 2 * own, 2 * own)
+                pairs.append((contexts[(2 * h + e) * units + k], context.at[e, at, lanes]))
+        c_copies.append(start_copies(pairs, c_sems, e * 2 * units))
     column = lax.broadcasted_iota(jnp.int32, (1, half), 1)
     row = lax.broadcasted_iota(jnp.int32, (half, half), 0)
     for turn in range(2):
@@ -673,6 +702,7 @@
     kv_head = rank * k_values.shape[0] // HD
     place = jnp.stack([jnp.asarray(v, jnp.int32) for v in (group, unit, side, quarter, kv_head)])
 
+    keep, send, pos = deal(place, row_lengths, row_dest, home, rows, slot)
     pieces, o_pieces = weight_pieces(
         place,
         q_values,
@@ -684,8 +714,8 @@
         o_values,
         o_scales,
         ranks,
+        [keep],
     )
-    keep, send, pos = deal(place, row_lengths, row_dest, home, rows, slot, pieces[:1])
     own_gain = lax.dynamic_slice_in_dim(
         gain.astype(F32), unit * 2 * features, 2 * features
     ).reshape(1, -1)
@@ -718,24 +748,37 @@
     weights = [collected, swap(collected, "dp"), swap(collected, "parts")]
     (o_pieces,) = gate([o_pieces], squares[1:])
     o_moved = lax.all_to_all(o_pieces, "tensor", split_axis=0, concat_axis=0, tiled=True)
-    (weights[2],) = gate(weights[2:], [weights[1], own_pieces[3]])
+    normed = normalize(place, squares, own_gain, keep, got, keep2, got2)
+    (weights[2],) = gate(weights[2:], [weights[1], own_pieces[3], normed])
 
     weights.append(swap(weights[2], "dp"))
-    normed = normalize(place, squares, own_gain, keep, got, keep2, got2)
-    parts = over_units(project(place, normed, own_pieces, weights, units))
-    (o_moved,) = gate([o_moved], parts[:1])
-    own_kv = key_value(parts, own_cos, own_sin)
+    kept_a, near_a, kept_b, near_b = project(place, normed, own_pieces, weights, units)
+    (o_moved,) = gate([o_moved], [kept_a])
+    parts = []
+    for kept, near in ((kept_a, near_a), (kept_b, near_b)):
+        got = swap(near, "tensor", 2)
+        sums = pair_sums(kept, got)
+        far = [swap(value, "tensor", 4 * (i + 1)) for i, value in enumerate(sums)]
+        parts.append([kept, got, *far])
+    own_kv = key_value(parts[0], own_cos, own_sin)
     other_kv = swap(own_kv, "tensor")
-    query = queries(parts, wide_cos, wide_sin)
     o_weights = [
         value.reshape(units, 2, *value.shape[1:]) for value in all_quarters(o_moved)
     ]
-    context = attend(place, row_lengths, row_dest, query, own_kv, other_kv, rows, slot)
-    mine = [context]
-    for k in range(1, units):
-        mine.append(swap(mine[k & (k - 1)], "tensor", 2 * (k & -k)))
-    theirs = [swap(value, "tensor") for value in mine]
-    return output(place, row_lengths, row_dest, o_weights, mine + theirs, rows, slot)
+    contexts = []
+    for h in range(2):
+        query = queries(parts[h], wide_cos, wide_sin, near_b.shape[2], contexts[units : units + 1])
+        context = attend(
+            place, row_lengths, row_dest, query, own_kv, other_kv, h, rows, slot
+        )
+        mine, theirs = [context], [swap(context, "tensor")]
+        for k in range(1, units):
+            mine.append(swap(mine[k & (k - 1)], "tensor", 2 * (k & -k)))
+            if k == 2:
+                (mine[2],) = gate(mine[2:], [mine[1], theirs[0]])
+        theirs += [swap(value, "tensor") for value in mine[1:]]
+        contexts += mine + theirs
+    return output(place, row_lengths, row_dest, o_weights, contexts, rows, slot)
 
 
 def solution(mesh):

time: 215 us -> 188 us (0.87)
  waiting for transfers between devices: 109 us -> 77.4 us
  starting transfers between devices: 41.7 us -> 53.7 us
  Pallas kernels: 46.8 us -> 35.3 us
  local copies, waits for them, and re-layouts: 11.1 us -> 15.9 us
    ppermute x28 -> x36, waiting for transfers between devices: 109 us -> 76 us  [swap(): return lax.ppermute(value, axis, [(i, i ^ mask) for i in range(size)])]
    ppermute x28 -> x36, starting transfers between devices: 37.3 us -> 48.6 us  [swap(): return lax.ppermute(value, axis, [(i, i ^ mask) for i in range(size)])]
    unnamed x62 -> x60, local copies, waits for them, and re-layouts: 9.33 us -> 15 us
    pallas_call x1 -> x2, Pallas kernels: 3.58 us -> 0.35 us  [queries(): pl.pallas_call(functools.partial(query_kernel, len(parts)), in_specs=[in_...]
    pallas_call x4 -> x7, Pallas kernels: 16 us -> 13.6 us  [the longest x1 6.15 us: deal(): pl.pallas_call(functools.partial(deal_kernel, rows, slot), grid=(features...]
  transfers between devices with their start and end apart: 30 -> 38, of which waited for: 16 -> 20; matrix products, arithmetic and copies ran while one was open for 3% -> 2% of each run, Pallas kernels for 14% -> 8%
where the time goes in v3:
time: 188 us; the launch traced here: 186 us
  waiting for transfers between devices  77.4 us (41%)
  starting transfers between devices  53.7 us (29%)
  Pallas kernels  35.3 us (19%)
  local copies, waits for them, and re-layouts  15.9 us (8%)
  other arithmetic  3.11 us (2%)
    ppermute x36, waiting for transfers between devices, swap(): return lax.ppermute(value, axis, [(i, i ^ mask) for i in range(size)])  76 us
    ppermute x36, starting transfers between devices, swap(): return lax.ppermute(value, axis, [(i, i ^ mask) for i in range(size)])  48.6 us
    unnamed x60, local copies, waits for them, and re-layouts  15 us
    pallas_call x1, Pallas kernels, project(): pl.pallas_call(functools.partial(project_kernel, units), in_specs=[in_sme...  9.36 us
    pallas_call x1, Pallas kernels, output(): pl.pallas_call(functools.partial(output_kernel, units, rows, slot), in_sp...  7.51 us
    pallas_call x1, Pallas kernels, deal(): pl.pallas_call(functools.partial(deal_kernel, rows, slot), grid=(features...  6.15 us
    all_to_all x1, starting transfers between devices, body(): lax.all_to_all(o_pieces, 'tensor', split_axis=0, concat_axis=0, tiled=True)  4.41 us
    pallas_call x1, Pallas kernels, weight_pieces(): pl.pallas_call(functools.partial(pieces_kernel, units, len(after)), in_sp...  3.93 us
  transfers between devices with their start and end apart: 38, of which 20 were waited for; matrix products, arithmetic and copies ran while one was open for 2% of the time, Pallas kernels for 8%

profile of v3, /device:TPU:0, one launch (start us, length us, event | category | flops | bytes accessed | tf_op | source)
XLA Modules:
  0.0 185.9 jit_solution(3343311143298319716)
XLA Ops:
  0.7 6.1 %deal.1 = (bf16[384,1024]{1,0:T(8,128)(2,1)}, bf16[384,1024]{1,0:T(8,128)(2,1)}, f32[192,128]{1,0:T(8,128)}) custom-call(s32[5]{0:T(128)} %stack.23.place, s32[16]{0:T(128)} %lens.7, s32[16]{0:T(128)} %dest.7, bf16[1024,1536]{1,0:T(8,128)(2,1)} %home.1), custom_call_target="tpu_custom_call" | custom-call | tf_op jit(solution)/shard_map/deal/pallas_call | solution.py:238
  6.8 3.9 %weight_pieces.1 = (bf16[640,256]{1,0:T(8,128)(2,1)}, bf16[640,256]{1,0:T(8,128)(2,1)}, bf16[640,256]{1,0:T(8,128)(2,1)}, bf16[640,256]{1,0:T(8,128)(2,1)}, bf16[8,64,1024]{2,1,0:T(8,128)(2,1)}) custom-call(s32[5]{0:T(128)} %stack.23.place, f32[2,64]{1,0:T(2,128)} %bitcast.16, f32[2,64]{1,0:T(2,128)} %ks.1, f32[2,64]{1,0:T(2,128)} %vs.1, f32[2,64]{1,0:T(2,128)} %os.1, ...), custom_call_target="tpu_custom_call" | custom-call | tf_op jit(solution)/shard_map/weight_pieces/pallas_call | solution.py:164
  10.8 3.1 %collective-permute-start.3 = (bf16[640,256]{1,0:T(8,128)(2,1)}, bf16[640,256]{1,0:T(8,128)(2,1)S(1)}, u32[]{:S(2)}, u32[]{:S(2)}) collective-permute-start(bf16[640,256]{1,0:T(8,128)(2,1)} %get-tuple-element.22), channel_id=1, source_target_pairs={{0,2},{1,3},{2,0},{3,1},{4,6},{5,7},{6,4},{7,5},{8,10},{9,11},{10,... | collective-permute-start | bytes 983048 | tf_op jit(solution)/shard_map/ppermute | solution.py:667
  16.0 2.6 %collective-permute-start.4 = (bf16[640,256]{1,0:T(8,128)(2,1)}, bf16[640,256]{1,0:T(8,128)(2,1)}, u32[]{:S(2)}, u32[]{:S(2)}) collective-permute-start(bf16[640,256]{1,0:T(8,128)(2,1)} %get-tuple-element.23), channel_id=1, source_target_pairs={{0,4},{1,5},{2,6},{3,7},{4,0},{5,1},{6,2},{7,3},{8,12},{9,13},{10,... | collective-permute-start | bytes 983048 | tf_op jit(solution)/shard_map/ppermute | solution.py:667
  18.7 7.6 %collective-permute-done.3.refs_4_ = bf16[640,256]{1,0:T(8,128)(2,1)S(1)} collective-permute-done((bf16[640,256]{1,0:T(8,128)(2,1)}, bf16[640,256]{1,0:T(8,128)(2,1)S(1)}, u32[]{:S(2)}, u32[]{:S(2)}) %collective-permute-start.3) | collective-permute-done | bytes 327712 | tf_op jit(solution)/shard_map/ppermute | solution.py:667
  27.1 2.7 %collective-permute-start.5 = (bf16[640,256]{1,0:T(8,128)(2,1)}, bf16[640,256]{1,0:T(8,128)(2,1)}, u32[]{:S(2)}, u32[]{:S(2)}) collective-permute-start(bf16[640,256]{1,0:T(8,128)(2,1)} %get-tuple-element.24), channel_id=1, source_target_pairs={{0,6},{1,7},{2,4},{3,5},{4,2},{5,3},{6,0},{7,1},{8,14},{9,15},{10,... | collective-permute-start | bytes 983048 | tf_op jit(solution)/shard_map/ppermute | solution.py:667
  31.0 10.9 %collective-permute-done.4.refs_5_ = bf16[640,256]{1,0:T(8,128)(2,1)} collective-permute-done((bf16[640,256]{1,0:T(8,128)(2,1)}, bf16[640,256]{1,0:T(8,128)(2,1)}, u32[]{:S(2)}, u32[]{:S(2)}) %collective-permute-start.4) | collective-permute-done | bytes 327712 | tf_op jit(solution)/shard_map/ppermute | solution.py:667
  45.3 4.1 %collective-permute-done.7.refs_13_.rest_2_ = bf16[640,256]{1,0:T(8,128)(2,1)S(1)} collective-permute-done((bf16[640,256]{1,0:T(8,128)(2,1)}, bf16[640,256]{1,0:T(8,128)(2,1)S(1)}, u32[]{:S(2)}, u32[]{:S(2)}) %collective-permute-start.7) | collective-permute-done | bytes 327712 | tf_op jit(solution)/shard_map/ppermute | solution.py:667
  56.5 2.5 %collective-permute-start.10 = (f32[8,768]{1,0:T(8,128)S(1)}, f32[8,768]{1,0:T(8,128)S(1)}, u32[]{:S(2)}, u32[]{:S(2)}) collective-permute-start(f32[8,768]{1,0:T(8,128)S(1)} %get-tuple-element.27.rest_0_), channel_id=1, source_target_pairs={{0,6},{1,7},{2,4},{3,5},{4,2},{5,3},{6,0},{7,1},{8,14},{9,15},{10,... | collective-permute-start | bytes 73736 | tf_op jit(solution)/shard_map/ppermute | solution.py:667
  65.8 4.4 %all-to-all-start = ((bf16[8,64,1024]{2,1,0:T(8,128)(2,1)}), bf16[8,64,1024]{2,1,0:T(8,128)(2,1)}, u32[]{:S(2)}, u32[]{:S(2)}) async-start(bf16[8,64,1024]{2,1,0:T(8,128)(2,1)} %gate.5), calls=%async_computation | async-start | bytes 2097152 | tf_op jit(solution)/shard_map/all_to_all | solution.py:750
  81.0 2.4 %collective-permute-done.14.rest_7_ = bf16[3,640,256]{2,1,0:T(8,128)(2,1)S(1)} collective-permute-done((bf16[3,640,256]{2,1,0:T(8,128)(2,1)}, bf16[3,640,256]{2,1,0:T(8,128)(2,1)S(1)}, u32[]{:S(2)}, u32[]{:S(2)}) %collective-permute-start.14) | collective-permute-done | bytes 983072 | tf_op jit(solution)/shard_map/ppermute | solution.py:667
  84.5 9.4 %project.1 = (bf16[2,192,768]{2,1,0:T(8,128)(2,1)}, bf16[2,192,768]{2,1,0:T(8,128)(2,1)}, bf16[2,192,512]{2,1,0:T(8,128)(2,1)}, bf16[2,192,512]{2,1,0:T(8,128)(2,1)}) custom-call(s32[5]{0:T(128)} %stack.23.place, bf16[768,2048]{1,0:T(8,128)(2,1)} %copy-done, bf16[640,256]{1,0:T(8,128)(2,1)} %get-tuple-element.26.rest_0_, bf16[640,256]{1,0:T(8,128)(2,1)} %copy-done.12, ...), custom_call_target="tpu_custom_call" | custom-call | tf_op jit(solution)/shard_map/project/pallas_call | solution.py:446
  99.0 14.4 %collective-permute-done.18.got.refs_1_ = bf16[2,192,768]{2,1,0:T(8,128)(2,1)S(1)} collective-permute-done((bf16[2,192,768]{2,1,0:T(8,128)(2,1)}, bf16[2,192,768]{2,1,0:T(8,128)(2,1)S(1)}, u32[]{:S(2)}, u32[]{:S(2)}) %collective-permute-start.18) | collective-permute-done | bytes 589856 | tf_op jit(solution)/shard_map/ppermute | solution.py:667
  114.7 6.0 %collective-permute-done.16 = bf16[8,64,1024]{2,1,0:T(8,128)(2,1)S(1)} collective-permute-done((bf16[8,64,1024]{2,1,0:T(8,128)(2,1)}, bf16[8,64,1024]{2,1,0:T(8,128)(2,1)S(1)}, u32[]{:S(2)}, u32[]{:S(2)}) %collective-permute-start.16) | collective-permute-done | bytes 1048608 | tf_op jit(solution)/shard_map/ppermute | solution.py:667
  120.6 5.2 %collective-permute-done.28.got.refs_1_ = bf16[2,192,512]{2,1,0:T(8,128)(2,1)S(1)} collective-permute-done((bf16[2,192,512]{2,1,0:T(8,128)(2,1)}, bf16[2,192,512]{2,1,0:T(8,128)(2,1)S(1)}, u32[]{:S(2)}, u32[]{:S(2)}) %collective-permute-start.28) | collective-permute-done | bytes 393248 | tf_op jit(solution)/shard_map/ppermute | solution.py:667
  128.7 3.0 %collective-permute-done.20.other_kv = bf16[192,256]{1,0:T(8,128)(2,1)S(1)} collective-permute-done((bf16[192,256]{1,0:T(8,128)(2,1)S(1)}, bf16[192,256]{1,0:T(8,128)(2,1)S(1)}, u32[]{:S(2)}, u32[]{:S(2)}) %collective-permute-start.20) | collective-permute-done | bytes 98336 | tf_op jit(solution)/shard_map/ppermute | solution.py:667
  145.1 3.0 %collective-permute-start.30 = (bf16[192,512]{1,0:T(8,128)(2,1)S(1)}, bf16[192,512]{1,0:T(8,128)(2,1)S(1)}, u32[]{:S(2)}, u32[]{:S(2)}) collective-permute-start(bf16[192,512]{1,0:T(8,128)(2,1)S(1)} %attend.3.refs_12_), channel_id=1, source_target_pairs={{0,2},{1,3},{2,0},{3,1},{4,6},{5,7},{6,4},{7,5},{8,10},{9,11},{10,... | collective-permute-start | bytes 589832 | tf_op jit(solution)/shard_map/ppermute | solution.py:667
  149.5 4.3 %collective-permute-done.31.refs_0_ = bf16[192,512]{1,0:T(8,128)(2,1)S(1)} collective-permute-done((bf16[192,512]{1,0:T(8,128)(2,1)S(1)}, bf16[192,512]{1,0:T(8,128)(2,1)S(1)}, u32[]{:S(2)}, u32[]{:S(2)}) %collective-permute-start.31) | collective-permute-done | bytes 196640 | tf_op jit(solution)/shard_map/ppermute | solution.py:667
  154.5 2.8 %collective-permute-start.25 = (bf16[192,512]{1,0:T(8,128)(2,1)S(1)}, bf16[192,512]{1,0:T(8,128)(2,1)S(1)}, u32[]{:S(2)}, u32[]{:S(2)}) collective-permute-start(bf16[192,512]{1,0:T(8,128)(2,1)S(1)} %collective-permute-done.21.refs_1_.refs_5_), channel_id=1, source_target_pairs={{0,1},{1,0},{2,3},{3,2},{4,5},{5,4},{6,7},{7,6},{8,9},{9,8},{10,11... | collective-permute-start | bytes 589832 | tf_op jit(solution)/shard_map/ppermute | solution.py:667
  160.3 4.7 %collective-permute-start.34 = (bf16[192,512]{1,0:T(8,128)(2,1)S(1)}, bf16[192,512]{1,0:T(8,128)(2,1)S(1)}, u32[]{:S(2)}, u32[]{:S(2)}) collective-permute-start(bf16[192,512]{1,0:T(8,128)(2,1)S(1)} %collective-permute-done.30.refs_1_.refs_13_), channel_id=1, source_target_pairs={{0,1},{1,0},{2,3},{3,2},{4,5},{5,4},{6,7},{7,6},{8,9},{9,8},{10,11... | collective-permute-start | bytes 589832 | tf_op jit(solution)/shard_map/ppermute | solution.py:667
  167.4 3.9 %collective-permute-done.34.refs_17_ = bf16[192,512]{1,0:T(8,128)(2,1)S(1)} collective-permute-done((bf16[192,512]{1,0:T(8,128)(2,1)S(1)}, bf16[192,512]{1,0:T(8,128)(2,1)S(1)}, u32[]{:S(2)}, u32[]{:S(2)}) %collective-permute-start.34) | collective-permute-done | bytes 196640 | tf_op jit(solution)/shard_map/ppermute | solution.py:667
  171.3 4.2 %collective-permute-done.27.refs_11_ = bf16[192,512]{1,0:T(8,128)(2,1)S(1)} collective-permute-done((bf16[192,512]{1,0:T(8,128)(2,1)S(1)}, bf16[192,512]{1,0:T(8,128)(2,1)S(1)}, u32[]{:S(2)}, u32[]{:S(2)}) %collective-permute-start.27) | collective-permute-done | bytes 196640 | tf_op jit(solution)/shard_map/ppermute | solution.py:667
  175.5 2.8 %collective-permute-done.36.refs_19_ = bf16[192,512]{1,0:T(8,128)(2,1)S(1)} collective-permute-done((bf16[192,512]{1,0:T(8,128)(2,1)S(1)}, bf16[192,512]{1,0:T(8,128)(2,1)S(1)}, u32[]{:S(2)}, u32[]{:S(2)}) %collective-permute-start.36) | collective-permute-done | bytes 196640 | tf_op jit(solution)/shard_map/ppermute | solution.py:667
  178.3 7.5 %output.1 = bf16[1024,768]{1,0:T(8,128)(2,1)} custom-call(s32[5]{0:T(128)S(1)} %copy-done.23, s32[16]{0:T(128)S(1)} %copy-done.26, s32[16]{0:T(128)S(1)} %copy-done.27, bf16[4,2,64,1024]{3,2,1,0:T(8,128)(2,1)} %bitcast.7.refs_0_, bf16[4,2,64,1024]{3,2,1,0:T(8,128)(2,1)S(1)} %bitcast.12, bf16[4,2,64,1024]{3,2,1,0:T(8,128)(2,1)S(1)} %bitcast.11, ...), custom_call_target="tpu_custom_call" | custom-call | tf_op jit(solution)/shard_map/output/pallas_call | solution.py:646
  (139 shorter events, 64.1 us)
Async XLA Ops:
  10.8 15.6 %collective-permute-start.3 = (bf16[640,256]{1,0:T(8,128)(2,1)}, bf16[640,256]{1,0:T(8,128)(2,1)S(1)}, u32[]{:S(2)}, u32[]{:S(2)}) collective-permute-start(bf16[640,256]{1,0:T(8,128)(2,1)} %get-tuple-element.22), channel_id=1, source_target_pairs={{0,2},{1,3},{2,0},{3,1},{4,6},{5,7},{6,4},{7,5},{8,10},{9,11},{10,... | collective-permute-start | bytes 983048 | tf_op jit(solution)/shard_map/ppermute | solution.py:667
  13.9 35.5 %collective-permute-start.2 = (bf16[384,1024]{1,0:T(8,128)(2,1)}, bf16[384,1024]{1,0:T(8,128)(2,1)S(1)}, u32[]{:S(2)}, u32[]{:S(2)}) collective-permute-start(bf16[384,1024]{1,0:T(8,128)(2,1)} %get-tuple-element.21), channel_id=1, source_target_pairs={{0,9},{1,8},{2,11},{3,10},{4,13},{5,12},{6,15},{7,14},{8,1},{9,0},... | collective-permute-start | bytes 2359304 | tf_op jit(solution)/shard_map/ppermute | solution.py:735
  14.5 34.8 %collective-permute-start = (bf16[384,1024]{1,0:T(8,128)(2,1)}, bf16[384,1024]{1,0:T(8,128)(2,1)S(1)}, u32[]{:S(2)}, u32[]{:S(2)}) collective-permute-start(bf16[384,1024]{1,0:T(8,128)(2,1)} %get-tuple-element.21), channel_id=1, source_target_pairs={{0,8},{8,0},{1,9},{9,1},{2,10},{10,2},{3,11},{11,3},{4,12},{12,4},... | collective-permute-start | bytes 2359304 | tf_op jit(solution)/shard_map/ppermute | solution.py:667
  15.5 35.3 %collective-permute-start.1 = (bf16[384,1024]{1,0:T(8,128)(2,1)S(1)}, bf16[384,1024]{1,0:T(8,128)(2,1)S(1)}, u32[]{:S(2)}, u32[]{:S(2)}) collective-permute-start(bf16[384,1024]{1,0:T(8,128)(2,1)S(1)} %copy-done.3), channel_id=1, source_target_pairs={{0,1},{1,0},{2,3},{3,2},{4,5},{5,4},{6,7},{7,6},{8,9},{9,8},{10,11... | collective-permute-start | bytes 2359304 | tf_op jit(solution)/shard_map/ppermute | solution.py:667
  16.0 25.9 %collective-permute-start.4 = (bf16[640,256]{1,0:T(8,128)(2,1)}, bf16[640,256]{1,0:T(8,128)(2,1)}, u32[]{:S(2)}, u32[]{:S(2)}) collective-permute-start(bf16[640,256]{1,0:T(8,128)(2,1)} %get-tuple-element.23), channel_id=1, source_target_pairs={{0,4},{1,5},{2,6},{3,7},{4,0},{5,1},{6,2},{7,3},{8,12},{9,13},{10,... | collective-permute-start | bytes 983048 | tf_op jit(solution)/shard_map/ppermute | solution.py:667
  27.1 16.3 %collective-permute-start.5 = (bf16[640,256]{1,0:T(8,128)(2,1)}, bf16[640,256]{1,0:T(8,128)(2,1)}, u32[]{:S(2)}, u32[]{:S(2)}) collective-permute-start(bf16[640,256]{1,0:T(8,128)(2,1)} %get-tuple-element.24), channel_id=1, source_target_pairs={{0,6},{1,7},{2,4},{3,5},{4,2},{5,3},{6,0},{7,1},{8,14},{9,15},{10,... | collective-permute-start | bytes 983048 | tf_op jit(solution)/shard_map/ppermute | solution.py:667
  55.0 24.0 %collective-permute-start.13 = (bf16[3,640,256]{2,1,0:T(8,128)(2,1)}, bf16[3,640,256]{2,1,0:T(8,128)(2,1)}, u32[]{:S(2)}, u32[]{:S(2)}) collective-permute-start(bf16[3,640,256]{2,1,0:T(8,128)(2,1)} %get-tuple-element.28.rest_4_), channel_id=1, source_target_pairs={{0,16},{16,0},{1,17},{17,1},{2,18},{18,2},{3,19},{19,3},{4,20},{20... | collective-permute-start | bytes 2949128 | tf_op jit(solution)/shard_map/ppermute | solution.py:667
  56.5 22.6 %collective-permute-start.12 = (bf16[3,640,256]{2,1,0:T(8,128)(2,1)}, bf16[3,640,256]{2,1,0:T(8,128)(2,1)}, u32[]{:S(2)}, u32[]{:S(2)}) collective-permute-start(bf16[3,640,256]{2,1,0:T(8,128)(2,1)} %get-tuple-element.28.rest_4_), channel_id=1, source_target_pairs={{0,8},{8,0},{1,9},{9,1},{2,10},{10,2},{3,11},{11,3},{4,12},{12,4},... | collective-permute-start | bytes 2949128 | tf_op jit(solution)/shard_map/ppermute | solution.py:667
  65.8 29.5 %all-to-all-start = ((bf16[8,64,1024]{2,1,0:T(8,128)(2,1)}), bf16[8,64,1024]{2,1,0:T(8,128)(2,1)}, u32[]{:S(2)}, u32[]{:S(2)}) async-start(bf16[8,64,1024]{2,1,0:T(8,128)(2,1)} %gate.5), calls=%async_computation | async-start | bytes 2097152 | tf_op jit(solution)/shard_map/all_to_all | solution.py:750
  96.4 24.2 %collective-permute-start.16 = (bf16[8,64,1024]{2,1,0:T(8,128)(2,1)}, bf16[8,64,1024]{2,1,0:T(8,128)(2,1)S(1)}, u32[]{:S(2)}, u32[]{:S(2)}) collective-permute-start(bf16[8,64,1024]{2,1,0:T(8,128)(2,1)} %gate.7), channel_id=1, source_target_pairs={{0,16},{16,0},{1,17},{17,1},{2,18},{18,2},{3,19},{19,3},{4,20},{20... | collective-permute-start | bytes 3145736 | tf_op jit(solution)/shard_map/ppermute | solution.py:667
  97.0 16.5 %collective-permute-start.18 = (bf16[2,192,768]{2,1,0:T(8,128)(2,1)}, bf16[2,192,768]{2,1,0:T(8,128)(2,1)S(1)}, u32[]{:S(2)}, u32[]{:S(2)}) collective-permute-start(bf16[2,192,768]{2,1,0:T(8,128)(2,1)} %get-tuple-element.30), channel_id=1, source_target_pairs={{0,2},{1,3},{2,0},{3,1},{4,6},{5,7},{6,4},{7,5},{8,10},{9,11},{10,... | collective-permute-start | bytes 1769480 | tf_op jit(solution)/shard_map/ppermute | solution.py:667
  97.2 60.1 %collective-permute-start.15 = (bf16[8,64,1024]{2,1,0:T(8,128)(2,1)}, bf16[8,64,1024]{2,1,0:T(8,128)(2,1)S(1)}, u32[]{:S(2)}, u32[]{:S(2)}) collective-permute-start(bf16[8,64,1024]{2,1,0:T(8,128)(2,1)} %gate.7), channel_id=1, source_target_pairs={{0,8},{8,0},{1,9},{9,1},{2,10},{10,2},{3,11},{11,3},{4,12},{12,4},... | collective-permute-start | bytes 3145736 | tf_op jit(solution)/shard_map/ppermute | solution.py:667
  97.2 28.6 %collective-permute-start.28 = (bf16[2,192,512]{2,1,0:T(8,128)(2,1)}, bf16[2,192,512]{2,1,0:T(8,128)(2,1)S(1)}, u32[]{:S(2)}, u32[]{:S(2)}) collective-permute-start(bf16[2,192,512]{2,1,0:T(8,128)(2,1)} %get-tuple-element.32), channel_id=1, source_target_pairs={{0,2},{1,3},{2,0},{3,1},{4,6},{5,7},{6,4},{7,5},{8,10},{9,11},{10,... | collective-permute-start | bytes 1179656 | tf_op jit(solution)/shard_map/ppermute | solution.py:667
  113.6 13.3 %collective-permute-start.19 = (bf16[192,768]{1,0:T(8,128)(2,1)S(1)}, bf16[192,768]{1,0:T(8,128)(2,1)S(1)}, u32[]{:S(2)}, u32[]{:S(2)}) collective-permute-start(bf16[192,768]{1,0:T(8,128)(2,1)S(1)} %pair_sums.2), channel_id=1, source_target_pairs={{0,4},{1,5},{2,6},{3,7},{4,0},{5,1},{6,2},{7,3},{8,12},{9,13},{10,... | collective-permute-start | bytes 884744 | tf_op jit(solution)/shard_map/ppermute | solution.py:667
  120.6 57.6 %collective-permute-start.17 = (bf16[8,64,1024]{2,1,0:T(8,128)(2,1)S(1)}, bf16[8,64,1024]{2,1,0:T(8,128)(2,1)S(1)}, u32[]{:S(2)}, u32[]{:S(2)}) collective-permute-start(bf16[8,64,1024]{2,1,0:T(8,128)(2,1)S(1)} %collective-permute-done.16), channel_id=1, source_target_pairs={{0,8},{8,0},{1,9},{9,1},{2,10},{10,2},{3,11},{11,3},{4,12},{12,4},... | collective-permute-start | bytes 3145736 | tf_op jit(solution)/shard_map/ppermute | solution.py:667
  125.9 11.2 %collective-permute-start.29 = (bf16[192,512]{1,0:T(8,128)(2,1)S(1)}, bf16[192,512]{1,0:T(8,128)(2,1)S(1)}, u32[]{:S(2)}, u32[]{:S(2)}) collective-permute-start(bf16[192,512]{1,0:T(8,128)(2,1)S(1)} %pair_sums.3), channel_id=1, source_target_pairs={{0,4},{1,5},{2,6},{3,7},{4,0},{5,1},{6,2},{7,3},{8,12},{9,13},{10,... | collective-permute-start | bytes 589832 | tf_op jit(solution)/shard_map/ppermute | solution.py:667
  134.9 9.8 %collective-permute-start.22 = (bf16[192,512]{1,0:T(8,128)(2,1)S(1)}, bf16[192,512]{1,0:T(8,128)(2,1)S(1)}, u32[]{:S(2)}, u32[]{:S(2)}) collective-permute-start(bf16[192,512]{1,0:T(8,128)(2,1)S(1)} %attend.2.refs_4_), channel_id=1, source_target_pairs={{0,4},{1,5},{2,6},{3,7},{4,0},{5,1},{6,2},{7,3},{8,12},{9,13},{10,... | collective-permute-start | bytes 589832 | tf_op jit(solution)/shard_map/ppermute | solution.py:667
  144.7 9.1 %collective-permute-start.31 = (bf16[192,512]{1,0:T(8,128)(2,1)S(1)}, bf16[192,512]{1,0:T(8,128)(2,1)S(1)}, u32[]{:S(2)}, u32[]{:S(2)}) collective-permute-start(bf16[192,512]{1,0:T(8,128)(2,1)S(1)} %attend.3.refs_12_), channel_id=1, source_target_pairs={{0,4},{1,5},{2,6},{3,7},{4,0},{5,1},{6,2},{7,3},{8,12},{9,13},{10,... | collective-permute-start | bytes 589832 | tf_op jit(solution)/shard_map/ppermute | solution.py:667
  145.1 9.4 %collective-permute-start.30 = (bf16[192,512]{1,0:T(8,128)(2,1)S(1)}, bf16[192,512]{1,0:T(8,128)(2,1)S(1)}, u32[]{:S(2)}, u32[]{:S(2)}) collective-permute-start(bf16[192,512]{1,0:T(8,128)(2,1)S(1)} %attend.3.refs_12_), channel_id=1, source_target_pairs={{0,2},{1,3},{2,0},{3,1},{4,6},{5,7},{6,4},{7,5},{8,10},{9,11},{10,... | collective-permute-start | bytes 589832 | tf_op jit(solution)/shard_map/ppermute | solution.py:667
  148.0 11.2 %collective-permute-start.26 = (bf16[192,512]{1,0:T(8,128)(2,1)S(1)}, bf16[192,512]{1,0:T(8,128)(2,1)S(1)}, u32[]{:S(2)}, u32[]{:S(2)}) collective-permute-start(bf16[192,512]{1,0:T(8,128)(2,1)S(1)} %gate.8.refs_6_), channel_id=1, source_target_pairs={{0,1},{1,0},{2,3},{3,2},{4,5},{5,4},{6,7},{7,6},{8,9},{9,8},{10,11... | collective-permute-start | bytes 589832 | tf_op jit(solution)/shard_map/ppermute | solution.py:667
  154.5 10.5 %collective-permute-start.25 = (bf16[192,512]{1,0:T(8,128)(2,1)S(1)}, bf16[192,512]{1,0:T(8,128)(2,1)S(1)}, u32[]{:S(2)}, u32[]{:S(2)}) collective-permute-start(bf16[192,512]{1,0:T(8,128)(2,1)S(1)} %collective-permute-done.21.refs_1_.refs_5_), channel_id=1, source_target_pairs={{0,1},{1,0},{2,3},{3,2},{4,5},{5,4},{6,7},{7,6},{8,9},{9,8},{10,11... | collective-permute-start | bytes 589832 | tf_op jit(solution)/shard_map/ppermute | solution.py:667
  160.3 11.0 %collective-permute-start.34 = (bf16[192,512]{1,0:T(8,128)(2,1)S(1)}, bf16[192,512]{1,0:T(8,128)(2,1)S(1)}, u32[]{:S(2)}, u32[]{:S(2)}) collective-permute-start(bf16[192,512]{1,0:T(8,128)(2,1)S(1)} %collective-permute-done.30.refs_1_.refs_13_), channel_id=1, source_target_pairs={{0,1},{1,0},{2,3},{3,2},{4,5},{5,4},{6,7},{7,6},{8,9},{9,8},{10,11... | collective-permute-start | bytes 589832 | tf_op jit(solution)/shard_map/ppermute | solution.py:667
  165.0 10.5 %collective-permute-start.27 = (bf16[192,512]{1,0:T(8,128)(2,1)S(1)}, bf16[192,512]{1,0:T(8,128)(2,1)S(1)}, u32[]{:S(2)}, u32[]{:S(2)}) collective-permute-start(bf16[192,512]{1,0:T(8,128)(2,1)S(1)} %collective-permute-done.24.refs_7_), channel_id=1, source_target_pairs={{0,1},{1,0},{2,3},{3,2},{4,5},{5,4},{6,7},{7,6},{8,9},{9,8},{10,11... | collective-permute-start | bytes 589832 | tf_op jit(solution)/shard_map/ppermute | solution.py:667
  165.2 13.1 %collective-permute-start.36 = (bf16[192,512]{1,0:T(8,128)(2,1)S(1)}, bf16[192,512]{1,0:T(8,128)(2,1)S(1)}, u32[]{:S(2)}, u32[]{:S(2)}) collective-permute-start(bf16[192,512]{1,0:T(8,128)(2,1)S(1)} %collective-permute-done.33.refs_15_), channel_id=1, source_target_pairs={{0,1},{1,0},{2,3},{3,2},{4,5},{5,4},{6,7},{7,6},{8,9},{9,8},{10,11... | collective-permute-start | bytes 589832 | tf_op jit(solution)/shard_map/ppermute | solution.py:667
  (44 other events, 354.1 us)

commit v4 on v3

--- a/solution.py
+++ b/solution.py
@@ -81,15 +81,14 @@
     return full, short
 
 
-def pieces_kernel(units, count, place, qs, ks, vs, os, q_hbm, k_hbm, v_hbm, o_hbm, *rest):
+def pieces_kernel(units, count, place, qs, ks, vs, q_hbm, k_hbm, v_hbm, *rest):
     rest = rest[count:]
-    outs, o_out = rest[:units], rest[units]
-    q_buf, k_buf, v_buf, o_buf, pieces, o_pieces, in_sems, out_sems = rest[units + 1 :]
+    outs = rest[:units]
+    q_buf, k_buf, v_buf, pieces, in_sems, out_sems = rest[units:]
     unit, quarter, head = place[UNIT], place[QUARTER], place[KV_HEAD]
     _, size, own = q_buf.shape
     part = k_buf.shape[1]
     width = min(size, own)
-    ranks, o_rows, features = o_pieces.shape
     copies = []
     for k in range(units):
         at = ((unit ^ k) * 4 + quarter) * size
@@ -104,9 +103,6 @@
                 3 * k,
             )
         )
-    (o_copy,) = start_copies(
-        [(o_hbm.at[aligned(quarter * o_rows, o_rows)], o_buf)], in_sems, 3 * units
-    )
     sent = []
     for k in range(units):
         for copy in copies[k]:
@@ -130,68 +126,64 @@
         if width < own:
             pieces[k, size:, width:] = jnp.zeros((2 * part, own - width), BF16)
         sent += start_copies([(pieces.at[k], outs[k])], out_sems, k)
-    o_copy.wait()
-    o_head = quarter * o_rows // HD
-    for rank in range(ranks):
-        for i in range(features // HD):
-            block = rank * (features // HD) + i
-            scaled = o_buf[:, block * HD : (block + 1) * HD].astype(F32) * os[o_head, block]
-            o_pieces[rank, :, i * HD : (i + 1) * HD] = scaled.astype(BF16)
-    sent += start_copies([(o_pieces, o_out)], out_sems, units)
     for copy in sent:
         copy.wait()
 
 
-def weight_pieces(
-    place,
-    q_values,
-    q_scales,
-    k_values,
-    k_scales,
-    v_values,
-    v_scales,
-    o_values,
-    o_scales,
-    ranks,
-    after,
-):
-    units = ranks // 2
-    o_shape = (ranks, o_values.shape[0] // 4, o_values.shape[1] // ranks)
+def weight_pieces(place, q_values, q_scales, k_values, k_scales, v_values, v_scales, units, after):
     own = q_values.shape[1]
     part = k_values.shape[0]
     size = q_values.shape[0] // units // 4
     rows = size + 2 * part * max(1, size // own)
-    outs = pl.pallas_call(
+    return pl.pallas_call(
         functools.partial(pieces_kernel, units, len(after)),
-        in_specs=[in_smem()] * 5 + [in_hbm()] * 4 + [anywhere()] * len(after),
-        out_specs=[anywhere()] * (units + 1),
-        out_shape=[jax.ShapeDtypeStruct((rows, own), BF16)] * units
-        + [jax.ShapeDtypeStruct(o_shape, BF16)],
+        in_specs=[in_smem()] * 4 + [in_hbm()] * 3 + [anywhere()] * len(after),
+        out_specs=[anywhere()] * units,
+        out_shape=[jax.ShapeDtypeStruct((rows, own), BF16)] * units,
         scratch_shapes=[
             pltpu.VMEM((units, size, own), BF16),
             pltpu.VMEM((units, part, size), BF16),
             pltpu.VMEM((units, part, size), BF16),
-            pltpu.VMEM((o_shape[1], o_values.shape[1]), BF16),
             pltpu.VMEM((units, rows, own), BF16),
-            pltpu.VMEM(o_shape, BF16),
-            pltpu.SemaphoreType.DMA((3 * units + 1,)),
-            pltpu.SemaphoreType.DMA((units + 1,)),
+            pltpu.SemaphoreType.DMA((3 * units,)),
+            pltpu.SemaphoreType.DMA((units,)),
         ],
         compiler_params=pltpu.CompilerParams(vmem_limit_bytes=ALL),
         name="weight_pieces",
-    )(
-        place,
-        q_scales.T,
-        k_scales,
-        v_scales,
-        o_scales,
-        q_values,
-        k_values,
-        v_values,
-        o_values,
-        *after,
-    )
-    return outs[:units], outs[units]
+    )(place, q_scales.T, k_scales, v_scales, q_values, k_values, v_values, *after)
+
+
+def o_pieces_kernel(count, place, scales, o_hbm, *rest):
+    out, o_buf, pieces, sem, out_sem = rest[count:]
+    ranks, rows, features = pieces.shape
+    first = place[QUARTER] * rows
+    (copy,) = start_copies([(o_hbm.at[aligned(first, rows)], o_buf)], sem)
+    copy.wait()
+    for rank in range(ranks):
+        for i in range(features // HD):
+            block = rank * (features // HD) + i
+            scaled = o_buf[:, block * HD : (block + 1) * HD].astype(F32) * scales[first // HD, block]
+            pieces[rank, :, i * HD : (i + 1) * HD] = scaled.astype(BF16)
+    (sent,) = start_copies([(pieces, out)], out_sem)
+    sent.wait()
+
+
+def output_pieces(place, o_values, o_scales, ranks, after):
+    shape = (ranks, o_values.shape[0] // 4, o_values.shape[1] // ranks)
+    return pl.pallas_call(
+        functools.partial(o_pieces_kernel, len(after)),
+        in_specs=[in_smem()] * 2 + [in_hbm()] + [anywhere()] * len(after),
+        out_specs=anywhere(),
+        out_shape=jax.ShapeDtypeStruct(shape, BF16),
+        scratch_shapes=[
+            pltpu.VMEM((shape[1], o_values.shape[1]), BF16),
+            pltpu.VMEM(shape, BF16),
+            pltpu.SemaphoreType.DMA((1,)),
+            pltpu.SemaphoreType.DMA((1,)),
+        ],
+        compiler_params=pltpu.CompilerParams(vmem_limit_bytes=ALL),
+        name="output_pieces",
+    )(place, o_scales, o_values, *after)
 
 
 def deal_kernel(rows, slot, place, lens, dest, home, keep, send, pos, pick):
@@ -370,68 +362,61 @@
     )(place, *squares, gain, keep, got, keep2, got2)
 
 
-def project_kernel(units, place, normed, *rest):
+def project_kernel(units, place, tokens, *rest):
     own_pieces, weights, outs = rest[:4], rest[4:8], rest[8:12]
-    weight, tokens, buf, x_sem, w_sems, out_sems = rest[12:]
+    buf, out_sems = rest[12:]
     unit, quarter = place[UNIT], place[QUARTER]
     count, wide = tokens.shape
     slot = count // BLOCKS
-    own = weight.shape[3]
+    rows, own = own_pieces[0].shape
     size = wide // 4
     width = min(size, own)
-    part = (weight.shape[2] - size) // (size // width)
-    (x_copy,) = start_copies([(normed, tokens)], x_sem)
-    copies = start_copies(
-        [
-            (
-                weights[r].at[k - 1] if k else own_pieces[r],
-                weight.at[quarter ^ r, (k >> 2) * 4 + ((unit ^ k) & 3)],
-            )
-            for k in range(units)
-            for r in range(4)
-        ],
-        w_sems,
-    )
-    x_copy.wait()
+    part = (rows - size) // (size // width)
+
+    def weight(k, r, rows, lanes=slice(None)):
+        return weights[r][k - 1, rows, lanes] if k else own_pieces[r][rows, lanes]
+
+    def features(r, first, count):
+        return tokens[:, aligned((quarter ^ r) * size + first, count)]
+
     sent = []
 
     def hand_out(group, cols, index, chunk, place_in_chunk):
         for k in range(4 * group, 4 * group + 4):
             rows = aligned(((unit ^ k) & 3) * slot, slot)
             target = outs[2 * chunk + (k & 1)].at[k >> 1, :, place_in_chunk]
-            sent.extend(start_copies([(buf.at[group, rows, cols], target)], out_sems, 5 * k + index))
+            sent.extend(start_copies([(buf.at[group, rows, cols], target)], out_sems, 3 * k + index))
 
     for group in range(units // BLOCKS):
-        sources = slice(group * 4, group * 4 + 4)
-        if group == 0:
-            for copy in copies:
-                copy.wait()
+        members = range(4 * group, 4 * group + 4)
+        for k in members:
+            s = (unit ^ k) & 3
+            value = None
+            for r in range(4):
+                term = dot(features(r, 0, size), weight(k, r, slice(0, size)))
+                value = term if value is None else value + term
+            buf[group, :, aligned(s * own, own)] = value.astype(BF16)
+        hand_out(group, slice(0, 2 * own), 0, 0, slice(0, 2 * own))
+        hand_out(group, slice(2 * own, 4 * own), 1, 1, slice(0, 2 * own))
         value = None
-        for q in range(4):
+        for r in range(4):
             for e in range(size // width):
-                at = q * size + e * width
-                first = size + e * part
-                middle, last = first + part // 2, first + part
-                w = jnp.concatenate(
-                    [
-                        weight[q, sources, first:middle, :width].reshape(2 * part, width),
-                        weight[q, sources, middle:last, :width].reshape(2 * part, width),
-                    ],
-                    axis=0,
-                )
-                term = dot(tokens[:, at : at + width], w, NT)
+                pieces = []
+                for half in range(2):
+                    first = size + e * part + half * (part // 2)
+                    rows, lanes = slice(first, first + part // 2), slice(0, width)
+                    for s in range(4):
+                        k = 4 * group + ((unit & 3) ^ s)
+                        piece = weights[r][jnp.maximum(k - 1, 0), rows, lanes]
+                        if group == 0:
+                            piece = jnp.where(k == 0, own_pieces[r][rows, lanes], piece)
+                        pieces.append(piece)
+                w = jnp.concatenate(pieces, axis=0)
+                term = dot(features(r, e * width, width), w, NT)
                 value = term if value is None else value + term
+        buf[group, :, 4 * own :] = value.astype(BF16)
         cols = slice(4 * own, 4 * own + 4 * part)
-        buf[group, :, cols] = value.astype(BF16)
-        hand_out(group, cols, 4, 0, slice(2 * own, 2 * own + 4 * part))
-        for s in range(4):
-            value = None
-            for q in range(4):
-                term = dot(tokens[:, q * size : (q + 1) * size], weight[q, group * 4 + s, :size])
-                value = term if value is None else value + term
-            cols = slice(s * own, (s + 1) * own)
-            buf[group, :, cols] = value.astype(BF16)
-            hand_out(group, cols, s, s >> 1, slice((s & 1) * own, ((s & 1) + 1) * own))
+        hand_out(group, cols, 2, 0, slice(2 * own, 2 * own + 4 * part))
     for copy in sent:
         copy.wait()
 
@@ -445,19 +430,15 @@
     groups = units // BLOCKS
     outs = pl.pallas_call(
         functools.partial(project_kernel, units),
-        in_specs=[in_smem()] + [anywhere()] * 9,
+        in_specs=[in_smem()] + [in_vmem()] * 9,
         out_specs=[anywhere()] * 4,
         out_shape=[jax.ShapeDtypeStruct((units // 2, slot, 2 * own + 4 * part), BF16)] * 2
         + [jax.ShapeDtypeStruct((units // 2, slot, 2 * own), BF16)] * 2,
         scratch_shapes=[
-            pltpu.VMEM((4, units, rows, own), BF16),
-            pltpu.VMEM((tokens, wide), BF16),
             pltpu.VMEM((groups, tokens, 4 * own + 4 * part), BF16),
-            pltpu.SemaphoreType.DMA((1,)),
-            pltpu.SemaphoreType.DMA((4 * units,)),
-            pltpu.SemaphoreType.DMA((5 * units,)),
-        ],
-        compiler_params=pltpu.CompilerParams(vmem_limit_bytes=ALL),
+            pltpu.SemaphoreType.DMA((3 * units,)),
+        ],
+        compiler_params=pltpu.CompilerParams(vmem_limit_bytes=VMEM),
         name="project",
     )(place, normed, *own_pieces, *weights)
     return outs
@@ -488,8 +469,8 @@
     return value.astype(BF16).astype(F32)
 
 
-def key_value_kernel(cosine, sine, *refs):
-    parts, out = refs[:-1], refs[-1]
+def key_value_kernel(count, cosine, sine, *refs):
+    parts, out = refs[:count], refs[-1]
     wide = parts[0].shape[2]
     value = all_parts(parts, slice(wide - out.shape[1], wide))
     keys, values = value[:, :HD], value[:, HD:]
@@ -501,15 +482,15 @@
     out[:, HD:] = values.astype(BF16)
 
 
-def key_value(parts, cosine, sine):
-    return pl.pallas_call(
-        key_value_kernel,
-        in_specs=[in_vmem()] * (2 + len(parts)),
+def key_value(parts, cosine, sine, after):
+    return pl.pallas_call(
+        functools.partial(key_value_kernel, len(parts)),
+        in_specs=[in_vmem()] * (2 + len(parts)) + [anywhere()] * len(after),
         out_specs=in_vmem(),
         out_shape=jax.ShapeDtypeStruct((parts[0].shape[1], parts[0].shape[2] // 3), BF16),
         compiler_params=pltpu.CompilerParams(vmem_limit_bytes=VMEM),
         name="key_value",
-    )(cosine, sine, *parts)
+    )(cosine, sine, *parts, *after)
 
 
 def query_kernel(count, cosine, sine, *refs):
@@ -703,18 +684,8 @@
     place = jnp.stack([jnp.asarray(v, jnp.int32) for v in (group, unit, side, quarter, kv_head)])
 
     keep, send, pos = deal(place, row_lengths, row_dest, home, rows, slot)
-    pieces, o_pieces = weight_pieces(
-        place,
-        q_values,
-        q_scales,
-        k_values,
-        k_scales,
-        v_values,
-        v_scales,
-        o_values,
-        o_scales,
-        ranks,
-        [keep],
+    pieces = weight_pieces(
+        place, q_values, q_scales, k_values, k_scales, v_values, v_scales, units, [keep]
     )
     own_gain = lax.dynamic_slice_in_dim(
         gain.astype(F32), unit * 2 * features, 2 * features
@@ -731,6 +702,7 @@
     wide_sin = jnp.concatenate([-sine, sine], axis=1)
 
     got = swap(send, "dp")
+    o_pieces = output_pieces(place, o_values, o_scales, ranks, [got])
     keep2 = swap(keep, "tensor")
     got2 = lax.ppermute(
         send, ("dp", "tensor"), [(i, i ^ (ranks + 1)) for i in range(2 * ranks)]
@@ -740,7 +712,7 @@
     collected, squares = collect(
         [keep, got, keep2, got2],
         pieces,
-        [own_gain, own_cos, own_sin, wide_cos, wide_sin, *own_pieces[1:]],
+        [own_gain, own_cos, own_sin, wide_cos, wide_sin, o_pieces, *own_pieces[1:]],
     )
 
     squares = over_units([squares] * units)
@@ -754,13 +726,14 @@
     weights.append(swap(weights[2], "dp"))
     kept_a, near_a, kept_b, near_b = project(place, normed, own_pieces, weights, units)
     (o_moved,) = gate([o_moved], [kept_a])
+    got_a = swap(near_a, "tensor", 2)
+    (near_b,) = gate([near_b], [got_a])
     parts = []
-    for kept, near in ((kept_a, near_a), (kept_b, near_b)):
-        got = swap(near, "tensor", 2)
-        sums = pair_sums(kept, got)
+    for kept, got in ((kept_a, got_a), (kept_b, swap(near_b, "tensor", 2))):
+        sums = list(pair_sums(kept, got))
         far = [swap(value, "tensor", 4 * (i + 1)) for i, value in enumerate(sums)]
         parts.append([kept, got, *far])
-    own_kv = key_value(parts[0], own_cos, own_sin)
+    own_kv = key_value(parts[0], own_cos, own_sin, sums[:1])
     other_kv = swap(own_kv, "tensor")
     o_weights = [
         value.reshape(units, 2, *value.shape[1:]) for value in all_quarters(o_moved)

time: 188 us -> 186 us (0.989)
  starting transfers between devices: 53.7 us -> 59.6 us
  local copies, waits for them, and re-layouts: 15.9 us -> 12 us
  waiting for transfers between devices: 77.4 us -> 74.7 us
    ppermute x36, waiting for transfers between devices: 76 us -> 67.1 us  [swap(): return lax.ppermute(value, axis, [(i, i ^ mask) for i in range(size)])]
    all_to_all x1, waiting for transfers between devices: 1.49 us -> 7.62 us  [body(): lax.all_to_all(o_pieces, 'tensor', split_axis=0, concat_axis=0, tiled=True)]
    ppermute x36, starting transfers between devices: 48.6 us -> 53.2 us  [swap(): return lax.ppermute(value, axis, [(i, i ^ mask) for i in range(size)])]
    unnamed x60 -> x64, local copies, waits for them, and re-layouts: 15 us -> 11.1 us
    pallas_call x1 -> x2, Pallas kernels: 0.13 us -> 3.41 us  [the longest x1 3.28 us: output_pieces(): pl.pallas_call(functools.partial(o_pieces_kernel, len(after)), in_specs=[...]
    ppermute x1, starting transfers between devices: 0.68 us -> 2.62 us  [body(): lax.ppermute(send, ('dp', 'tensor'), [(i, i ^ ranks + 1) for i in range(2...]
  transfers between devices with their start and end apart: 38 -> 38, of which waited for: 20 -> 18; matrix products, arithmetic and copies ran while one was open for 2% -> 1% of each run, Pallas kernels for 8% -> 11%
where the time goes in v4:
time: 186 us; the launch traced here: 185 us
  waiting for transfers between devices  74.7 us (40%)
  starting transfers between devices  59.6 us (32%)
  Pallas kernels  36.5 us (20%)
  local copies, waits for them, and re-layouts  12 us (6%)
    ppermute x36, waiting for transfers between devices, swap(): return lax.ppermute(value, axis, [(i, i ^ mask) for i in range(size)])  67.1 us
    ppermute x36, starting transfers between devices, swap(): return lax.ppermute(value, axis, [(i, i ^ mask) for i in range(size)])  53.2 us
    unnamed x64, local copies, waits for them, and re-layouts  11.1 us
    pallas_call x1, Pallas kernels, project(): pl.pallas_call(functools.partial(project_kernel, units), in_specs=[in_sme...  8.25 us
    all_to_all x1, waiting for transfers between devices, body(): lax.all_to_all(o_pieces, 'tensor', split_axis=0, concat_axis=0, tiled=True)  7.62 us
    pallas_call x1, Pallas kernels, output(): pl.pallas_call(functools.partial(output_kernel, units, rows, slot), in_sp...  7.5 us
    pallas_call x1, Pallas kernels, deal(): pl.pallas_call(functools.partial(deal_kernel, rows, slot), grid=(features...  6.14 us
    all_to_all x1, starting transfers between devices, body(): lax.all_to_all(o_pieces, 'tensor', split_axis=0, concat_axis=0, tiled=True)  3.74 us
  transfers between devices with their start and end apart: 38, of which 18 were waited for; matrix products, arithmetic and copies ran while one was open for 1% of the time, Pallas kernels for 11%

profile of v4, /device:TPU:0, one launch (start us, length us, event | category | flops | bytes accessed | tf_op | source)
XLA Modules:
  0.0 184.9 jit_solution(7529840711047123842)
XLA Ops:
  0.7 6.1 %deal.1 = (bf16[384,1024]{1,0:T(8,128)(2,1)}, bf16[384,1024]{1,0:T(8,128)(2,1)}, f32[192,128]{1,0:T(8,128)}) custom-call(s32[5]{0:T(128)} %stack.23.place, s32[16]{0:T(128)} %lens.7, s32[16]{0:T(128)} %dest.7, bf16[1024,1536]{1,0:T(8,128)(2,1)} %home.1), custom_call_target="tpu_custom_call" | custom-call | tf_op jit(solution)/shard_map/deal/pallas_call | solution.py:230
  7.3 2.6 %collective-permute-start.2 = (bf16[384,1024]{1,0:T(8,128)(2,1)}, bf16[384,1024]{1,0:T(8,128)(2,1)S(1)}, u32[]{:S(2)}, u32[]{:S(2)}) collective-permute-start(bf16[384,1024]{1,0:T(8,128)(2,1)} %get-tuple-element.18), channel_id=1, source_target_pairs={{0,9},{1,8},{2,11},{3,10},{4,13},{5,12},{6,15},{7,14},{8,1},{9,0},... | collective-permute-start | bytes 2359304 | tf_op jit(solution)/shard_map/ppermute | solution.py:707
  10.0 3.0 %weight_pieces.1 = (bf16[640,256]{1,0:T(8,128)(2,1)}, bf16[640,256]{1,0:T(8,128)(2,1)}, bf16[640,256]{1,0:T(8,128)(2,1)}, bf16[640,256]{1,0:T(8,128)(2,1)}) custom-call(s32[5]{0:T(128)} %stack.23.place, f32[2,64]{1,0:T(2,128)} %bitcast.17, f32[2,64]{1,0:T(2,128)} %ks.1, f32[2,64]{1,0:T(2,128)} %vs.1, bf16[8192,256]{1,0:T(8,128)(2,1)} %q_hbm.1, ...), custom_call_target="tpu_custom_call" | custom-call | tf_op jit(solution)/shard_map/weight_pieces/pallas_call | solution.py:138
  15.0 2.6 %collective-permute-start.4 = (bf16[640,256]{1,0:T(8,128)(2,1)}, bf16[640,256]{1,0:T(8,128)(2,1)S(1)}, u32[]{:S(2)}, u32[]{:S(2)}) collective-permute-start(bf16[640,256]{1,0:T(8,128)(2,1)} %get-tuple-element.21), channel_id=1, source_target_pairs={{0,4},{1,5},{2,6},{3,7},{4,0},{5,1},{6,2},{7,3},{8,12},{9,13},{10,... | collective-permute-start | bytes 983048 | tf_op jit(solution)/shard_map/ppermute | solution.py:648
  18.4 11.4 %collective-permute-done.3.refs_4_ = bf16[640,256]{1,0:T(8,128)(2,1)S(1)} collective-permute-done((bf16[640,256]{1,0:T(8,128)(2,1)}, bf16[640,256]{1,0:T(8,128)(2,1)S(1)}, u32[]{:S(2)}, u32[]{:S(2)}) %collective-permute-start.3) | collective-permute-done | bytes 327712 | tf_op jit(solution)/shard_map/ppermute | solution.py:648
  36.7 3.3 %output_pieces.1.refs_12_.refs_0_ = bf16[8,64,1024]{2,1,0:T(8,128)(2,1)} custom-call(s32[5]{0:T(128)} %stack.23.place, f32[2,64]{1,0:T(2,128)} %scales.1, bf16[256,8192]{1,0:T(8,128)(2,1)} %o_hbm.1, bf16[384,1024]{1,0:T(8,128)(2,1)} %copy-done.3), custom_call_target="tpu_custom_call" | custom-call | tf_op jit(solution)/shard_map/output_pieces/pallas_call | solution.py:173
  40.0 5.4 %collective-permute-done.5.refs_6_ = bf16[640,256]{1,0:T(8,128)(2,1)} collective-permute-done((bf16[640,256]{1,0:T(8,128)(2,1)}, bf16[640,256]{1,0:T(8,128)(2,1)}, u32[]{:S(2)}, u32[]{:S(2)}) %collective-permute-start.5) | collective-permute-done | bytes 327712 | tf_op jit(solution)/shard_map/ppermute | solution.py:648
  54.0 3.3 %collective-permute-start.10 = (f32[8,768]{1,0:T(8,128)S(1)}, f32[8,768]{1,0:T(8,128)S(1)}, u32[]{:S(2)}, u32[]{:S(2)}) collective-permute-start(f32[8,768]{1,0:T(8,128)S(1)} %get-tuple-element.25.rest_0_), channel_id=1, source_target_pairs={{0,6},{1,7},{2,4},{3,5},{4,2},{5,3},{6,0},{7,1},{8,14},{9,15},{10,... | collective-permute-start | bytes 73736 | tf_op jit(solution)/shard_map/ppermute | solution.py:648
  57.3 3.7 %collective-permute-start.9 = (f32[8,768]{1,0:T(8,128)S(1)}, f32[8,768]{1,0:T(8,128)S(1)}, u32[]{:S(2)}, u32[]{:S(2)}) collective-permute-start(f32[8,768]{1,0:T(8,128)S(1)} %get-tuple-element.25.rest_0_), channel_id=1, source_target_pairs={{0,4},{1,5},{2,6},{3,7},{4,0},{5,1},{6,2},{7,3},{8,12},{9,13},{10,... | collective-permute-start | bytes 73736 | tf_op jit(solution)/shard_map/ppermute | solution.py:648
  65.9 3.7 %all-to-all-start = ((bf16[8,64,1024]{2,1,0:T(8,128)(2,1)}), bf16[8,64,1024]{2,1,0:T(8,128)(2,1)S(1)}, u32[]{:S(2)}, u32[]{:S(2)}) async-start(bf16[8,64,1024]{2,1,0:T(8,128)(2,1)} %copy-done.1), calls=%async_computation | async-start | bytes 2097152 | tf_op jit(solution)/shard_map/all_to_all | solution.py:722
  78.9 8.2 %project.1 = (bf16[2,192,768]{2,1,0:T(8,128)(2,1)S(1)}, bf16[2,192,768]{2,1,0:T(8,128)(2,1)S(1)}, bf16[2,192,512]{2,1,0:T(8,128)(2,1)S(1)}, bf16[2,192,512]{2,1,0:T(8,128)(2,1)S(1)}) custom-call(s32[5]{0:T(128)S(1)} %copy-done.26, bf16[768,2048]{1,0:T(8,128)(2,1)S(1)} %normalize.1.refs_3_.tokens, bf16[640,256]{1,0:T(8,128)(2,1)S(1)} %copy-done.16, ...), custom_call_target="tpu_custom_call" | custom-call | tf_op jit(solution)/shard_map/project/pallas_call | solution.py:431
  87.2 7.6 %all-to-all-done.refs_0_ = bf16[8,64,1024]{2,1,0:T(8,128)(2,1)S(1)} async-done(((bf16[8,64,1024]{2,1,0:T(8,128)(2,1)}), bf16[8,64,1024]{2,1,0:T(8,128)(2,1)S(1)}, u32[]{:S(2)}, u32[]{:S(2)}) %all-to-all-start) | async-done | bytes 1048608 | tf_op jit(solution)/shard_map/all_to_all | solution.py:722
  95.5 12.8 %collective-permute-done.18.got.refs_1_ = bf16[2,192,768]{2,1,0:T(8,128)(2,1)S(1)} collective-permute-done((bf16[2,192,768]{2,1,0:T(8,128)(2,1)S(1)}, bf16[2,192,768]{2,1,0:T(8,128)(2,1)S(1)}, u32[]{:S(2)}, u32[]{:S(2)}) %collective-permute-start.18) | collective-permute-done | bytes 589856 | tf_op jit(solution)/shard_map/ppermute | solution.py:648
  111.9 5.9 %collective-permute-done.16 = bf16[8,64,1024]{2,1,0:T(8,128)(2,1)S(1)} collective-permute-done((bf16[8,64,1024]{2,1,0:T(8,128)(2,1)S(1)}, bf16[8,64,1024]{2,1,0:T(8,128)(2,1)S(1)}, u32[]{:S(2)}, u32[]{:S(2)}) %collective-permute-start.16) | collective-permute-done | bytes 1048608 | tf_op jit(solution)/shard_map/ppermute | solution.py:648
  117.8 5.1 %collective-permute-done.20.got.refs_1_ = bf16[2,192,512]{2,1,0:T(8,128)(2,1)S(1)} collective-permute-done((bf16[2,192,512]{2,1,0:T(8,128)(2,1)S(1)}, bf16[2,192,512]{2,1,0:T(8,128)(2,1)S(1)}, u32[]{:S(2)}, u32[]{:S(2)}) %collective-permute-start.20) | collective-permute-done | bytes 393248 | tf_op jit(solution)/shard_map/ppermute | solution.py:648
  125.2 2.7 %collective-permute-start.21 = (bf16[192,256]{1,0:T(8,128)(2,1)S(1)}, bf16[192,256]{1,0:T(8,128)(2,1)S(1)}, u32[]{:S(2)}, u32[]{:S(2)}) collective-permute-start(bf16[192,256]{1,0:T(8,128)(2,1)S(1)} %key_value.1.own_kv), channel_id=1, source_target_pairs={{0,1},{1,0},{2,3},{3,2},{4,5},{5,4},{6,7},{7,6},{8,9},{9,8},{10,11... | collective-permute-start | bytes 294920 | tf_op jit(solution)/shard_map/ppermute | solution.py:648
  141.8 3.5 %collective-permute-start.31 = (bf16[192,512]{1,0:T(8,128)(2,1)S(1)}, bf16[192,512]{1,0:T(8,128)(2,1)S(1)}, u32[]{:S(2)}, u32[]{:S(2)}) collective-permute-start(bf16[192,512]{1,0:T(8,128)(2,1)S(1)} %attend.3.refs_12_), channel_id=1, source_target_pairs={{0,4},{1,5},{2,6},{3,7},{4,0},{5,1},{6,2},{7,3},{8,12},{9,13},{10,... | collective-permute-start | bytes 589832 | tf_op jit(solution)/shard_map/ppermute | solution.py:648
  147.9 3.9 %collective-permute-done.31.refs_0_ = bf16[192,512]{1,0:T(8,128)(2,1)S(1)} collective-permute-done((bf16[192,512]{1,0:T(8,128)(2,1)S(1)}, bf16[192,512]{1,0:T(8,128)(2,1)S(1)}, u32[]{:S(2)}, u32[]{:S(2)}) %collective-permute-start.31) | collective-permute-done | bytes 196640 | tf_op jit(solution)/shard_map/ppermute | solution.py:648
  157.8 5.7 %collective-permute-start.28 = (bf16[192,512]{1,0:T(8,128)(2,1)S(1)}, bf16[192,512]{1,0:T(8,128)(2,1)S(1)}, u32[]{:S(2)}, u32[]{:S(2)}) collective-permute-start(bf16[192,512]{1,0:T(8,128)(2,1)S(1)} %collective-permute-done.25.refs_7_), channel_id=1, source_target_pairs={{0,1},{1,0},{2,3},{3,2},{4,5},{5,4},{6,7},{7,6},{8,9},{9,8},{10,11... | collective-permute-start | bytes 589832 | tf_op jit(solution)/shard_map/ppermute | solution.py:648
  163.6 2.7 %collective-permute-start.36 = (bf16[192,512]{1,0:T(8,128)(2,1)S(1)}, bf16[192,512]{1,0:T(8,128)(2,1)S(1)}, u32[]{:S(2)}, u32[]{:S(2)}) collective-permute-start(bf16[192,512]{1,0:T(8,128)(2,1)S(1)} %collective-permute-done.33.refs_15_), channel_id=1, source_target_pairs={{0,1},{1,0},{2,3},{3,2},{4,5},{5,4},{6,7},{7,6},{8,9},{9,8},{10,11... | collective-permute-start | bytes 589832 | tf_op jit(solution)/shard_map/ppermute | solution.py:648
  166.3 3.7 %collective-permute-done.28.refs_11_ = bf16[192,512]{1,0:T(8,128)(2,1)S(1)} collective-permute-done((bf16[192,512]{1,0:T(8,128)(2,1)S(1)}, bf16[192,512]{1,0:T(8,128)(2,1)S(1)}, u32[]{:S(2)}, u32[]{:S(2)}) %collective-permute-start.28) | collective-permute-done | bytes 196640 | tf_op jit(solution)/shard_map/ppermute | solution.py:648
  170.0 4.2 %collective-permute-done.34.refs_17_ = bf16[192,512]{1,0:T(8,128)(2,1)S(1)} collective-permute-done((bf16[192,512]{1,0:T(8,128)(2,1)S(1)}, bf16[192,512]{1,0:T(8,128)(2,1)S(1)}, u32[]{:S(2)}, u32[]{:S(2)}) %collective-permute-start.34) | collective-permute-done | bytes 196640 | tf_op jit(solution)/shard_map/ppermute | solution.py:648
  174.2 3.0 %collective-permute-done.36.refs_19_ = bf16[192,512]{1,0:T(8,128)(2,1)S(1)} collective-permute-done((bf16[192,512]{1,0:T(8,128)(2,1)S(1)}, bf16[192,512]{1,0:T(8,128)(2,1)S(1)}, u32[]{:S(2)}, u32[]{:S(2)}) %collective-permute-start.36) | collective-permute-done | bytes 196640 | tf_op jit(solution)/shard_map/ppermute | solution.py:648
  177.2 7.5 %output.1 = bf16[1024,768]{1,0:T(8,128)(2,1)} custom-call(s32[5]{0:T(128)S(1)} %copy-done.26, s32[16]{0:T(128)S(1)} %copy-done.29, s32[16]{0:T(128)S(1)} %copy-done.30, bf16[4,2,64,1024]{3,2,1,0:T(8,128)(2,1)S(1)} %bitcast.11, bf16[4,2,64,1024]{3,2,1,0:T(8,128)(2,1)S(1)} %bitcast.13, bf16[4,2,64,1024]{3,2,1,0:T(8,128)(2,1)S(1)} %bitcast.12, ...), custom_call_target="tpu_custom_call" | custom-call | tf_op jit(solution)/shard_map/output/pallas_call | solution.py:627
  (145 shorter events, 62.5 us)
Async XLA Ops:
  6.8 26.2 %collective-permute-start = (bf16[384,1024]{1,0:T(8,128)(2,1)}, bf16[384,1024]{1,0:T(8,128)(2,1)S(1)}, u32[]{:S(2)}, u32[]{:S(2)}) collective-permute-start(bf16[384,1024]{1,0:T(8,128)(2,1)} %get-tuple-element.18), channel_id=1, source_target_pairs={{0,8},{8,0},{1,9},{9,1},{2,10},{10,2},{3,11},{11,3},{4,12},{12,4},... | collective-permute-start | bytes 2359304 | tf_op jit(solution)/shard_map/ppermute | solution.py:648
  7.3 38.1 %collective-permute-start.2 = (bf16[384,1024]{1,0:T(8,128)(2,1)}, bf16[384,1024]{1,0:T(8,128)(2,1)S(1)}, u32[]{:S(2)}, u32[]{:S(2)}) collective-permute-start(bf16[384,1024]{1,0:T(8,128)(2,1)} %get-tuple-element.18), channel_id=1, source_target_pairs={{0,9},{1,8},{2,11},{3,10},{4,13},{5,12},{6,15},{7,14},{8,1},{9,0},... | collective-permute-start | bytes 2359304 | tf_op jit(solution)/shard_map/ppermute | solution.py:707
  9.9 35.5 %collective-permute-start.1 = (bf16[384,1024]{1,0:T(8,128)(2,1)}, bf16[384,1024]{1,0:T(8,128)(2,1)S(1)}, u32[]{:S(2)}, u32[]{:S(2)}) collective-permute-start(bf16[384,1024]{1,0:T(8,128)(2,1)} %get-tuple-element.19.rest_0_.refs_0_.rest_5_), channel_id=1, source_target_pairs={{0,1},{1,0},{2,3},{3,2},{4,5},{5,4},{6,7},{7,6},{8,9},{9,8},{10,11... | collective-permute-start | bytes 2359304 | tf_op jit(solution)/shard_map/ppermute | solution.py:648
  12.9 16.9 %collective-permute-start.3 = (bf16[640,256]{1,0:T(8,128)(2,1)}, bf16[640,256]{1,0:T(8,128)(2,1)S(1)}, u32[]{:S(2)}, u32[]{:S(2)}) collective-permute-start(bf16[640,256]{1,0:T(8,128)(2,1)} %get-tuple-element.20), channel_id=1, source_target_pairs={{0,2},{1,3},{2,0},{3,1},{4,6},{5,7},{6,4},{7,5},{8,10},{9,11},{10,... | collective-permute-start | bytes 983048 | tf_op jit(solution)/shard_map/ppermute | solution.py:648
  15.0 17.3 %collective-permute-start.4 = (bf16[640,256]{1,0:T(8,128)(2,1)}, bf16[640,256]{1,0:T(8,128)(2,1)S(1)}, u32[]{:S(2)}, u32[]{:S(2)}) collective-permute-start(bf16[640,256]{1,0:T(8,128)(2,1)} %get-tuple-element.21), channel_id=1, source_target_pairs={{0,4},{1,5},{2,6},{3,7},{4,0},{5,1},{6,2},{7,3},{8,12},{9,13},{10,... | collective-permute-start | bytes 983048 | tf_op jit(solution)/shard_map/ppermute | solution.py:648
  30.6 14.8 %collective-permute-start.7 = (bf16[640,256]{1,0:T(8,128)(2,1)}, bf16[640,256]{1,0:T(8,128)(2,1)S(1)}, u32[]{:S(2)}, u32[]{:S(2)}) collective-permute-start(bf16[640,256]{1,0:T(8,128)(2,1)} %get-tuple-element.24.rest_0_), channel_id=1, source_target_pairs={{0,16},{16,0},{1,17},{17,1},{2,18},{18,2},{3,19},{19,3},{4,20},{20... | collective-permute-start | bytes 983048 | tf_op jit(solution)/shard_map/ppermute | solution.py:648
  33.1 12.4 %collective-permute-start.6 = (bf16[640,256]{1,0:T(8,128)(2,1)}, bf16[640,256]{1,0:T(8,128)(2,1)}, u32[]{:S(2)}, u32[]{:S(2)}) collective-permute-start(bf16[640,256]{1,0:T(8,128)(2,1)} %get-tuple-element.24.rest_0_), channel_id=1, source_target_pairs={{0,8},{8,0},{1,9},{9,1},{2,10},{10,2},{3,11},{11,3},{4,12},{12,4},... | collective-permute-start | bytes 983048 | tf_op jit(solution)/shard_map/ppermute | solution.py:648
  33.1 12.3 %collective-permute-start.5 = (bf16[640,256]{1,0:T(8,128)(2,1)}, bf16[640,256]{1,0:T(8,128)(2,1)}, u32[]{:S(2)}, u32[]{:S(2)}) collective-permute-start(bf16[640,256]{1,0:T(8,128)(2,1)} %get-tuple-element.22), channel_id=1, source_target_pairs={{0,6},{1,7},{2,4},{3,5},{4,2},{5,3},{6,0},{7,1},{8,14},{9,15},{10,... | collective-permute-start | bytes 983048 | tf_op jit(solution)/shard_map/ppermute | solution.py:648
  52.5 23.6 %collective-permute-start.13 = (bf16[3,640,256]{2,1,0:T(8,128)(2,1)}, bf16[3,640,256]{2,1,0:T(8,128)(2,1)}, u32[]{:S(2)}, u32[]{:S(2)}) collective-permute-start(bf16[3,640,256]{2,1,0:T(8,128)(2,1)} %get-tuple-element.26.rest_4_), channel_id=1, source_target_pairs={{0,16},{16,0},{1,17},{17,1},{2,18},{18,2},{3,19},{19,3},{4,20},{20... | collective-permute-start | bytes 2949128 | tf_op jit(solution)/shard_map/ppermute | solution.py:648
  54.0 22.1 %collective-permute-start.12 = (bf16[3,640,256]{2,1,0:T(8,128)(2,1)}, bf16[3,640,256]{2,1,0:T(8,128)(2,1)}, u32[]{:S(2)}, u32[]{:S(2)}) collective-permute-start(bf16[3,640,256]{2,1,0:T(8,128)(2,1)} %get-tuple-element.26.rest_4_), channel_id=1, source_target_pairs={{0,8},{8,0},{1,9},{9,1},{2,10},{10,2},{3,11},{11,3},{4,12},{12,4},... | collective-permute-start | bytes 2949128 | tf_op jit(solution)/shard_map/ppermute | solution.py:648
  65.9 28.9 %all-to-all-start = ((bf16[8,64,1024]{2,1,0:T(8,128)(2,1)}), bf16[8,64,1024]{2,1,0:T(8,128)(2,1)S(1)}, u32[]{:S(2)}, u32[]{:S(2)}) async-start(bf16[8,64,1024]{2,1,0:T(8,128)(2,1)} %copy-done.1), calls=%async_computation | async-start | bytes 2097152 | tf_op jit(solution)/shard_map/all_to_all | solution.py:722
  94.8 23.0 %collective-permute-start.16 = (bf16[8,64,1024]{2,1,0:T(8,128)(2,1)S(1)}, bf16[8,64,1024]{2,1,0:T(8,128)(2,1)S(1)}, u32[]{:S(2)}, u32[]{:S(2)}) collective-permute-start(bf16[8,64,1024]{2,1,0:T(8,128)(2,1)S(1)} %gate.8), channel_id=1, source_target_pairs={{0,16},{16,0},{1,17},{17,1},{2,18},{18,2},{3,19},{19,3},{4,20},{20... | collective-permute-start | bytes 3145736 | tf_op jit(solution)/shard_map/ppermute | solution.py:648
  95.5 12.8 %collective-permute-start.18 = (bf16[2,192,768]{2,1,0:T(8,128)(2,1)S(1)}, bf16[2,192,768]{2,1,0:T(8,128)(2,1)S(1)}, u32[]{:S(2)}, u32[]{:S(2)}) collective-permute-start(bf16[2,192,768]{2,1,0:T(8,128)(2,1)S(1)} %get-tuple-element.28), channel_id=1, source_target_pairs={{0,2},{1,3},{2,0},{3,1},{4,6},{5,7},{6,4},{7,5},{8,10},{9,11},{10,... | collective-permute-start | bytes 1769480 | tf_op jit(solution)/shard_map/ppermute | solution.py:648
  95.5 60.3 %collective-permute-start.15 = (bf16[8,64,1024]{2,1,0:T(8,128)(2,1)S(1)}, bf16[8,64,1024]{2,1,0:T(8,128)(2,1)S(1)}, u32[]{:S(2)}, u32[]{:S(2)}) collective-permute-start(bf16[8,64,1024]{2,1,0:T(8,128)(2,1)S(1)} %gate.8), channel_id=1, source_target_pairs={{0,8},{8,0},{1,9},{9,1},{2,10},{10,2},{3,11},{11,3},{4,12},{12,4},... | collective-permute-start | bytes 3145736 | tf_op jit(solution)/shard_map/ppermute | solution.py:648
  108.2 14.7 %collective-permute-start.20 = (bf16[2,192,512]{2,1,0:T(8,128)(2,1)S(1)}, bf16[2,192,512]{2,1,0:T(8,128)(2,1)S(1)}, u32[]{:S(2)}, u32[]{:S(2)}) collective-permute-start(bf16[2,192,512]{2,1,0:T(8,128)(2,1)S(1)} %gate.9), channel_id=1, source_target_pairs={{0,2},{1,3},{2,0},{3,1},{4,6},{5,7},{6,4},{7,5},{8,10},{9,11},{10,... | collective-permute-start | bytes 1179656 | tf_op jit(solution)/shard_map/ppermute | solution.py:648
  109.5 15.5 %collective-permute-start.19 = (bf16[192,768]{1,0:T(8,128)(2,1)S(1)}, bf16[192,768]{1,0:T(8,128)(2,1)S(1)}, u32[]{:S(2)}, u32[]{:S(2)}) collective-permute-start(bf16[192,768]{1,0:T(8,128)(2,1)S(1)} %pair_sums.2), channel_id=1, source_target_pairs={{0,4},{1,5},{2,6},{3,7},{4,0},{5,1},{6,2},{7,3},{8,12},{9,13},{10,... | collective-permute-start | bytes 884744 | tf_op jit(solution)/shard_map/ppermute | solution.py:648
  117.8 59.4 %collective-permute-start.17 = (bf16[8,64,1024]{2,1,0:T(8,128)(2,1)S(1)}, bf16[8,64,1024]{2,1,0:T(8,128)(2,1)S(1)}, u32[]{:S(2)}, u32[]{:S(2)}) collective-permute-start(bf16[8,64,1024]{2,1,0:T(8,128)(2,1)S(1)} %collective-permute-done.16), channel_id=1, source_target_pairs={{0,8},{8,0},{1,9},{9,1},{2,10},{10,2},{3,11},{11,3},{4,12},{12,4},... | collective-permute-start | bytes 3145736 | tf_op jit(solution)/shard_map/ppermute | solution.py:648
  123.0 12.6 %collective-permute-start.29 = (bf16[192,512]{1,0:T(8,128)(2,1)S(1)}, bf16[192,512]{1,0:T(8,128)(2,1)S(1)}, u32[]{:S(2)}, u32[]{:S(2)}) collective-permute-start(bf16[192,512]{1,0:T(8,128)(2,1)S(1)} %pair_sums.3.refs_3_), channel_id=1, source_target_pairs={{0,4},{1,5},{2,6},{3,7},{4,0},{5,1},{6,2},{7,3},{8,12},{9,13},{10,... | collective-permute-start | bytes 589832 | tf_op jit(solution)/shard_map/ppermute | solution.py:648
  141.8 10.0 %collective-permute-start.31 = (bf16[192,512]{1,0:T(8,128)(2,1)S(1)}, bf16[192,512]{1,0:T(8,128)(2,1)S(1)}, u32[]{:S(2)}, u32[]{:S(2)}) collective-permute-start(bf16[192,512]{1,0:T(8,128)(2,1)S(1)} %attend.3.refs_12_), channel_id=1, source_target_pairs={{0,4},{1,5},{2,6},{3,7},{4,0},{5,1},{6,2},{7,3},{8,12},{9,13},{10,... | collective-permute-start | bytes 589832 | tf_op jit(solution)/shard_map/ppermute | solution.py:648
  145.6 12.1 %collective-permute-start.27 = (bf16[192,512]{1,0:T(8,128)(2,1)S(1)}, bf16[192,512]{1,0:T(8,128)(2,1)S(1)}, u32[]{:S(2)}, u32[]{:S(2)}) collective-permute-start(bf16[192,512]{1,0:T(8,128)(2,1)S(1)} %gate.10.refs_6_), channel_id=1, source_target_pairs={{0,1},{1,0},{2,3},{3,2},{4,5},{5,4},{6,7},{7,6},{8,9},{9,8},{10,11... | collective-permute-start | bytes 589832 | tf_op jit(solution)/shard_map/ppermute | solution.py:648
  157.7 12.3 %collective-permute-start.35 = (bf16[192,512]{1,0:T(8,128)(2,1)S(1)}, bf16[192,512]{1,0:T(8,128)(2,1)S(1)}, u32[]{:S(2)}, u32[]{:S(2)}) collective-permute-start(bf16[192,512]{1,0:T(8,128)(2,1)S(1)} %gate.11.refs_14_), channel_id=1, source_target_pairs={{0,1},{1,0},{2,3},{3,2},{4,5},{5,4},{6,7},{7,6},{8,9},{9,8},{10,11... | collective-permute-start | bytes 589832 | tf_op jit(solution)/shard_map/ppermute | solution.py:648
  157.8 12.2 %collective-permute-start.28 = (bf16[192,512]{1,0:T(8,128)(2,1)S(1)}, bf16[192,512]{1,0:T(8,128)(2,1)S(1)}, u32[]{:S(2)}, u32[]{:S(2)}) collective-permute-start(bf16[192,512]{1,0:T(8,128)(2,1)S(1)} %collective-permute-done.25.refs_7_), channel_id=1, source_target_pairs={{0,1},{1,0},{2,3},{3,2},{4,5},{5,4},{6,7},{7,6},{8,9},{9,8},{10,11... | collective-permute-start | bytes 589832 | tf_op jit(solution)/shard_map/ppermute | solution.py:648
  163.5 10.7 %collective-permute-start.34 = (bf16[192,512]{1,0:T(8,128)(2,1)S(1)}, bf16[192,512]{1,0:T(8,128)(2,1)S(1)}, u32[]{:S(2)}, u32[]{:S(2)}) collective-permute-start(bf16[192,512]{1,0:T(8,128)(2,1)S(1)} %collective-permute-done.30.refs_1_.refs_13_), channel_id=1, source_target_pairs={{0,1},{1,0},{2,3},{3,2},{4,5},{5,4},{6,7},{7,6},{8,9},{9,8},{10,11... | collective-permute-start | bytes 589832 | tf_op jit(solution)/shard_map/ppermute | solution.py:648
  163.6 13.6 %collective-permute-start.36 = (bf16[192,512]{1,0:T(8,128)(2,1)S(1)}, bf16[192,512]{1,0:T(8,128)(2,1)S(1)}, u32[]{:S(2)}, u32[]{:S(2)}) collective-permute-start(bf16[192,512]{1,0:T(8,128)(2,1)S(1)} %collective-permute-done.33.refs_15_), channel_id=1, source_target_pairs={{0,1},{1,0},{2,3},{3,2},{4,5},{5,4},{6,7},{7,6},{8,9},{9,8},{10,11... | collective-permute-start | bytes 589832 | tf_op jit(solution)/shard_map/ppermute | solution.py:648
  (46 other events, 392.5 us)

commit v5 on v4

--- a/solution.py
+++ b/solution.py
@@ -154,7 +154,8 @@
 
 
 def o_pieces_kernel(count, place, scales, o_hbm, *rest):
-    out, o_buf, pieces, sem, out_sem = rest[count:]
+    out, token, o_buf, pieces, sem, out_sem = rest[count:]
+    token[...] = jnp.zeros_like(token)
     ranks, rows, features = pieces.shape
     first = place[QUARTER] * rows
     (copy,) = start_copies([(o_hbm.at[aligned(first, rows)], o_buf)], sem)
@@ -173,8 +174,8 @@
     return pl.pallas_call(
         functools.partial(o_pieces_kernel, len(after)),
         in_specs=[in_smem()] * 2 + [in_hbm()] + [anywhere()] * len(after),
-        out_specs=anywhere(),
-        out_shape=jax.ShapeDtypeStruct(shape, BF16),
+        out_specs=[anywhere(), in_vmem()],
+        out_shape=[jax.ShapeDtypeStruct(shape, BF16), jax.ShapeDtypeStruct((8, 128), F32)],
         scratch_shapes=[
             pltpu.VMEM((shape[1], o_values.shape[1]), BF16),
             pltpu.VMEM(shape, BF16),
@@ -297,7 +298,7 @@
             pltpu.SemaphoreType.DMA((count,)),
             pltpu.SemaphoreType.DMA((count,)),
         ],
-        compiler_params=pltpu.CompilerParams(vmem_limit_bytes=VMEM),
+        compiler_params=pltpu.CompilerParams(vmem_limit_bytes=ALL),
         name="collect",
     )(*tokens, *pieces, *after)
 
@@ -702,7 +703,7 @@
     wide_sin = jnp.concatenate([-sine, sine], axis=1)
 
     got = swap(send, "dp")
-    o_pieces = output_pieces(place, o_values, o_scales, ranks, [got])
+    o_pieces, o_made = output_pieces(place, o_values, o_scales, ranks, [got])
     keep2 = swap(keep, "tensor")
     got2 = lax.ppermute(
         send, ("dp", "tensor"), [(i, i ^ (ranks + 1)) for i in range(2 * ranks)]
@@ -712,7 +713,7 @@
     collected, squares = collect(
         [keep, got, keep2, got2],
         pieces,
-        [own_gain, own_cos, own_sin, wide_cos, wide_sin, o_pieces, *own_pieces[1:]],
+        [own_gain, own_cos, own_sin, wide_cos, wide_sin, o_made, *own_pieces[1:]],
     )
 
     squares = over_units([squares] * units)

time: 186 us -> 183 us (0.984)
  local copies, waits for them, and re-layouts: 12 us -> 3.96 us
  waiting for transfers between devices: 74.7 us -> 79.6 us
  starting transfers between devices: 59.6 us -> 56.7 us
  other arithmetic: 1.56 us -> 3.54 us
    unnamed x64 -> x48, local copies, waits for them, and re-layouts: 11.1 us -> 3.17 us
    ppermute x36, waiting for transfers between devices: 67.1 us -> 71.6 us  [swap(): return lax.ppermute(value, axis, [(i, i ^ mask) for i in range(size)])]
    ppermute x36, starting transfers between devices: 53.2 us -> 50.3 us  [swap(): return lax.ppermute(value, axis, [(i, i ^ mask) for i in range(size)])]
  transfers between devices with their start and end apart: 38 -> 38, of which waited for: 18 -> 20; matrix products, arithmetic and copies ran while one was open for 1% -> 2% of each run, Pallas kernels for 11% -> 11%
where the time goes in v5:
time: 183 us; the launch traced here: 182 us
  waiting for transfers between devices  79.6 us (43%)
  starting transfers between devices  56.7 us (31%)
  Pallas kernels  38 us (21%)
  local copies, waits for them, and re-layouts  3.96 us (2%)
  other arithmetic  3.54 us (2%)
    ppermute x36, waiting for transfers between devices, swap(): return lax.ppermute(value, axis, [(i, i ^ mask) for i in range(size)])  71.6 us
    ppermute x36, starting transfers between devices, swap(): return lax.ppermute(value, axis, [(i, i ^ mask) for i in range(size)])  50.3 us
    all_to_all x1, waiting for transfers between devices, body(): lax.all_to_all(o_pieces, 'tensor', split_axis=0, concat_axis=0, tiled=True)  7.98 us
    pallas_call x1, Pallas kernels, project(): pl.pallas_call(functools.partial(project_kernel, units), in_specs=[in_sme...  7.95 us
    pallas_call x1, Pallas kernels, output(): pl.pallas_call(functools.partial(output_kernel, units, rows, slot), in_sp...  7.5 us
    pallas_call x1, Pallas kernels, deal(): pl.pallas_call(functools.partial(deal_kernel, rows, slot), grid=(features...  6.14 us
    all_to_all x1, starting transfers between devices, body(): lax.all_to_all(o_pieces, 'tensor', split_axis=0, concat_axis=0, tiled=True)  3.74 us
    pallas_call x1, Pallas kernels, output_pieces(): pl.pallas_call(functools.partial(o_pieces_kernel, len(after)), in_specs=[...  3.74 us
  transfers between devices with their start and end apart: 38, of which 20 were waited for; matrix products, arithmetic and copies ran while one was open for 2% of the time, Pallas kernels for 11%

profile of v5, /device:TPU:0, one launch (start us, length us, event | category | flops | bytes accessed | tf_op | source)
XLA Modules:
  0.0 182.3 jit_solution(11676830579476537981)
XLA Ops:
  0.6 6.1 %deal.1 = (bf16[384,1024]{1,0:T(8,128)(2,1)}, bf16[384,1024]{1,0:T(8,128)(2,1)}, f32[192,128]{1,0:T(8,128)}) custom-call(s32[5]{0:T(128)} %stack.23.place, s32[16]{0:T(128)} %lens.7, s32[16]{0:T(128)} %dest.7, bf16[1024,1536]{1,0:T(8,128)(2,1)} %home.1), custom_call_target="tpu_custom_call" | custom-call | tf_op jit(solution)/shard_map/deal/pallas_call | solution.py:231
  9.9 3.0 %weight_pieces.1 = (bf16[640,256]{1,0:T(8,128)(2,1)}, bf16[640,256]{1,0:T(8,128)(2,1)}, bf16[640,256]{1,0:T(8,128)(2,1)}, bf16[640,256]{1,0:T(8,128)(2,1)}) custom-call(s32[5]{0:T(128)} %stack.23.place, f32[2,64]{1,0:T(2,128)} %bitcast.17, f32[2,64]{1,0:T(2,128)} %ks.1, f32[2,64]{1,0:T(2,128)} %vs.1, bf16[8192,256]{1,0:T(8,128)(2,1)} %q_hbm.1, ...), custom_call_target="tpu_custom_call" | custom-call | tf_op jit(solution)/shard_map/weight_pieces/pallas_call | solution.py:138
  18.3 11.4 %collective-permute-done.3.refs_4_ = bf16[640,256]{1,0:T(8,128)(2,1)S(1)} collective-permute-done((bf16[640,256]{1,0:T(8,128)(2,1)}, bf16[640,256]{1,0:T(8,128)(2,1)S(1)}, u32[]{:S(2)}, u32[]{:S(2)}) %collective-permute-start.3) | collective-permute-done | bytes 327712 | tf_op jit(solution)/shard_map/ppermute | solution.py:649
  37.9 3.7 %output_pieces.1 = (bf16[8,64,1024]{2,1,0:T(8,128)(2,1)}, f32[8,128]{1,0:T(8,128)}) custom-call(s32[5]{0:T(128)} %stack.23.place, f32[2,64]{1,0:T(2,128)} %scales.1, bf16[256,8192]{1,0:T(8,128)(2,1)} %o_hbm.1, bf16[384,1024]{1,0:T(8,128)(2,1)} %copy-done.1), custom_call_target="tpu_custom_call" | custom-call | tf_op jit(solution)/shard_map/output_pieces/pallas_call | solution.py:174
  41.7 3.1 %collective-permute-done.5.refs_6_ = bf16[640,256]{1,0:T(8,128)(2,1)} collective-permute-done((bf16[640,256]{1,0:T(8,128)(2,1)}, bf16[640,256]{1,0:T(8,128)(2,1)}, u32[]{:S(2)}, u32[]{:S(2)}) %collective-permute-start.5) | collective-permute-done | bytes 327712 | tf_op jit(solution)/shard_map/ppermute | solution.py:649
  46.0 3.7 %collect.1 = (bf16[3,640,256]{2,1,0:T(8,128)(2,1)}, f32[8,768]{1,0:T(8,128)}) custom-call(bf16[384,1024]{1,0:T(8,128)(2,1)} %get-tuple-element.22.rest_0_.refs_0_.rest_5_, bf16[384,1024]{1,0:T(8,128)(2,1)} %copy-done.1, bf16[384,1024]{1,0:T(8,128)(2,1)} %copy-done.7, bf16[384,1024]{1,0:T(8,128)(2,1)} %copy-done.5, bf16[640,256]{1,0:T(8,128)(2,1)} %copy-done.22, ...), custom_call_target="tpu_custom_call" | custom-call | tf_op jit(solution)/shard_map/collect/pallas_call | solution.py:286
  51.3 3.6 %collective-permute-start.10 = (f32[8,768]{1,0:T(8,128)}, f32[8,768]{1,0:T(8,128)S(1)}, u32[]{:S(2)}, u32[]{:S(2)}) collective-permute-start(f32[8,768]{1,0:T(8,128)} %get-tuple-element.29.rest_0_), channel_id=1, source_target_pairs={{0,6},{1,7},{2,4},{3,5},{4,2},{5,3},{6,0},{7,1},{8,14},{9,15},{10,... | collective-permute-start | bytes 73736 | tf_op jit(solution)/shard_map/ppermute | solution.py:649
  54.9 3.4 %collective-permute-start.9 = (f32[8,768]{1,0:T(8,128)}, f32[8,768]{1,0:T(8,128)S(1)}, u32[]{:S(2)}, u32[]{:S(2)}) collective-permute-start(f32[8,768]{1,0:T(8,128)} %get-tuple-element.29.rest_0_), channel_id=1, source_target_pairs={{0,4},{1,5},{2,6},{3,7},{4,0},{5,1},{6,2},{7,3},{8,12},{9,13},{10,... | collective-permute-start | bytes 73736 | tf_op jit(solution)/shard_map/ppermute | solution.py:649
  63.3 3.7 %all-to-all-start = ((bf16[8,64,1024]{2,1,0:T(8,128)(2,1)}), bf16[8,64,1024]{2,1,0:T(8,128)(2,1)S(1)}, u32[]{:S(2)}, u32[]{:S(2)}) async-start(bf16[8,64,1024]{2,1,0:T(8,128)(2,1)} %copy-done.4), calls=%async_computation | async-start | bytes 2097152 | tf_op jit(solution)/shard_map/all_to_all | solution.py:723
  70.5 3.0 %collective-permute-done.13.refs_0_ = bf16[3,640,256]{2,1,0:T(8,128)(2,1)} collective-permute-done((bf16[3,640,256]{2,1,0:T(8,128)(2,1)}, bf16[3,640,256]{2,1,0:T(8,128)(2,1)}, u32[]{:S(2)}, u32[]{:S(2)}) %collective-permute-start.13) | collective-permute-done | bytes 983072 | tf_op jit(solution)/shard_map/ppermute | solution.py:649
  73.5 2.8 %collective-permute-done.14.rest_7_ = bf16[3,640,256]{2,1,0:T(8,128)(2,1)S(1)} collective-permute-done((bf16[3,640,256]{2,1,0:T(8,128)(2,1)}, bf16[3,640,256]{2,1,0:T(8,128)(2,1)S(1)}, u32[]{:S(2)}, u32[]{:S(2)}) %collective-permute-start.14) | collective-permute-done | bytes 983072 | tf_op jit(solution)/shard_map/ppermute | solution.py:649
  76.3 8.0 %project.1 = (bf16[2,192,768]{2,1,0:T(8,128)(2,1)S(1)}, bf16[2,192,768]{2,1,0:T(8,128)(2,1)S(1)}, bf16[2,192,512]{2,1,0:T(8,128)(2,1)S(1)}, bf16[2,192,512]{2,1,0:T(8,128)(2,1)S(1)}) custom-call(s32[5]{0:T(128)S(1)} %copy-done.18, bf16[768,2048]{1,0:T(8,128)(2,1)S(1)} %normalize.1.refs_3_.tokens, bf16[640,256]{1,0:T(8,128)(2,1)S(1)} %copy-done.16, ...), custom_call_target="tpu_custom_call" | custom-call | tf_op jit(solution)/shard_map/project/pallas_call | solution.py:432
  84.2 8.0 %all-to-all-done.refs_0_ = bf16[8,64,1024]{2,1,0:T(8,128)(2,1)S(1)} async-done(((bf16[8,64,1024]{2,1,0:T(8,128)(2,1)}), bf16[8,64,1024]{2,1,0:T(8,128)(2,1)S(1)}, u32[]{:S(2)}, u32[]{:S(2)}) %all-to-all-start) | async-done | bytes 1048608 | tf_op jit(solution)/shard_map/all_to_all | solution.py:723
  92.8 13.5 %collective-permute-done.18.got.refs_1_ = bf16[2,192,768]{2,1,0:T(8,128)(2,1)S(1)} collective-permute-done((bf16[2,192,768]{2,1,0:T(8,128)(2,1)S(1)}, bf16[2,192,768]{2,1,0:T(8,128)(2,1)S(1)}, u32[]{:S(2)}, u32[]{:S(2)}) %collective-permute-start.18) | collective-permute-done | bytes 589856 | tf_op jit(solution)/shard_map/ppermute | solution.py:649
  106.5 3.0 %collective-permute-start.19 = (bf16[192,768]{1,0:T(8,128)(2,1)S(1)}, bf16[192,768]{1,0:T(8,128)(2,1)S(1)}, u32[]{:S(2)}, u32[]{:S(2)}) collective-permute-start(bf16[192,768]{1,0:T(8,128)(2,1)S(1)} %pair_sums.2), channel_id=1, source_target_pairs={{0,4},{1,5},{2,6},{3,7},{4,0},{5,1},{6,2},{7,3},{8,12},{9,13},{10,... | collective-permute-start | bytes 884744 | tf_op jit(solution)/shard_map/ppermute | solution.py:649
  109.5 5.8 %collective-permute-done.16 = bf16[8,64,1024]{2,1,0:T(8,128)(2,1)S(1)} collective-permute-done((bf16[8,64,1024]{2,1,0:T(8,128)(2,1)S(1)}, bf16[8,64,1024]{2,1,0:T(8,128)(2,1)S(1)}, u32[]{:S(2)}, u32[]{:S(2)}) %collective-permute-start.16) | collective-permute-done | bytes 1048608 | tf_op jit(solution)/shard_map/ppermute | solution.py:649
  115.3 5.1 %collective-permute-done.20.got.refs_1_ = bf16[2,192,512]{2,1,0:T(8,128)(2,1)S(1)} collective-permute-done((bf16[2,192,512]{2,1,0:T(8,128)(2,1)S(1)}, bf16[2,192,512]{2,1,0:T(8,128)(2,1)S(1)}, u32[]{:S(2)}, u32[]{:S(2)}) %collective-permute-start.20) | collective-permute-done | bytes 393248 | tf_op jit(solution)/shard_map/ppermute | solution.py:649
  145.3 4.0 %collective-permute-done.31.refs_0_ = bf16[192,512]{1,0:T(8,128)(2,1)S(1)} collective-permute-done((bf16[192,512]{1,0:T(8,128)(2,1)S(1)}, bf16[192,512]{1,0:T(8,128)(2,1)S(1)}, u32[]{:S(2)}, u32[]{:S(2)}) %collective-permute-start.31) | collective-permute-done | bytes 196640 | tf_op jit(solution)/shard_map/ppermute | solution.py:649
  155.2 5.7 %collective-permute-start.28 = (bf16[192,512]{1,0:T(8,128)(2,1)S(1)}, bf16[192,512]{1,0:T(8,128)(2,1)S(1)}, u32[]{:S(2)}, u32[]{:S(2)}) collective-permute-start(bf16[192,512]{1,0:T(8,128)(2,1)S(1)} %collective-permute-done.25.refs_7_), channel_id=1, source_target_pairs={{0,1},{1,0},{2,3},{3,2},{4,5},{5,4},{6,7},{7,6},{8,9},{9,8},{10,11... | collective-permute-start | bytes 589832 | tf_op jit(solution)/shard_map/ppermute | solution.py:649
  161.0 2.7 %collective-permute-start.36 = (bf16[192,512]{1,0:T(8,128)(2,1)S(1)}, bf16[192,512]{1,0:T(8,128)(2,1)S(1)}, u32[]{:S(2)}, u32[]{:S(2)}) collective-permute-start(bf16[192,512]{1,0:T(8,128)(2,1)S(1)} %collective-permute-done.33.refs_15_), channel_id=1, source_target_pairs={{0,1},{1,0},{2,3},{3,2},{4,5},{5,4},{6,7},{7,6},{8,9},{9,8},{10,11... | collective-permute-start | bytes 589832 | tf_op jit(solution)/shard_map/ppermute | solution.py:649
  163.7 3.7 %collective-permute-done.28.refs_11_ = bf16[192,512]{1,0:T(8,128)(2,1)S(1)} collective-permute-done((bf16[192,512]{1,0:T(8,128)(2,1)S(1)}, bf16[192,512]{1,0:T(8,128)(2,1)S(1)}, u32[]{:S(2)}, u32[]{:S(2)}) %collective-permute-start.28) | collective-permute-done | bytes 196640 | tf_op jit(solution)/shard_map/ppermute | solution.py:649
  167.4 4.2 %collective-permute-done.34.refs_17_ = bf16[192,512]{1,0:T(8,128)(2,1)S(1)} collective-permute-done((bf16[192,512]{1,0:T(8,128)(2,1)S(1)}, bf16[192,512]{1,0:T(8,128)(2,1)S(1)}, u32[]{:S(2)}, u32[]{:S(2)}) %collective-permute-start.34) | collective-permute-done | bytes 196640 | tf_op jit(solution)/shard_map/ppermute | solution.py:649
  171.6 3.0 %collective-permute-done.36.refs_19_ = bf16[192,512]{1,0:T(8,128)(2,1)S(1)} collective-permute-done((bf16[192,512]{1,0:T(8,128)(2,1)S(1)}, bf16[192,512]{1,0:T(8,128)(2,1)S(1)}, u32[]{:S(2)}, u32[]{:S(2)}) %collective-permute-start.36) | collective-permute-done | bytes 196640 | tf_op jit(solution)/shard_map/ppermute | solution.py:649
  174.6 7.5 %output.1 = bf16[1024,768]{1,0:T(8,128)(2,1)} custom-call(s32[5]{0:T(128)S(1)} %copy-done.18, s32[16]{0:T(128)S(1)} %copy-done.20, s32[16]{0:T(128)S(1)} %copy-done.21, bf16[4,2,64,1024]{3,2,1,0:T(8,128)(2,1)S(1)} %bitcast.11, bf16[4,2,64,1024]{3,2,1,0:T(8,128)(2,1)S(1)} %bitcast.13, bf16[4,2,64,1024]{3,2,1,0:T(8,128)(2,1)S(1)} %bitcast.12, ...), custom_call_target="tpu_custom_call" | custom-call | tf_op jit(solution)/shard_map/output/pallas_call | solution.py:628
  (129 shorter events, 60.2 us)
Async XLA Ops:
  6.7 25.6 %collective-permute-start = (bf16[384,1024]{1,0:T(8,128)(2,1)}, bf16[384,1024]{1,0:T(8,128)(2,1)S(1)}, u32[]{:S(2)}, u32[]{:S(2)}) collective-permute-start(bf16[384,1024]{1,0:T(8,128)(2,1)} %get-tuple-element.20), channel_id=1, source_target_pairs={{0,8},{8,0},{1,9},{9,1},{2,10},{10,2},{3,11},{11,3},{4,12},{12,4},... | collective-permute-start | bytes 2359304 | tf_op jit(solution)/shard_map/ppermute | solution.py:649
  7.2 37.5 %collective-permute-start.2 = (bf16[384,1024]{1,0:T(8,128)(2,1)}, bf16[384,1024]{1,0:T(8,128)(2,1)S(1)}, u32[]{:S(2)}, u32[]{:S(2)}) collective-permute-start(bf16[384,1024]{1,0:T(8,128)(2,1)} %get-tuple-element.20), channel_id=1, source_target_pairs={{0,9},{1,8},{2,11},{3,10},{4,13},{5,12},{6,15},{7,14},{8,1},{9,0},... | collective-permute-start | bytes 2359304 | tf_op jit(solution)/shard_map/ppermute | solution.py:708
  9.8 35.2 %collective-permute-start.1 = (bf16[384,1024]{1,0:T(8,128)(2,1)}, bf16[384,1024]{1,0:T(8,128)(2,1)S(1)}, u32[]{:S(2)}, u32[]{:S(2)}) collective-permute-start(bf16[384,1024]{1,0:T(8,128)(2,1)} %get-tuple-element.22.rest_0_.refs_0_.rest_5_), channel_id=1, source_target_pairs={{0,1},{1,0},{2,3},{3,2},{4,5},{5,4},{6,7},{7,6},{8,9},{9,8},{10,11... | collective-permute-start | bytes 2359304 | tf_op jit(solution)/shard_map/ppermute | solution.py:649
  12.8 16.9 %collective-permute-start.3 = (bf16[640,256]{1,0:T(8,128)(2,1)}, bf16[640,256]{1,0:T(8,128)(2,1)S(1)}, u32[]{:S(2)}, u32[]{:S(2)}) collective-permute-start(bf16[640,256]{1,0:T(8,128)(2,1)} %get-tuple-element.23), channel_id=1, source_target_pairs={{0,2},{1,3},{2,0},{3,1},{4,6},{5,7},{6,4},{7,5},{8,10},{9,11},{10,... | collective-permute-start | bytes 983048 | tf_op jit(solution)/shard_map/ppermute | solution.py:649
  15.0 17.4 %collective-permute-start.4 = (bf16[640,256]{1,0:T(8,128)(2,1)}, bf16[640,256]{1,0:T(8,128)(2,1)}, u32[]{:S(2)}, u32[]{:S(2)}) collective-permute-start(bf16[640,256]{1,0:T(8,128)(2,1)} %get-tuple-element.24), channel_id=1, source_target_pairs={{0,4},{1,5},{2,6},{3,7},{4,0},{5,1},{6,2},{7,3},{8,12},{9,13},{10,... | collective-permute-start | bytes 983048 | tf_op jit(solution)/shard_map/ppermute | solution.py:649
  29.7 15.0 %collective-permute-start.7 = (bf16[640,256]{1,0:T(8,128)(2,1)}, bf16[640,256]{1,0:T(8,128)(2,1)}, u32[]{:S(2)}, u32[]{:S(2)}) collective-permute-start(bf16[640,256]{1,0:T(8,128)(2,1)} %get-tuple-element.28.rest_0_), channel_id=1, source_target_pairs={{0,16},{16,0},{1,17},{17,1},{2,18},{18,2},{3,19},{19,3},{4,20},{20... | collective-permute-start | bytes 983048 | tf_op jit(solution)/shard_map/ppermute | solution.py:649
  32.4 12.4 %collective-permute-start.6 = (bf16[640,256]{1,0:T(8,128)(2,1)}, bf16[640,256]{1,0:T(8,128)(2,1)S(1)}, u32[]{:S(2)}, u32[]{:S(2)}) collective-permute-start(bf16[640,256]{1,0:T(8,128)(2,1)} %get-tuple-element.28.rest_0_), channel_id=1, source_target_pairs={{0,8},{8,0},{1,9},{9,1},{2,10},{10,2},{3,11},{11,3},{4,12},{12,4},... | collective-permute-start | bytes 983048 | tf_op jit(solution)/shard_map/ppermute | solution.py:649
  32.4 12.3 %collective-permute-start.5 = (bf16[640,256]{1,0:T(8,128)(2,1)}, bf16[640,256]{1,0:T(8,128)(2,1)}, u32[]{:S(2)}, u32[]{:S(2)}) collective-permute-start(bf16[640,256]{1,0:T(8,128)(2,1)} %get-tuple-element.25), channel_id=1, source_target_pairs={{0,6},{1,7},{2,4},{3,5},{4,2},{5,3},{6,0},{7,1},{8,14},{9,15},{10,... | collective-permute-start | bytes 983048 | tf_op jit(solution)/shard_map/ppermute | solution.py:649
  49.7 23.8 %collective-permute-start.13 = (bf16[3,640,256]{2,1,0:T(8,128)(2,1)}, bf16[3,640,256]{2,1,0:T(8,128)(2,1)}, u32[]{:S(2)}, u32[]{:S(2)}) collective-permute-start(bf16[3,640,256]{2,1,0:T(8,128)(2,1)} %get-tuple-element.30.rest_4_), channel_id=1, source_target_pairs={{0,16},{16,0},{1,17},{17,1},{2,18},{18,2},{3,19},{19,3},{4,20},{20... | collective-permute-start | bytes 2949128 | tf_op jit(solution)/shard_map/ppermute | solution.py:649
  51.3 22.2 %collective-permute-start.12 = (bf16[3,640,256]{2,1,0:T(8,128)(2,1)}, bf16[3,640,256]{2,1,0:T(8,128)(2,1)}, u32[]{:S(2)}, u32[]{:S(2)}) collective-permute-start(bf16[3,640,256]{2,1,0:T(8,128)(2,1)} %get-tuple-element.30.rest_4_), channel_id=1, source_target_pairs={{0,8},{8,0},{1,9},{9,1},{2,10},{10,2},{3,11},{11,3},{4,12},{12,4},... | collective-permute-start | bytes 2949128 | tf_op jit(solution)/shard_map/ppermute | solution.py:649
  63.3 28.9 %all-to-all-start = ((bf16[8,64,1024]{2,1,0:T(8,128)(2,1)}), bf16[8,64,1024]{2,1,0:T(8,128)(2,1)S(1)}, u32[]{:S(2)}, u32[]{:S(2)}) async-start(bf16[8,64,1024]{2,1,0:T(8,128)(2,1)} %copy-done.4), calls=%async_computation | async-start | bytes 2097152 | tf_op jit(solution)/shard_map/all_to_all | solution.py:723
  92.2 23.1 %collective-permute-start.16 = (bf16[8,64,1024]{2,1,0:T(8,128)(2,1)S(1)}, bf16[8,64,1024]{2,1,0:T(8,128)(2,1)S(1)}, u32[]{:S(2)}, u32[]{:S(2)}) collective-permute-start(bf16[8,64,1024]{2,1,0:T(8,128)(2,1)S(1)} %gate.8), channel_id=1, source_target_pairs={{0,16},{16,0},{1,17},{17,1},{2,18},{18,2},{3,19},{19,3},{4,20},{20... | collective-permute-start | bytes 3145736 | tf_op jit(solution)/shard_map/ppermute | solution.py:649
  92.8 13.5 %collective-permute-start.18 = (bf16[2,192,768]{2,1,0:T(8,128)(2,1)S(1)}, bf16[2,192,768]{2,1,0:T(8,128)(2,1)S(1)}, u32[]{:S(2)}, u32[]{:S(2)}) collective-permute-start(bf16[2,192,768]{2,1,0:T(8,128)(2,1)S(1)} %get-tuple-element.32), channel_id=1, source_target_pairs={{0,2},{1,3},{2,0},{3,1},{4,6},{5,7},{6,4},{7,5},{8,10},{9,11},{10,... | collective-permute-start | bytes 1769480 | tf_op jit(solution)/shard_map/ppermute | solution.py:649
  92.8 60.3 %collective-permute-start.15 = (bf16[8,64,1024]{2,1,0:T(8,128)(2,1)S(1)}, bf16[8,64,1024]{2,1,0:T(8,128)(2,1)S(1)}, u32[]{:S(2)}, u32[]{:S(2)}) collective-permute-start(bf16[8,64,1024]{2,1,0:T(8,128)(2,1)S(1)} %gate.8), channel_id=1, source_target_pairs={{0,8},{8,0},{1,9},{9,1},{2,10},{10,2},{3,11},{11,3},{4,12},{12,4},... | collective-permute-start | bytes 3145736 | tf_op jit(solution)/shard_map/ppermute | solution.py:649
  106.3 14.1 %collective-permute-start.20 = (bf16[2,192,512]{2,1,0:T(8,128)(2,1)S(1)}, bf16[2,192,512]{2,1,0:T(8,128)(2,1)S(1)}, u32[]{:S(2)}, u32[]{:S(2)}) collective-permute-start(bf16[2,192,512]{2,1,0:T(8,128)(2,1)S(1)} %gate.9), channel_id=1, source_target_pairs={{0,2},{1,3},{2,0},{3,1},{4,6},{5,7},{6,4},{7,5},{8,10},{9,11},{10,... | collective-permute-start | bytes 1179656 | tf_op jit(solution)/shard_map/ppermute | solution.py:649
  106.5 16.4 %collective-permute-start.19 = (bf16[192,768]{1,0:T(8,128)(2,1)S(1)}, bf16[192,768]{1,0:T(8,128)(2,1)S(1)}, u32[]{:S(2)}, u32[]{:S(2)}) collective-permute-start(bf16[192,768]{1,0:T(8,128)(2,1)S(1)} %pair_sums.2), channel_id=1, source_target_pairs={{0,4},{1,5},{2,6},{3,7},{4,0},{5,1},{6,2},{7,3},{8,12},{9,13},{10,... | collective-permute-start | bytes 884744 | tf_op jit(solution)/shard_map/ppermute | solution.py:649
  115.3 59.3 %collective-permute-start.17 = (bf16[8,64,1024]{2,1,0:T(8,128)(2,1)S(1)}, bf16[8,64,1024]{2,1,0:T(8,128)(2,1)S(1)}, u32[]{:S(2)}, u32[]{:S(2)}) collective-permute-start(bf16[8,64,1024]{2,1,0:T(8,128)(2,1)S(1)} %collective-permute-done.16), channel_id=1, source_target_pairs={{0,8},{8,0},{1,9},{9,1},{2,10},{10,2},{3,11},{11,3},{4,12},{12,4},... | collective-permute-start | bytes 3145736 | tf_op jit(solution)/shard_map/ppermute | solution.py:649
  120.5 12.5 %collective-permute-start.29 = (bf16[192,512]{1,0:T(8,128)(2,1)S(1)}, bf16[192,512]{1,0:T(8,128)(2,1)S(1)}, u32[]{:S(2)}, u32[]{:S(2)}) collective-permute-start(bf16[192,512]{1,0:T(8,128)(2,1)S(1)} %pair_sums.3.refs_3_), channel_id=1, source_target_pairs={{0,4},{1,5},{2,6},{3,7},{4,0},{5,1},{6,2},{7,3},{8,12},{9,13},{10,... | collective-permute-start | bytes 589832 | tf_op jit(solution)/shard_map/ppermute | solution.py:649
  133.0 9.7 %collective-permute-start.22 = (bf16[192,512]{1,0:T(8,128)(2,1)S(1)}, bf16[192,512]{1,0:T(8,128)(2,1)S(1)}, u32[]{:S(2)}, u32[]{:S(2)}) collective-permute-start(bf16[192,512]{1,0:T(8,128)(2,1)S(1)} %attend.2.refs_4_), channel_id=1, source_target_pairs={{0,2},{1,3},{2,0},{3,1},{4,6},{5,7},{6,4},{7,5},{8,10},{9,11},{10,... | collective-permute-start | bytes 589832 | tf_op jit(solution)/shard_map/ppermute | solution.py:649
  142.9 12.2 %collective-permute-start.27 = (bf16[192,512]{1,0:T(8,128)(2,1)S(1)}, bf16[192,512]{1,0:T(8,128)(2,1)S(1)}, u32[]{:S(2)}, u32[]{:S(2)}) collective-permute-start(bf16[192,512]{1,0:T(8,128)(2,1)S(1)} %gate.10.refs_6_), channel_id=1, source_target_pairs={{0,1},{1,0},{2,3},{3,2},{4,5},{5,4},{6,7},{7,6},{8,9},{9,8},{10,11... | collective-permute-start | bytes 589832 | tf_op jit(solution)/shard_map/ppermute | solution.py:649
  155.1 12.2 %collective-permute-start.35 = (bf16[192,512]{1,0:T(8,128)(2,1)S(1)}, bf16[192,512]{1,0:T(8,128)(2,1)S(1)}, u32[]{:S(2)}, u32[]{:S(2)}) collective-permute-start(bf16[192,512]{1,0:T(8,128)(2,1)S(1)} %gate.11.refs_14_), channel_id=1, source_target_pairs={{0,1},{1,0},{2,3},{3,2},{4,5},{5,4},{6,7},{7,6},{8,9},{9,8},{10,11... | collective-permute-start | bytes 589832 | tf_op jit(solution)/shard_map/ppermute | solution.py:649
  155.2 12.2 %collective-permute-start.28 = (bf16[192,512]{1,0:T(8,128)(2,1)S(1)}, bf16[192,512]{1,0:T(8,128)(2,1)S(1)}, u32[]{:S(2)}, u32[]{:S(2)}) collective-permute-start(bf16[192,512]{1,0:T(8,128)(2,1)S(1)} %collective-permute-done.25.refs_7_), channel_id=1, source_target_pairs={{0,1},{1,0},{2,3},{3,2},{4,5},{5,4},{6,7},{7,6},{8,9},{9,8},{10,11... | collective-permute-start | bytes 589832 | tf_op jit(solution)/shard_map/ppermute | solution.py:649
  160.9 10.7 %collective-permute-start.34 = (bf16[192,512]{1,0:T(8,128)(2,1)S(1)}, bf16[192,512]{1,0:T(8,128)(2,1)S(1)}, u32[]{:S(2)}, u32[]{:S(2)}) collective-permute-start(bf16[192,512]{1,0:T(8,128)(2,1)S(1)} %collective-permute-done.30.refs_1_.refs_13_), channel_id=1, source_target_pairs={{0,1},{1,0},{2,3},{3,2},{4,5},{5,4},{6,7},{7,6},{8,9},{9,8},{10,11... | collective-permute-start | bytes 589832 | tf_op jit(solution)/shard_map/ppermute | solution.py:649
  161.0 13.6 %collective-permute-start.36 = (bf16[192,512]{1,0:T(8,128)(2,1)S(1)}, bf16[192,512]{1,0:T(8,128)(2,1)S(1)}, u32[]{:S(2)}, u32[]{:S(2)}) collective-permute-start(bf16[192,512]{1,0:T(8,128)(2,1)S(1)} %collective-permute-done.33.refs_15_), channel_id=1, source_target_pairs={{0,1},{1,0},{2,3},{3,2},{4,5},{5,4},{6,7},{7,6},{8,9},{9,8},{10,11... | collective-permute-start | bytes 589832 | tf_op jit(solution)/shard_map/ppermute | solution.py:649
  (38 other events, 438.9 us)

commit v6 on v5

--- a/solution.py
+++ b/solution.py
@@ -226,7 +226,7 @@
 
 def deal(place, lens, dest, home, rows, slot):
     features = home.shape[0]
-    width = min(features, 256)
+    width = min(features, 512)
     tokens = BLOCKS * slot
     return pl.pallas_call(
         functools.partial(deal_kernel, rows, slot),

time: 183 us -> 182 us (level)
  no operation moved by 1% of the time
where the time goes in v6:
time: 182 us
  waiting for transfers between devices  79.5 us (44%)
  starting transfers between devices  56.7 us (31%)
  Pallas kernels  37.5 us (21%)
  local copies, waits for them, and re-layouts  3.95 us (2%)
  other arithmetic  3.54 us (2%)
    ppermute x36, waiting for transfers between devices, swap(): return lax.ppermute(value, axis, [(i, i ^ mask) for i in range(size)])  71.6 us
    ppermute x36, starting transfers between devices, swap(): return lax.ppermute(value, axis, [(i, i ^ mask) for i in range(size)])  50.3 us
    all_to_all x1, waiting for transfers between devices, body(): lax.all_to_all(o_pieces, 'tensor', split_axis=0, concat_axis=0, tiled=True)  7.97 us
    pallas_call x1, Pallas kernels, project(): pl.pallas_call(functools.partial(project_kernel, units), in_specs=[in_sme...  7.95 us
    pallas_call x1, Pallas kernels, output(): pl.pallas_call(functools.partial(output_kernel, units, rows, slot), in_sp...  7.5 us
    pallas_call x1, Pallas kernels, deal(): pl.pallas_call(functools.partial(deal_kernel, rows, slot), grid=(features...  5.69 us
    all_to_all x1, starting transfers between devices, body(): lax.all_to_all(o_pieces, 'tensor', split_axis=0, concat_axis=0, tiled=True)  3.74 us
    pallas_call x1, Pallas kernels, output_pieces(): pl.pallas_call(functools.partial(o_pieces_kernel, len(after)), in_specs=[...  3.74 us
  transfers between devices with their start and end apart: 38, of which 20 were waited for; matrix products, arithmetic and copies ran while one was open for 2% of the time, Pallas kernels for 11%

profile of v6, /device:TPU:0, one launch (start us, length us, event | category | flops | bytes accessed | tf_op | source)
XLA Modules:
  0.0 181.8 jit_solution(9575555416914685538)
XLA Ops:
  0.6 5.7 %deal.1 = (bf16[384,1024]{1,0:T(8,128)(2,1)}, bf16[384,1024]{1,0:T(8,128)(2,1)}, f32[192,128]{1,0:T(8,128)}) custom-call(s32[5]{0:T(128)} %stack.23.place, s32[16]{0:T(128)} %lens.7, s32[16]{0:T(128)} %dest.7, bf16[1024,1536]{1,0:T(8,128)(2,1)} %home.1), custom_call_target="tpu_custom_call" | custom-call | tf_op jit(solution)/shard_map/deal/pallas_call | solution.py:231
  9.4 3.0 %weight_pieces.1 = (bf16[640,256]{1,0:T(8,128)(2,1)}, bf16[640,256]{1,0:T(8,128)(2,1)}, bf16[640,256]{1,0:T(8,128)(2,1)}, bf16[640,256]{1,0:T(8,128)(2,1)}) custom-call(s32[5]{0:T(128)} %stack.23.place, f32[2,64]{1,0:T(2,128)} %bitcast.17, f32[2,64]{1,0:T(2,128)} %ks.1, f32[2,64]{1,0:T(2,128)} %vs.1, bf16[8192,256]{1,0:T(8,128)(2,1)} %q_hbm.1, ...), custom_call_target="tpu_custom_call" | custom-call | tf_op jit(solution)/shard_map/weight_pieces/pallas_call | solution.py:138
  17.9 11.4 %collective-permute-done.3.refs_4_ = bf16[640,256]{1,0:T(8,128)(2,1)S(1)} collective-permute-done((bf16[640,256]{1,0:T(8,128)(2,1)}, bf16[640,256]{1,0:T(8,128)(2,1)S(1)}, u32[]{:S(2)}, u32[]{:S(2)}) %collective-permute-start.3) | collective-permute-done | bytes 327712 | tf_op jit(solution)/shard_map/ppermute | solution.py:649
  37.5 3.7 %output_pieces.1 = (bf16[8,64,1024]{2,1,0:T(8,128)(2,1)}, f32[8,128]{1,0:T(8,128)}) custom-call(s32[5]{0:T(128)} %stack.23.place, f32[2,64]{1,0:T(2,128)} %scales.1, bf16[256,8192]{1,0:T(8,128)(2,1)} %o_hbm.1, bf16[384,1024]{1,0:T(8,128)(2,1)} %copy-done.1), custom_call_target="tpu_custom_call" | custom-call | tf_op jit(solution)/shard_map/output_pieces/pallas_call | solution.py:174
  41.2 3.0 %collective-permute-done.5.refs_6_ = bf16[640,256]{1,0:T(8,128)(2,1)} collective-permute-done((bf16[640,256]{1,0:T(8,128)(2,1)}, bf16[640,256]{1,0:T(8,128)(2,1)}, u32[]{:S(2)}, u32[]{:S(2)}) %collective-permute-start.5) | collective-permute-done | bytes 327712 | tf_op jit(solution)/shard_map/ppermute | solution.py:649
  45.5 3.7 %collect.1 = (bf16[3,640,256]{2,1,0:T(8,128)(2,1)}, f32[8,768]{1,0:T(8,128)}) custom-call(bf16[384,1024]{1,0:T(8,128)(2,1)} %get-tuple-element.22.rest_0_.refs_0_.rest_5_, bf16[384,1024]{1,0:T(8,128)(2,1)} %copy-done.1, bf16[384,1024]{1,0:T(8,128)(2,1)} %copy-done.7, bf16[384,1024]{1,0:T(8,128)(2,1)} %copy-done.5, bf16[640,256]{1,0:T(8,128)(2,1)} %copy-done.22, ...), custom_call_target="tpu_custom_call" | custom-call | tf_op jit(solution)/shard_map/collect/pallas_call | solution.py:286
  50.9 3.6 %collective-permute-start.10 = (f32[8,768]{1,0:T(8,128)}, f32[8,768]{1,0:T(8,128)S(1)}, u32[]{:S(2)}, u32[]{:S(2)}) collective-permute-start(f32[8,768]{1,0:T(8,128)} %get-tuple-element.29.rest_0_), channel_id=1, source_target_pairs={{0,6},{1,7},{2,4},{3,5},{4,2},{5,3},{6,0},{7,1},{8,14},{9,15},{10,... | collective-permute-start | bytes 73736 | tf_op jit(solution)/shard_map/ppermute | solution.py:649
  54.5 3.4 %collective-permute-start.9 = (f32[8,768]{1,0:T(8,128)}, f32[8,768]{1,0:T(8,128)S(1)}, u32[]{:S(2)}, u32[]{:S(2)}) collective-permute-start(f32[8,768]{1,0:T(8,128)} %get-tuple-element.29.rest_0_), channel_id=1, source_target_pairs={{0,4},{1,5},{2,6},{3,7},{4,0},{5,1},{6,2},{7,3},{8,12},{9,13},{10,... | collective-permute-start | bytes 73736 | tf_op jit(solution)/shard_map/ppermute | solution.py:649
  62.8 3.7 %all-to-all-start = ((bf16[8,64,1024]{2,1,0:T(8,128)(2,1)}), bf16[8,64,1024]{2,1,0:T(8,128)(2,1)S(1)}, u32[]{:S(2)}, u32[]{:S(2)}) async-start(bf16[8,64,1024]{2,1,0:T(8,128)(2,1)} %copy-done.4), calls=%async_computation | async-start | bytes 2097152 | tf_op jit(solution)/shard_map/all_to_all | solution.py:723
  70.1 3.0 %collective-permute-done.13.refs_0_ = bf16[3,640,256]{2,1,0:T(8,128)(2,1)} collective-permute-done((bf16[3,640,256]{2,1,0:T(8,128)(2,1)}, bf16[3,640,256]{2,1,0:T(8,128)(2,1)}, u32[]{:S(2)}, u32[]{:S(2)}) %collective-permute-start.13) | collective-permute-done | bytes 983072 | tf_op jit(solution)/shard_map/ppermute | solution.py:649
  73.0 2.8 %collective-permute-done.14.rest_7_ = bf16[3,640,256]{2,1,0:T(8,128)(2,1)S(1)} collective-permute-done((bf16[3,640,256]{2,1,0:T(8,128)(2,1)}, bf16[3,640,256]{2,1,0:T(8,128)(2,1)S(1)}, u32[]{:S(2)}, u32[]{:S(2)}) %collective-permute-start.14) | collective-permute-done | bytes 983072 | tf_op jit(solution)/shard_map/ppermute | solution.py:649
  75.8 7.9 %project.1 = (bf16[2,192,768]{2,1,0:T(8,128)(2,1)S(1)}, bf16[2,192,768]{2,1,0:T(8,128)(2,1)S(1)}, bf16[2,192,512]{2,1,0:T(8,128)(2,1)S(1)}, bf16[2,192,512]{2,1,0:T(8,128)(2,1)S(1)}) custom-call(s32[5]{0:T(128)S(1)} %copy-done.18, bf16[768,2048]{1,0:T(8,128)(2,1)S(1)} %normalize.1.refs_3_.tokens, bf16[640,256]{1,0:T(8,128)(2,1)S(1)} %copy-done.16, ...), custom_call_target="tpu_custom_call" | custom-call | tf_op jit(solution)/shard_map/project/pallas_call | solution.py:432
  83.8 8.0 %all-to-all-done.refs_0_ = bf16[8,64,1024]{2,1,0:T(8,128)(2,1)S(1)} async-done(((bf16[8,64,1024]{2,1,0:T(8,128)(2,1)}), bf16[8,64,1024]{2,1,0:T(8,128)(2,1)S(1)}, u32[]{:S(2)}, u32[]{:S(2)}) %all-to-all-start) | async-done | bytes 1048608 | tf_op jit(solution)/shard_map/all_to_all | solution.py:723
  92.4 13.5 %collective-permute-done.18.got.refs_1_ = bf16[2,192,768]{2,1,0:T(8,128)(2,1)S(1)} collective-permute-done((bf16[2,192,768]{2,1,0:T(8,128)(2,1)S(1)}, bf16[2,192,768]{2,1,0:T(8,128)(2,1)S(1)}, u32[]{:S(2)}, u32[]{:S(2)}) %collective-permute-start.18) | collective-permute-done | bytes 589856 | tf_op jit(solution)/shard_map/ppermute | solution.py:649
  106.0 3.1 %collective-permute-start.19 = (bf16[192,768]{1,0:T(8,128)(2,1)S(1)}, bf16[192,768]{1,0:T(8,128)(2,1)S(1)}, u32[]{:S(2)}, u32[]{:S(2)}) collective-permute-start(bf16[192,768]{1,0:T(8,128)(2,1)S(1)} %pair_sums.2), channel_id=1, source_target_pairs={{0,4},{1,5},{2,6},{3,7},{4,0},{5,1},{6,2},{7,3},{8,12},{9,13},{10,... | collective-permute-start | bytes 884744 | tf_op jit(solution)/shard_map/ppermute | solution.py:649
  109.1 5.7 %collective-permute-done.16 = bf16[8,64,1024]{2,1,0:T(8,128)(2,1)S(1)} collective-permute-done((bf16[8,64,1024]{2,1,0:T(8,128)(2,1)S(1)}, bf16[8,64,1024]{2,1,0:T(8,128)(2,1)S(1)}, u32[]{:S(2)}, u32[]{:S(2)}) %collective-permute-start.16) | collective-permute-done | bytes 1048608 | tf_op jit(solution)/shard_map/ppermute | solution.py:649
  114.8 5.2 %collective-permute-done.20.got.refs_1_ = bf16[2,192,512]{2,1,0:T(8,128)(2,1)S(1)} collective-permute-done((bf16[2,192,512]{2,1,0:T(8,128)(2,1)S(1)}, bf16[2,192,512]{2,1,0:T(8,128)(2,1)S(1)}, u32[]{:S(2)}, u32[]{:S(2)}) %collective-permute-start.20) | collective-permute-done | bytes 393248 | tf_op jit(solution)/shard_map/ppermute | solution.py:649
  144.8 4.0 %collective-permute-done.31.refs_0_ = bf16[192,512]{1,0:T(8,128)(2,1)S(1)} collective-permute-done((bf16[192,512]{1,0:T(8,128)(2,1)S(1)}, bf16[192,512]{1,0:T(8,128)(2,1)S(1)}, u32[]{:S(2)}, u32[]{:S(2)}) %collective-permute-start.31) | collective-permute-done | bytes 196640 | tf_op jit(solution)/shard_map/ppermute | solution.py:649
  154.7 5.7 %collective-permute-start.28 = (bf16[192,512]{1,0:T(8,128)(2,1)S(1)}, bf16[192,512]{1,0:T(8,128)(2,1)S(1)}, u32[]{:S(2)}, u32[]{:S(2)}) collective-permute-start(bf16[192,512]{1,0:T(8,128)(2,1)S(1)} %collective-permute-done.25.refs_7_), channel_id=1, source_target_pairs={{0,1},{1,0},{2,3},{3,2},{4,5},{5,4},{6,7},{7,6},{8,9},{9,8},{10,11... | collective-permute-start | bytes 589832 | tf_op jit(solution)/shard_map/ppermute | solution.py:649
  160.6 2.7 %collective-permute-start.36 = (bf16[192,512]{1,0:T(8,128)(2,1)S(1)}, bf16[192,512]{1,0:T(8,128)(2,1)S(1)}, u32[]{:S(2)}, u32[]{:S(2)}) collective-permute-start(bf16[192,512]{1,0:T(8,128)(2,1)S(1)} %collective-permute-done.33.refs_15_), channel_id=1, source_target_pairs={{0,1},{1,0},{2,3},{3,2},{4,5},{5,4},{6,7},{7,6},{8,9},{9,8},{10,11... | collective-permute-start | bytes 589832 | tf_op jit(solution)/shard_map/ppermute | solution.py:649
  163.2 3.7 %collective-permute-done.28.refs_11_ = bf16[192,512]{1,0:T(8,128)(2,1)S(1)} collective-permute-done((bf16[192,512]{1,0:T(8,128)(2,1)S(1)}, bf16[192,512]{1,0:T(8,128)(2,1)S(1)}, u32[]{:S(2)}, u32[]{:S(2)}) %collective-permute-start.28) | collective-permute-done | bytes 196640 | tf_op jit(solution)/shard_map/ppermute | solution.py:649
  166.9 4.2 %collective-permute-done.34.refs_17_ = bf16[192,512]{1,0:T(8,128)(2,1)S(1)} collective-permute-done((bf16[192,512]{1,0:T(8,128)(2,1)S(1)}, bf16[192,512]{1,0:T(8,128)(2,1)S(1)}, u32[]{:S(2)}, u32[]{:S(2)}) %collective-permute-start.34) | collective-permute-done | bytes 196640 | tf_op jit(solution)/shard_map/ppermute | solution.py:649
  171.1 3.0 %collective-permute-done.36.refs_19_ = bf16[192,512]{1,0:T(8,128)(2,1)S(1)} collective-permute-done((bf16[192,512]{1,0:T(8,128)(2,1)S(1)}, bf16[192,512]{1,0:T(8,128)(2,1)S(1)}, u32[]{:S(2)}, u32[]{:S(2)}) %collective-permute-start.36) | collective-permute-done | bytes 196640 | tf_op jit(solution)/shard_map/ppermute | solution.py:649
  174.1 7.5 %output.1 = bf16[1024,768]{1,0:T(8,128)(2,1)} custom-call(s32[5]{0:T(128)S(1)} %copy-done.18, s32[16]{0:T(128)S(1)} %copy-done.20, s32[16]{0:T(128)S(1)} %copy-done.21, bf16[4,2,64,1024]{3,2,1,0:T(8,128)(2,1)S(1)} %bitcast.11, bf16[4,2,64,1024]{3,2,1,0:T(8,128)(2,1)S(1)} %bitcast.13, bf16[4,2,64,1024]{3,2,1,0:T(8,128)(2,1)S(1)} %bitcast.12, ...), custom_call_target="tpu_custom_call" | custom-call | tf_op jit(solution)/shard_map/output/pallas_call | solution.py:628
  (129 shorter events, 60.2 us)
Async XLA Ops:
  6.3 25.6 %collective-permute-start = (bf16[384,1024]{1,0:T(8,128)(2,1)}, bf16[384,1024]{1,0:T(8,128)(2,1)S(1)}, u32[]{:S(2)}, u32[]{:S(2)}) collective-permute-start(bf16[384,1024]{1,0:T(8,128)(2,1)} %get-tuple-element.20), channel_id=1, source_target_pairs={{0,8},{8,0},{1,9},{9,1},{2,10},{10,2},{3,11},{11,3},{4,12},{12,4},... | collective-permute-start | bytes 2359304 | tf_op jit(solution)/shard_map/ppermute | solution.py:649
  6.7 37.5 %collective-permute-start.2 = (bf16[384,1024]{1,0:T(8,128)(2,1)}, bf16[384,1024]{1,0:T(8,128)(2,1)S(1)}, u32[]{:S(2)}, u32[]{:S(2)}) collective-permute-start(bf16[384,1024]{1,0:T(8,128)(2,1)} %get-tuple-element.20), channel_id=1, source_target_pairs={{0,9},{1,8},{2,11},{3,10},{4,13},{5,12},{6,15},{7,14},{8,1},{9,0},... | collective-permute-start | bytes 2359304 | tf_op jit(solution)/shard_map/ppermute | solution.py:708
  9.4 35.2 %collective-permute-start.1 = (bf16[384,1024]{1,0:T(8,128)(2,1)}, bf16[384,1024]{1,0:T(8,128)(2,1)S(1)}, u32[]{:S(2)}, u32[]{:S(2)}) collective-permute-start(bf16[384,1024]{1,0:T(8,128)(2,1)} %get-tuple-element.22.rest_0_.refs_0_.rest_5_), channel_id=1, source_target_pairs={{0,1},{1,0},{2,3},{3,2},{4,5},{5,4},{6,7},{7,6},{8,9},{9,8},{10,11... | collective-permute-start | bytes 2359304 | tf_op jit(solution)/shard_map/ppermute | solution.py:649
  12.4 16.9 %collective-permute-start.3 = (bf16[640,256]{1,0:T(8,128)(2,1)}, bf16[640,256]{1,0:T(8,128)(2,1)S(1)}, u32[]{:S(2)}, u32[]{:S(2)}) collective-permute-start(bf16[640,256]{1,0:T(8,128)(2,1)} %get-tuple-element.23), channel_id=1, source_target_pairs={{0,2},{1,3},{2,0},{3,1},{4,6},{5,7},{6,4},{7,5},{8,10},{9,11},{10,... | collective-permute-start | bytes 983048 | tf_op jit(solution)/shard_map/ppermute | solution.py:649
  14.5 17.4 %collective-permute-start.4 = (bf16[640,256]{1,0:T(8,128)(2,1)}, bf16[640,256]{1,0:T(8,128)(2,1)}, u32[]{:S(2)}, u32[]{:S(2)}) collective-permute-start(bf16[640,256]{1,0:T(8,128)(2,1)} %get-tuple-element.24), channel_id=1, source_target_pairs={{0,4},{1,5},{2,6},{3,7},{4,0},{5,1},{6,2},{7,3},{8,12},{9,13},{10,... | collective-permute-start | bytes 983048 | tf_op jit(solution)/shard_map/ppermute | solution.py:649
  29.3 15.0 %collective-permute-start.7 = (bf16[640,256]{1,0:T(8,128)(2,1)}, bf16[640,256]{1,0:T(8,128)(2,1)}, u32[]{:S(2)}, u32[]{:S(2)}) collective-permute-start(bf16[640,256]{1,0:T(8,128)(2,1)} %get-tuple-element.28.rest_0_), channel_id=1, source_target_pairs={{0,16},{16,0},{1,17},{17,1},{2,18},{18,2},{3,19},{19,3},{4,20},{20... | collective-permute-start | bytes 983048 | tf_op jit(solution)/shard_map/ppermute | solution.py:649
  31.9 12.4 %collective-permute-start.6 = (bf16[640,256]{1,0:T(8,128)(2,1)}, bf16[640,256]{1,0:T(8,128)(2,1)S(1)}, u32[]{:S(2)}, u32[]{:S(2)}) collective-permute-start(bf16[640,256]{1,0:T(8,128)(2,1)} %get-tuple-element.28.rest_0_), channel_id=1, source_target_pairs={{0,8},{8,0},{1,9},{9,1},{2,10},{10,2},{3,11},{11,3},{4,12},{12,4},... | collective-permute-start | bytes 983048 | tf_op jit(solution)/shard_map/ppermute | solution.py:649
  31.9 12.3 %collective-permute-start.5 = (bf16[640,256]{1,0:T(8,128)(2,1)}, bf16[640,256]{1,0:T(8,128)(2,1)}, u32[]{:S(2)}, u32[]{:S(2)}) collective-permute-start(bf16[640,256]{1,0:T(8,128)(2,1)} %get-tuple-element.25), channel_id=1, source_target_pairs={{0,6},{1,7},{2,4},{3,5},{4,2},{5,3},{6,0},{7,1},{8,14},{9,15},{10,... | collective-permute-start | bytes 983048 | tf_op jit(solution)/shard_map/ppermute | solution.py:649
  49.2 23.8 %collective-permute-start.13 = (bf16[3,640,256]{2,1,0:T(8,128)(2,1)}, bf16[3,640,256]{2,1,0:T(8,128)(2,1)}, u32[]{:S(2)}, u32[]{:S(2)}) collective-permute-start(bf16[3,640,256]{2,1,0:T(8,128)(2,1)} %get-tuple-element.30.rest_4_), channel_id=1, source_target_pairs={{0,16},{16,0},{1,17},{17,1},{2,18},{18,2},{3,19},{19,3},{4,20},{20... | collective-permute-start | bytes 2949128 | tf_op jit(solution)/shard_map/ppermute | solution.py:649
  50.9 22.2 %collective-permute-start.12 = (bf16[3,640,256]{2,1,0:T(8,128)(2,1)}, bf16[3,640,256]{2,1,0:T(8,128)(2,1)}, u32[]{:S(2)}, u32[]{:S(2)}) collective-permute-start(bf16[3,640,256]{2,1,0:T(8,128)(2,1)} %get-tuple-element.30.rest_4_), channel_id=1, source_target_pairs={{0,8},{8,0},{1,9},{9,1},{2,10},{10,2},{3,11},{11,3},{4,12},{12,4},... | collective-permute-start | bytes 2949128 | tf_op jit(solution)/shard_map/ppermute | solution.py:649
  62.8 28.9 %all-to-all-start = ((bf16[8,64,1024]{2,1,0:T(8,128)(2,1)}), bf16[8,64,1024]{2,1,0:T(8,128)(2,1)S(1)}, u32[]{:S(2)}, u32[]{:S(2)}) async-start(bf16[8,64,1024]{2,1,0:T(8,128)(2,1)} %copy-done.4), calls=%async_computation | async-start | bytes 2097152 | tf_op jit(solution)/shard_map/all_to_all | solution.py:723
  91.8 23.1 %collective-permute-start.16 = (bf16[8,64,1024]{2,1,0:T(8,128)(2,1)S(1)}, bf16[8,64,1024]{2,1,0:T(8,128)(2,1)S(1)}, u32[]{:S(2)}, u32[]{:S(2)}) collective-permute-start(bf16[8,64,1024]{2,1,0:T(8,128)(2,1)S(1)} %gate.8), channel_id=1, source_target_pairs={{0,16},{16,0},{1,17},{17,1},{2,18},{18,2},{3,19},{19,3},{4,20},{20... | collective-permute-start | bytes 3145736 | tf_op jit(solution)/shard_map/ppermute | solution.py:649
  92.4 13.5 %collective-permute-start.18 = (bf16[2,192,768]{2,1,0:T(8,128)(2,1)S(1)}, bf16[2,192,768]{2,1,0:T(8,128)(2,1)S(1)}, u32[]{:S(2)}, u32[]{:S(2)}) collective-permute-start(bf16[2,192,768]{2,1,0:T(8,128)(2,1)S(1)} %get-tuple-element.32), channel_id=1, source_target_pairs={{0,2},{1,3},{2,0},{3,1},{4,6},{5,7},{6,4},{7,5},{8,10},{9,11},{10,... | collective-permute-start | bytes 1769480 | tf_op jit(solution)/shard_map/ppermute | solution.py:649
  92.4 60.3 %collective-permute-start.15 = (bf16[8,64,1024]{2,1,0:T(8,128)(2,1)S(1)}, bf16[8,64,1024]{2,1,0:T(8,128)(2,1)S(1)}, u32[]{:S(2)}, u32[]{:S(2)}) collective-permute-start(bf16[8,64,1024]{2,1,0:T(8,128)(2,1)S(1)} %gate.8), channel_id=1, source_target_pairs={{0,8},{8,0},{1,9},{9,1},{2,10},{10,2},{3,11},{11,3},{4,12},{12,4},... | collective-permute-start | bytes 3145736 | tf_op jit(solution)/shard_map/ppermute | solution.py:649
  105.9 14.1 %collective-permute-start.20 = (bf16[2,192,512]{2,1,0:T(8,128)(2,1)S(1)}, bf16[2,192,512]{2,1,0:T(8,128)(2,1)S(1)}, u32[]{:S(2)}, u32[]{:S(2)}) collective-permute-start(bf16[2,192,512]{2,1,0:T(8,128)(2,1)S(1)} %gate.9), channel_id=1, source_target_pairs={{0,2},{1,3},{2,0},{3,1},{4,6},{5,7},{6,4},{7,5},{8,10},{9,11},{10,... | collective-permute-start | bytes 1179656 | tf_op jit(solution)/shard_map/ppermute | solution.py:649
  106.0 16.6 %collective-permute-start.19 = (bf16[192,768]{1,0:T(8,128)(2,1)S(1)}, bf16[192,768]{1,0:T(8,128)(2,1)S(1)}, u32[]{:S(2)}, u32[]{:S(2)}) collective-permute-start(bf16[192,768]{1,0:T(8,128)(2,1)S(1)} %pair_sums.2), channel_id=1, source_target_pairs={{0,4},{1,5},{2,6},{3,7},{4,0},{5,1},{6,2},{7,3},{8,12},{9,13},{10,... | collective-permute-start | bytes 884744 | tf_op jit(solution)/shard_map/ppermute | solution.py:649
  114.8 59.3 %collective-permute-start.17 = (bf16[8,64,1024]{2,1,0:T(8,128)(2,1)S(1)}, bf16[8,64,1024]{2,1,0:T(8,128)(2,1)S(1)}, u32[]{:S(2)}, u32[]{:S(2)}) collective-permute-start(bf16[8,64,1024]{2,1,0:T(8,128)(2,1)S(1)} %collective-permute-done.16), channel_id=1, source_target_pairs={{0,8},{8,0},{1,9},{9,1},{2,10},{10,2},{3,11},{11,3},{4,12},{12,4},... | collective-permute-start | bytes 3145736 | tf_op jit(solution)/shard_map/ppermute | solution.py:649
  120.1 12.5 %collective-permute-start.29 = (bf16[192,512]{1,0:T(8,128)(2,1)S(1)}, bf16[192,512]{1,0:T(8,128)(2,1)S(1)}, u32[]{:S(2)}, u32[]{:S(2)}) collective-permute-start(bf16[192,512]{1,0:T(8,128)(2,1)S(1)} %pair_sums.3.refs_3_), channel_id=1, source_target_pairs={{0,4},{1,5},{2,6},{3,7},{4,0},{5,1},{6,2},{7,3},{8,12},{9,13},{10,... | collective-permute-start | bytes 589832 | tf_op jit(solution)/shard_map/ppermute | solution.py:649
  132.6 9.7 %collective-permute-start.22 = (bf16[192,512]{1,0:T(8,128)(2,1)S(1)}, bf16[192,512]{1,0:T(8,128)(2,1)S(1)}, u32[]{:S(2)}, u32[]{:S(2)}) collective-permute-start(bf16[192,512]{1,0:T(8,128)(2,1)S(1)} %attend.2.refs_4_), channel_id=1, source_target_pairs={{0,2},{1,3},{2,0},{3,1},{4,6},{5,7},{6,4},{7,5},{8,10},{9,11},{10,... | collective-permute-start | bytes 589832 | tf_op jit(solution)/shard_map/ppermute | solution.py:649
  142.5 12.2 %collective-permute-start.27 = (bf16[192,512]{1,0:T(8,128)(2,1)S(1)}, bf16[192,512]{1,0:T(8,128)(2,1)S(1)}, u32[]{:S(2)}, u32[]{:S(2)}) collective-permute-start(bf16[192,512]{1,0:T(8,128)(2,1)S(1)} %gate.10.refs_6_), channel_id=1, source_target_pairs={{0,1},{1,0},{2,3},{3,2},{4,5},{5,4},{6,7},{7,6},{8,9},{9,8},{10,11... | collective-permute-start | bytes 589832 | tf_op jit(solution)/shard_map/ppermute | solution.py:649
  154.7 12.3 %collective-permute-start.35 = (bf16[192,512]{1,0:T(8,128)(2,1)S(1)}, bf16[192,512]{1,0:T(8,128)(2,1)S(1)}, u32[]{:S(2)}, u32[]{:S(2)}) collective-permute-start(bf16[192,512]{1,0:T(8,128)(2,1)S(1)} %gate.11.refs_14_), channel_id=1, source_target_pairs={{0,1},{1,0},{2,3},{3,2},{4,5},{5,4},{6,7},{7,6},{8,9},{9,8},{10,11... | collective-permute-start | bytes 589832 | tf_op jit(solution)/shard_map/ppermute | solution.py:649
  154.7 12.2 %collective-permute-start.28 = (bf16[192,512]{1,0:T(8,128)(2,1)S(1)}, bf16[192,512]{1,0:T(8,128)(2,1)S(1)}, u32[]{:S(2)}, u32[]{:S(2)}) collective-permute-start(bf16[192,512]{1,0:T(8,128)(2,1)S(1)} %collective-permute-done.25.refs_7_), channel_id=1, source_target_pairs={{0,1},{1,0},{2,3},{3,2},{4,5},{5,4},{6,7},{7,6},{8,9},{9,8},{10,11... | collective-permute-start | bytes 589832 | tf_op jit(solution)/shard_map/ppermute | solution.py:649
  160.5 10.7 %collective-permute-start.34 = (bf16[192,512]{1,0:T(8,128)(2,1)S(1)}, bf16[192,512]{1,0:T(8,128)(2,1)S(1)}, u32[]{:S(2)}, u32[]{:S(2)}) collective-permute-start(bf16[192,512]{1,0:T(8,128)(2,1)S(1)} %collective-permute-done.30.refs_1_.refs_13_), channel_id=1, source_target_pairs={{0,1},{1,0},{2,3},{3,2},{4,5},{5,4},{6,7},{7,6},{8,9},{9,8},{10,11... | collective-permute-start | bytes 589832 | tf_op jit(solution)/shard_map/ppermute | solution.py:649
  160.6 13.6 %collective-permute-start.36 = (bf16[192,512]{1,0:T(8,128)(2,1)S(1)}, bf16[192,512]{1,0:T(8,128)(2,1)S(1)}, u32[]{:S(2)}, u32[]{:S(2)}) collective-permute-start(bf16[192,512]{1,0:T(8,128)(2,1)S(1)} %collective-permute-done.33.refs_15_), channel_id=1, source_target_pairs={{0,1},{1,0},{2,3},{3,2},{4,5},{5,4},{6,7},{7,6},{8,9},{9,8},{10,11... | collective-permute-start | bytes 589832 | tf_op jit(solution)/shard_map/ppermute | solution.py:649
  (38 other events, 439.1 us)
